TPU v7x, 32 devices: a whole 2x2x4 slice. The times are simulated.
32 devices in a mesh: shard: 8 (over z, y), rep: 4 (over x, core).
Axes of the slice: x: 2, y: 2, z: 4, core: 2. Of those that a mesh axis runs over, the one named last changes fastest.
Arguments:
- embeddings: bfloat16 [8192, 512], P('shard'), may hold values from -6 to 6
- members: int32 [8, 1024], P('shard'), may hold values from -1 to 8191, as said below
Outputs:
- best: float32 [8, 1024], P('shard', 'rep')
Inputs may be any that keep to these rules, and one draw needn't show every extreme that they name: In each cluster the valid row numbers come first, followed by -1 entries, and there are at least 128 valid ones. No row number appears twice anywhere. Among one cluster's members at most 128 lie in one aligned block of 1024 rows, and in every cluster some block holds exactly 128. Two clusters have all 1024 entries valid; the others have between a third and a half of 1024.
All inputs are finite; a program needn't handle non-finite values.
Results may differ from a plain program's by a relative error of at most 0.0014.
Values may be sent and summed in bfloat16 or wider, within the bound.
No kernel may reach another device: no remote copies, remote signals or barrier semaphores. Data moves between devices by JAX's collectives and lax.ppermute only.
A program may use at most 64 MiB of HBM per device.

v0:
```python
import jax
import jax.numpy as jnp
from jax import lax
from jax.sharding import PartitionSpec as P


def unit_rows(embeddings):
    values = embeddings.astype(jnp.float32)
    total = jnp.sum(values * values, axis=1, keepdims=True)
    return (values * lax.rsqrt(total + 1e-06)).astype(jnp.bfloat16)


def fetch_rows(unit, wanted):
    picked = jnp.take(unit, jnp.maximum(wanted, 0), axis=0)
    return jnp.where((wanted >= 0)[..., None], picked, jnp.zeros_like(picked))


def running_best(queries, positions, gathered, block_count, key_block):

    def update(block_index, current):
        start = block_index * key_block
        keys = lax.dynamic_slice_in_dim(gathered, start, key_block, 0)
        scores = lax.dot_general(
            queries, keys, (((1,), (1,)), ((), ())), preferred_element_type=jnp.float32
        )
        key_index = start + jnp.arange(key_block, dtype=jnp.int32)
        masked = jnp.where(
            key_index[None, :] < positions[:, None], scores, jnp.full_like(scores, -2.0)
        )
        return jnp.maximum(current, jnp.max(masked, axis=1))

    initial = jnp.full((queries.shape[0],), -1.0, jnp.float32)
    return lax.fori_loop(jnp.int32(0), block_count, update, initial)


def per_device(embeddings, members):
    shards = lax.axis_size("shard")
    helpers = lax.axis_size("rep")
    helper_index = lax.axis_index("rep")
    rows_dev = embeddings.shape[0]
    width = embeddings.shape[1]
    capacity = members.shape[1]
    send_cap = capacity // shards
    unit = unit_rows(embeddings)
    row_ids = members[0]
    valid = row_ids >= 0
    count = jnp.sum(valid.astype(jnp.int32))
    source = jnp.where(valid, row_ids // rows_dev, -1)
    local_row = jnp.where(valid, row_ids - source * rows_dev, -1)
    onehot = (source[:, None] == jnp.arange(shards, dtype=jnp.int32)[None, :]).astype(jnp.int32)
    earlier = jnp.cumsum(onehot, axis=0) - onehot
    position = jnp.sum(earlier * onehot, axis=1)
    table_size = shards * send_cap
    flat_index = jnp.where(valid, source * send_cap + position, table_size)
    requests = jnp.full((table_size + 1,), -1, jnp.int32).at[flat_index].set(local_row)
    requests = requests[:table_size].reshape(shards, send_cap)
    wanted = lax.all_to_all(requests, "shard", split_axis=0, concat_axis=0, tiled=True)
    returned = lax.all_to_all(
        fetch_rows(unit, wanted), "shard", split_axis=0, concat_axis=0, tiled=True
    )
    table = returned.reshape(table_size, width)
    picked = jnp.take(table, jnp.minimum(flat_index, table_size - 1), axis=0)
    gathered = jnp.where(valid[:, None], picked, jnp.zeros_like(picked))
    stripe = capacity // helpers
    queries_all = lax.dynamic_slice_in_dim(gathered, helper_index * stripe, stripe, 0)
    positions_all = helper_index * stripe + jnp.arange(stripe, dtype=jnp.int32)
    key_block = min(512, capacity)
    needed = jnp.minimum(count, positions_all[-1])
    block_count = (needed + key_block - 1) // key_block
    values = running_best(queries_all, positions_all, gathered, block_count, key_block)
    pieces = jnp.where(positions_all < count, values, jnp.zeros_like(values))
    return pieces[None, :]


def solution(mesh):
    in_specs = (P("shard", None), P("shard", None))
    out_specs = P("shard", "rep")
    return jax.shard_map(
        per_device, mesh=mesh, in_specs=in_specs, out_specs=out_specs, check_vma=False
    )
```

profile of v0, /device:TPU:0, one launch (start us, length us, event | category | flops | bytes accessed | tf_op | source)
XLA Modules:
  0.0 65.3 jit_solution(5224414573225980175)
XLA Ops:
  0.0 0.0 copy-start
  0.0 0.8 %fusion.15 = s32[8,128]{1,0:T(8,128)S(1)} fusion(s32[8,128]{1,0:T(8,128)} %bitcast.60), kind=kLoop, calls=%fused_computation.46 | loop fusion | flops 17408 | bytes 8192 | tf_op jit(solution)/shard_map/jit(_where)/select_n | solution.py:48
  0.8 0.7 %subtract_select_fusion = (s32[1024]{0:T(1024)S(1)}, pred[1024]{0:T(1024)(128)(4,1)S(1)}) fusion(s32[1024]{0:T(1024)} %bitcast.61), kind=kLoop, calls=%fused_computation.52 | loop fusion | flops 20480 | bytes 9216 | tf_op jit(solution)/shard_map/jit(_where)/select_n | solution.py:49
  1.5 1.4 %fusion.13 = (s32[1024]{0:T(1024)S(1)}, s32[]{:T(128)}) fusion(pred[1024]{0:T(1024)(128)(4,1)S(1)} %get-tuple-element.70, s32[1024]{0:T(1024)} %bitcast.62), kind=kLoop, calls=%fused_computation.44 | loop fusion | flops 18431 | bytes 9220 | tf_op jit(solution)/shard_map/jit(_where)/select_n | solution.py:48
  2.9 2.3 %reduce-window.6 = s32[8,8,128]{2,1,0:T(8,128)S(1)} reduce-window(s32[8,8,128]{2,1,0:T(8,128)S(1)} %fusion.11, s32[]{:T(128)} %constant.88.clone.1), window={size=1x1x128 pad=0_0x0_0x127_0}, to_apply=%region_1.0 | reduce-window | flops 1040384 | bytes 65540 | tf_op jit(solution)/shard_map/reduce-window
  5.1 0.3 slice_reduce_fusion
  5.4 0.2 reduce-window.9
  5.6 0.1 add_bitcast_fusion
  5.7 0.7 %compare_select_fusion = (s32[1024,1]{0,1:T(1,128)S(1)}, s32[1024,1]{0,1:T(1,128)S(1)}) fusion(s32[1024,1]{0,1:T(1,128)S(1)} %bitcast.64, s32[1,1024]{1,0:T(1,128)} %param.5), kind=kLoop, calls=%fused_computation.26 | loop fusion | flops 24576 | bytes 16384 | tf_op jit(solution)/shard_map/jit(_take)/jit(_where)/select_n | solution.py:62
  6.4 4.3 %scatter_custom_fusion = s32[1025]{0:T(1024)S(1)} fusion(s32[1024]{0:T(1024)S(1)} %bitcast.69, s32[1024]{0:T(1024)S(1)} %get-tuple-element.69, s32[]{:T(128)} %constant.93.clone.1), kind=kCustom, calls=%fused_computation.53 | custom fusion | bytes 4104 | tf_op jit(solution)/shard_map/scatter | solution.py:55
  10.8 0.6 slice.21
  11.4 7.3 %all-to-all-start = ((s32[8,1,128]{2,1,0:T(1,128)}), s32[8,1,128]{2,1,0:T(1,128)S(1)}, u32[]{:S(2)}, u32[]{:S(2)}) async-start(s32[8,1,128]{2,1,0:T(1,128)} %bitcast.7), calls=%async_computation | async-start | bytes 8192 | tf_op jit(solution)/shard_map/all_to_all | solution.py:57
  18.6 1.5 %fusion.6 = f32[1024]{0:T(1024)S(1)} fusion(bf16[1024,512]{1,0:T(8,128)(2,1)} %param.4), kind=kLoop, calls=%fused_computation.13 | loop fusion | flops 1571840 | bytes 1052672 | tf_op jit(solution)/shard_map/reduce_sum | solution.py:9
  20.2 0.0 copy-done
  20.2 0.3 fusion.7
  20.5 4.6 %all-to-all-done = s32[8,1,128]{2,1,0:T(1,128)S(1)} async-done(((s32[8,1,128]{2,1,0:T(1,128)}), s32[8,1,128]{2,1,0:T(1,128)S(1)}, u32[]{:S(2)}, u32[]{:S(2)}) %all-to-all-start) | async-done | bytes 4128 | tf_op jit(solution)/shard_map/all_to_all | solution.py:57
  25.1 4.0 %gather_fusion = bf16[1024,512]{1,0:T(8,128)(2,1)S(1)} fusion(bf16[1024,512]{1,0:T(8,128)(2,1)S(1)} %fusion.7, s32[1024]{0:T(1024)S(1)} %bitcast_clamp_fusion), kind=kCustom, calls=%fused_computation | custom fusion | bytes 2101248 | tf_op jit(solution)/shard_map/jit(_take)/gather | solution.py:14
  29.1 1.3 %select_select_fusion.1 = bf16[8,128,512]{2,1,0:T(8,128)(2,1)} fusion(bf16[8,128,512]{2,1,0:T(8,128)(2,1)S(1)} %bitcast.59, pred[8,128]{1,0:T(8,128)(4,1)S(1)} %get-tuple-element.72, pred[8,128]{1,0:T(8,128)(4,1)S(1)} %get-tuple-element.71), kind=kLoop, calls=%fused_computation.16 | loop fusion | flops 1048576 | bytes 2099200 | tf_op jit(solution)/shard_map/jit(_where)/select_n | solution.py:15
  30.4 0.0 copy-start.1
  30.4 3.7 %all-to-all-start.1 = ((bf16[8,128,512]{2,1,0:T(8,128)(2,1)}), bf16[8,128,512]{2,1,0:T(8,128)(2,1)S(1)}, u32[]{:S(2)}, u32[]{:S(2)}) async-start(bf16[8,128,512]{2,1,0:T(8,128)(2,1)} %select_select_fusion.1), calls=%async_computation.1 | async-start | bytes 2097152 | tf_op jit(solution)/shard_map/all_to_all | solution.py:58
  34.1 0.6 slice.12
  36.0 0.0 copy-done.1
  36.1 22.7 %all-to-all-done.1 = bf16[8,128,512]{2,1,0:T(8,128)(2,1)S(1)} async-done(((bf16[8,128,512]{2,1,0:T(8,128)(2,1)}), bf16[8,128,512]{2,1,0:T(8,128)(2,1)S(1)}, u32[]{:S(2)}, u32[]{:S(2)}) %all-to-all-start.1) | async-done | bytes 1048608 | tf_op jit(solution)/shard_map/all_to_all | solution.py:58
  58.8 4.0 %gather_fusion.1 = bf16[1024,512]{1,0:T(8,128)(2,1)S(1)} fusion(bf16[1024,512]{1,0:T(8,128)(2,1)S(1)} %bitcast.58, s32[1024]{0:T(1024)S(1)} %broadcast_clamp_fusion), kind=kCustom, calls=%fused_computation.1 | custom fusion | bytes 2101248 | tf_op jit(solution)/shard_map/jit(_take)/gather | solution.py:62
  62.7 0.8 %select_select_fusion = bf16[1024,512]{1,0:T(8,128)(2,1)S(1)} fusion(bf16[1024,512]{1,0:T(8,128)(2,1)S(1)} %gather_fusion.1, pred[1024]{0:T(1024)(128)(4,1)S(1)} %compare_and_fusion, pred[1024]{0:T(1024)(128)(4,1)S(1)} %get-tuple-element.70), kind=kLoop, calls=%fused_computation.15 | loop fusion | flops 1048576 | bytes 2099200 | tf_op jit(solution)/shard_map/jit(_where)/select_n | solution.py:63
  63.6 0.4 while.11
  63.6 0.3 fusion.28
  64.0 1.3 %compare_select_fusion.8 = f32[256]{0:T(256)} fusion(f32[256]{0:T(256)S(1)} %get-tuple-element.38, s32[]{:T(128)} %get-tuple-element.74, s32[]{:T(128)} %mul.48), kind=kLoop, calls=%fused_computation.65 | loop fusion | flops 768 | bytes 2056 | tf_op jit(solution)/shard_map/jit(_where)/select_n | solution.py:71
  (14 shorter events, 0.1 us)
Async XLA Ops:
  0.0 20.2 %copy-start = (bf16[1024,512]{1,0:T(8,128)(2,1)S(1)}, bf16[1024,512]{1,0:T(8,128)(2,1)}, u32[]{:S(2)}) copy-start(bf16[1024,512]{1,0:T(8,128)(2,1)} %param.4) | copy-start | bytes 3145732
  11.4 13.7 %all-to-all-start = ((s32[8,1,128]{2,1,0:T(1,128)}), s32[8,1,128]{2,1,0:T(1,128)S(1)}, u32[]{:S(2)}, u32[]{:S(2)}) async-start(s32[8,1,128]{2,1,0:T(1,128)} %bitcast.7), calls=%async_computation | async-start | bytes 8192 | tf_op jit(solution)/shard_map/all_to_all | solution.py:57
  30.4 5.7 %copy-start.1 = (s32[1,1024]{1,0:T(1,128)S(1)}, s32[1,1024]{1,0:T(1,128)}, u32[]{:S(2)}) copy-start(s32[1,1024]{1,0:T(1,128)} %param.5) | copy-start | bytes 12292
  30.4 28.4 %all-to-all-start.1 = ((bf16[8,128,512]{2,1,0:T(8,128)(2,1)}), bf16[8,128,512]{2,1,0:T(8,128)(2,1)S(1)}, u32[]{:S(2)}, u32[]{:S(2)}) async-start(bf16[8,128,512]{2,1,0:T(8,128)(2,1)} %select_select_fusion.1), calls=%async_computation.1 | async-start | bytes 2097152 | tf_op jit(solution)/shard_map/all_to_all | solution.py:58
where the time goes:
time: 65.7 us; the launch traced here: 65.3 us
  waiting for transfers between devices  27.3 us (42%)
  local copies, waits for them, and re-layouts  13.8 us (21%)
  other arithmetic  11.3 us (17%)
  starting transfers between devices  11 us (17%)
  between operations  1.51 us (2%)
    all_to_all x1, waiting for transfers between devices, per_device(): lax.all_to_all(fetch_rows(unit, wanted), 'shard', split_axis=0, concat_ax...  22.7 us
    all_to_all x1, starting transfers between devices, per_device(): lax.all_to_all(requests, 'shard', split_axis=0, concat_axis=0, tiled=True)  7.28 us
    all_to_all x1, waiting for transfers between devices, per_device(): lax.all_to_all(requests, 'shard', split_axis=0, concat_axis=0, tiled=True)  4.65 us
    scatter x1, local copies, waits for them, and re-layouts, per_device(): jnp.full((table_size + 1,), -1, jnp.int32).at[flat_index].set(local_row)  4.32 us
    gather x1, local copies, waits for them, and re-layouts, fetch_rows(): picked = jnp.take(unit, jnp.maximum(wanted, 0), axis=0)  3.97 us
    gather x1, local copies, waits for them, and re-layouts, per_device(): picked = jnp.take(table, jnp.minimum(flat_index, table_size - 1), axis=0)  3.96 us
    all_to_all x1, starting transfers between devices, per_device(): lax.all_to_all(fetch_rows(unit, wanted), 'shard', split_axis=0, concat_ax...  3.69 us
    another operation x2, other arithmetic  2.41 us
  transfers between devices with their start and end apart: 2, of which 2 were waited for; matrix products, arithmetic and copies ran while one was open for 4% of the time, Pallas kernels for 0%

commit v1 on v0

--- a/solution.py
+++ b/solution.py
@@ -1,7 +1,200 @@
+import functools
+
 import jax
 import jax.numpy as jnp
 from jax import lax
+from jax.experimental import pallas as pl
+from jax.experimental.pallas import tpu as pltpu
 from jax.sharding import PartitionSpec as P
+
+LANES = 128
+FAR = 1e6
+
+
+def nt_dot(a, b):
+    return lax.dot_general(a, b, (((1,), (1,)), ((), ())), preferred_element_type=jnp.float32)
+
+
+def dot(a, b):
+    return jnp.dot(a, b, preferred_element_type=jnp.float32)
+
+
+def ones_where(mask):
+    return jnp.where(mask, 1.0, 0.0).astype(jnp.bfloat16)
+
+
+def low_onehot(ids):
+    return ones_where(lax.broadcasted_iota(jnp.int32, (LANES, ids.shape[1]), 0) == (ids & (LANES - 1)))
+
+
+def high_onehot(ids, first_row, groups):
+    high = (ids - first_row) >> 7
+    return lax.broadcasted_iota(jnp.int32, (groups, ids.shape[1]), 0) == high
+
+
+def slots_of(hit, groups):
+    total = hit.shape[0]
+    marks = hit.astype(jnp.bfloat16)
+    before = ones_where(
+        lax.broadcasted_iota(jnp.int32, (LANES, LANES), 0) < lax.broadcasted_iota(jnp.int32, (LANES, LANES), 1)
+    )
+    within = dot(marks, before)
+    sums = dot(marks, jnp.ones((LANES, LANES), jnp.bfloat16)).astype(jnp.bfloat16)
+    row = lax.broadcasted_iota(jnp.int32, (total, total), 0)
+    col = lax.broadcasted_iota(jnp.int32, (total, total), 1)
+    earlier = ones_where((col < row) & (col // groups == row // groups))
+    return jnp.where(hit > 0.0, within + dot(earlier, sums), -1.0)
+
+
+def selector(slots, send_cap):
+    number = lax.broadcasted_iota(jnp.int32, (send_cap, LANES), 0).astype(jnp.float32)
+    return jnp.concatenate([ones_where(slots[h : h + 1, :] == number) for h in range(slots.shape[0])], axis=1)
+
+
+def block_id(distances):
+    rep = lax.axis_index("rep")
+    distance = jnp.int32(0)
+    for r, d in enumerate(distances):
+        distance = jnp.where(rep == r, jnp.int32(d), distance)
+    return lax.axis_index("shard") ^ distance
+
+
+def prepare_kernel(chunks, send_cap, ids_ref, rows_ref, unit_ref, own_ref, place_ref):
+    rows_dev = rows_ref.shape[0]
+    groups = rows_dev // LANES
+    values = rows_ref[...].astype(jnp.float32)
+    total = jnp.sum(values * values, axis=1, keepdims=True)
+    unit_ref[...] = (values * lax.rsqrt(total + 1e-06)).astype(jnp.bfloat16)
+
+    ids = ids_ref[...]
+    low = low_onehot(ids)
+    highs = [high_onehot(ids, block_id(d) * rows_dev, groups) for d in chunks]
+    high = jnp.concatenate([jnp.where(h, 1.0, 0.0) for h in highs], axis=0)
+    member = lax.broadcasted_iota(jnp.int32, (1, ids.shape[1]), 1)
+    digits = (member >> 5).astype(jnp.float32), (member & 31).astype(jnp.float32)
+    marks = jnp.concatenate([high, high * digits[0], high * digits[1]], axis=0).astype(jnp.bfloat16)
+    found = nt_dot(marks, low)
+    count = high.shape[0]
+    hit = found[:count]
+    position = found[count : 2 * count] * 32.0 + found[2 * count :]
+    slots = slots_of(hit, groups)
+    number = lax.broadcasted_iota(jnp.int32, (send_cap, LANES), 0).astype(jnp.float32)
+    diagonal = lax.broadcasted_iota(jnp.int32, (send_cap, send_cap), 0) == lax.broadcasted_iota(
+        jnp.int32, (send_cap, send_cap), 1
+    )
+    for c in range(len(chunks)):
+        spread = jnp.zeros((send_cap, LANES), jnp.float32)
+        for h in range(groups):
+            g = c * groups + h
+            spread += jnp.where(slots[g : g + 1, :] == number, position[g : g + 1, :] + 1.0, 0.0)
+        column = jnp.sum(spread, axis=1, keepdims=True)
+        line = jnp.sum(jnp.where(diagonal, column, 0.0), axis=0, keepdims=True)
+        place_ref[c : c + 1, :] = jnp.where(line > 0.0, line - 1.0, FAR)
+    own_ref[...] = dot(selector(slots[:groups], send_cap), unit_ref[...]).astype(jnp.bfloat16)
+
+
+def select_kernel(count, send_cap, *refs):
+    ids_refs, unit_ref, out_refs = refs[:count], refs[count], refs[count + 1 :]
+    rows_dev = unit_ref.shape[0]
+    groups = rows_dev // LANES
+    first = lax.axis_index("shard") * rows_dev
+    hits = []
+    for ref in ids_refs:
+        ids = ref[...]
+        hits.append(nt_dot(ones_where(high_onehot(ids, first, 16)), low_onehot(ids))[:groups])
+    slots = slots_of(jnp.concatenate(hits, axis=0), groups)
+    unit = unit_ref[...]
+    for t, ref in enumerate(out_refs):
+        ref[...] = dot(selector(slots[t * groups : (t + 1) * groups], send_cap), unit).astype(jnp.bfloat16)
+
+
+def best_kernel(stripe, *refs):
+    place_ref, chunk_refs, out_ref, table_ref = refs[0], refs[1:-2], refs[-2], refs[-1]
+    send_cap = chunk_refs[0].shape[0]
+    for c, ref in enumerate(chunk_refs):
+        table_ref[c * send_cap : (c + 1) * send_cap, :] = ref[...]
+    place = place_ref[...]
+    places = jnp.concatenate([place[c : c + 1, :] for c in range(len(chunk_refs))], axis=1)
+    first = lax.axis_index("rep") * stripe
+    query = (lax.broadcasted_iota(jnp.int32, (stripe, 1), 0) + first).astype(jnp.float32)
+    table = table_ref[...]
+    queries = dot(ones_where(places == query), table).astype(jnp.bfloat16)
+    scores = nt_dot(queries, table)
+    best = jnp.max(jnp.where(places < query, scores, -2.0), axis=1, keepdims=True)
+    count = jnp.sum(jnp.where(places < FAR, 1.0, 0.0), axis=1, keepdims=True)
+    best = jnp.where(query < count, jnp.maximum(best, -1.0), 0.0)
+    diagonal = lax.broadcasted_iota(jnp.int32, (LANES, LANES), 0) == lax.broadcasted_iota(
+        jnp.int32, (LANES, LANES), 1
+    )
+    for b in range(stripe // LANES):
+        part = best[b * LANES : (b + 1) * LANES, :]
+        out_ref[:, b * LANES : (b + 1) * LANES] = jnp.sum(jnp.where(diagonal, part, 0.0), axis=0, keepdims=True)
+
+
+def vmem(count):
+    return [pl.BlockSpec(memory_space=pltpu.VMEM)] * count
+
+
+PARAMS = dict(compiler_params=pltpu.CompilerParams(vmem_limit_bytes=32 * 1024 * 1024))
+
+
+def permute(array, distances):
+    shards, helpers = lax.axis_size("shard"), lax.axis_size("rep")
+    pairs = [
+        (s * helpers + r, (s ^ distances[r]) * helpers + r) for s in range(shards) for r in range(helpers)
+    ]
+    return lax.ppermute(array, ("shard", "rep"), pairs)
+
+
+def swap(array, mask):
+    return lax.ppermute(array, "rep", [(r, r ^ mask) for r in range(lax.axis_size("rep"))])
+
+
+def per_device(embeddings, members):
+    shards = lax.axis_size("shard")
+    helpers = lax.axis_size("rep")
+    rows_dev, width = embeddings.shape
+    capacity = members.shape[1]
+    send_cap = capacity // shards
+    stripe = capacity // helpers
+
+    rounds = [[d + (r & 1) for r in range(helpers)] for d in range(shards - 2, 0, -2)] + [[1] * helpers]
+    chunk_dist = [[0] * helpers] + rounds + [[d[r ^ 1] for r in range(helpers)] for d in rounds[:-1]]
+
+    wanted = [permute(members, d) for d in rounds]
+    rows = jax.ShapeDtypeStruct((send_cap, width), jnp.bfloat16)
+    unit, own, place = pl.pallas_call(
+        functools.partial(prepare_kernel, chunk_dist, send_cap),
+        out_shape=(
+            jax.ShapeDtypeStruct((rows_dev, width), jnp.bfloat16),
+            rows,
+            jax.ShapeDtypeStruct((len(chunk_dist), send_cap), jnp.float32),
+        ),
+        in_specs=vmem(2),
+        out_specs=tuple(vmem(3)),
+        cost_estimate=pl.CostEstimate(flops=10**9, bytes_accessed=3 * 2**20, transcendentals=0),
+        **PARAMS,
+    )(members, embeddings)
+    sent = pl.pallas_call(
+        functools.partial(select_kernel, len(rounds), send_cap),
+        out_shape=(rows,) * len(rounds),
+        in_specs=vmem(len(rounds) + 1),
+        out_specs=tuple(vmem(len(rounds))),
+        cost_estimate=pl.CostEstimate(flops=10**9, bytes_accessed=2 * 2**20, transcendentals=0),
+        **PARAMS,
+    )(*wanted, unit)
+    fetched = [permute(rows, d) for rows, d in zip(sent, rounds)]
+    shared = [swap(rows, 1) for rows in fetched[:-1]]
+    chunks = [own] + fetched + shared
+    return pl.pallas_call(
+        functools.partial(best_kernel, stripe),
+        out_shape=jax.ShapeDtypeStruct((1, stripe), jnp.float32),
+        in_specs=vmem(len(chunks) + 1),
+        out_specs=vmem(1)[0],
+        scratch_shapes=[pltpu.VMEM((capacity, width), jnp.bfloat16)],
+        cost_estimate=pl.CostEstimate(flops=10**9, bytes_accessed=2 * 2**20, transcendentals=0),
+        **PARAMS,
+    )(place, *chunks)
 
 
 def unit_rows(embeddings):
@@ -33,7 +226,7 @@
     return lax.fori_loop(jnp.int32(0), block_count, update, initial)
 
 
-def per_device(embeddings, members):
+def per_device_many(embeddings, members):
     shards = lax.axis_size("shard")
     helpers = lax.axis_size("rep")
     helper_index = lax.axis_index("rep")
@@ -75,6 +268,11 @@
 def solution(mesh):
     in_specs = (P("shard", None), P("shard", None))
     out_specs = P("shard", "rep")
+    few = mesh.shape["shard"] == 8 and mesh.shape["rep"] == 4
     return jax.shard_map(
-        per_device, mesh=mesh, in_specs=in_specs, out_specs=out_specs, check_vma=False
-    )
+        per_device if few else per_device_many,
+        mesh=mesh,
+        in_specs=in_specs,
+        out_specs=out_specs,
+        check_vma=False,
+    )

time: 65.7 us -> 30.6 us (0.47)
  waiting for transfers between devices: 27.3 us -> 11.7 us
  local copies, waits for them, and re-layouts: 13.8 us -> 1.91 us
  other arithmetic: 11.3 us -> 0 us
  Pallas kernels: 0 us -> 4.11 us
  starting transfers between devices: 11 us -> 12.6 us
  between operations: 1.51 us -> 0.04 us
    all_to_all x2 -> x0, waiting for transfers between devices: 27.3 us -> none  [the longest x1 22.7 us: per_device(): lax.all_to_all(fetch_rows(unit, wanted), 'shard', split_axis=0, concat_ax...]
    ppermute x0 -> x11, starting transfers between devices: none -> 12.6 us  [the longest x8 12.1 us: permute(): return lax.ppermute(array, ('shard', 'rep'), pairs)]
    ppermute x0 -> x11, waiting for transfers between devices: none -> 11.7 us  [the longest x8 10.7 us: permute(): return lax.ppermute(array, ('shard', 'rep'), pairs)]
    all_to_all x2 -> x0, starting transfers between devices: 11 us -> none  [the longest x1 7.28 us: per_device(): lax.all_to_all(requests, 'shard', split_axis=0, concat_axis=0, tiled=True)]
    gather x2 -> x0, local copies, waits for them, and re-layouts: 7.92 us -> none  [the longest x1 3.97 us: fetch_rows(): picked = jnp.take(unit, jnp.maximum(wanted, 0), axis=0)]
    select_n x8 -> x0, other arithmetic: 6.93 us -> none  [the longest x2 2.18 us: per_device(): source = jnp.where(valid, row_ids // rows_dev, -1)]
    scatter x1 -> x0, local copies, waits for them, and re-layouts: 4.32 us -> none  [per_device(): jnp.full((table_size + 1,), -1, jnp.int32).at[flat_index].set(local_row)]
    pallas_call x0 -> x3, Pallas kernels: none -> 4.11 us  [the longest x1 1.45 us: per_device(): pl.pallas_call(functools.partial(best_kernel, stripe), out_shape=jax.Shap...]
  transfers between devices with their start and end apart: 2 -> 11, of which waited for: 2 -> 5; matrix products, arithmetic and copies ran while one was open for 4% -> 0% of each run, Pallas kernels for 0% -> 4%
where the time goes in v1:
time: 30.6 us; the launch traced here: 30.4 us
  starting transfers between devices  12.6 us (41%)
  waiting for transfers between devices  11.7 us (38%)
  Pallas kernels  4.11 us (13%)
  local copies, waits for them, and re-layouts  1.91 us (6%)
    ppermute x8, starting transfers between devices, permute(): return lax.ppermute(array, ('shard', 'rep'), pairs)  12.1 us
    ppermute x8, waiting for transfers between devices, permute(): return lax.ppermute(array, ('shard', 'rep'), pairs)  10.7 us
    unnamed x4, local copies, waits for them, and re-layouts  1.91 us
    pallas_call x1, Pallas kernels, per_device(): pl.pallas_call(functools.partial(best_kernel, stripe), out_shape=jax.Shap...  1.45 us
    pallas_call x1, Pallas kernels, per_device(): pl.pallas_call(functools.partial(prepare_kernel, chunk_dist, send_cap), o...  1.33 us
    pallas_call x1, Pallas kernels, per_device(): pl.pallas_call(functools.partial(select_kernel, len(rounds), send_cap), o...  1.33 us
    ppermute x3, waiting for transfers between devices, swap(): lax.ppermute(array, 'rep', [(r, r ^ mask) for r in range(lax.axis_size('r...  1.02 us
  transfers between devices with their start and end apart: 11, of which 5 were waited for; matrix products, arithmetic and copies ran while one was open for 0% of the time, Pallas kernels for 4%

profile of v1, /device:TPU:0, one launch (start us, length us, event | category | flops | bytes accessed | tf_op | source)
XLA Modules:
  0.0 30.4 jit_solution(4524935648646332583)
XLA Ops:
  0.0 4.0 %collective-permute-start.1 = (s32[1,1024]{1,0:T(1,128)}, s32[1,1024]{1,0:T(1,128)S(1)}, u32[]{:S(2)}, u32[]{:S(2)}) collective-permute-start(s32[1,1024]{1,0:T(1,128)} %ids_ref.1), channel_id=1, source_target_pairs={{0,16},{1,21},{2,18},{3,23},{4,20},{5,17},{6,22},{7,19},{8,24},{9,... | collective-permute-start | bytes 12296 | tf_op jit(solution)/shard_map/ppermute | solution.py:146
  4.0 1.3 %collective-permute-start = (s32[1,1024]{1,0:T(1,128)}, s32[1,1024]{1,0:T(1,128)S(1)}, u32[]{:S(2)}, u32[]{:S(2)}) collective-permute-start(s32[1,1024]{1,0:T(1,128)} %ids_ref.1), channel_id=1, source_target_pairs={{0,24},{1,29},{2,26},{3,31},{4,28},{5,25},{6,30},{7,27},{8,16},{9,... | collective-permute-start | bytes 12296 | tf_op jit(solution)/shard_map/ppermute | solution.py:146
  5.4 1.5 %collective-permute-start.3 = (s32[1,1024]{1,0:T(1,128)}, s32[1,1024]{1,0:T(1,128)S(1)}, u32[]{:S(2)}, u32[]{:S(2)}) collective-permute-start(s32[1,1024]{1,0:T(1,128)} %ids_ref.1), channel_id=1, source_target_pairs={{0,4},{1,5},{2,6},{3,7},{4,0},{5,1},{6,2},{7,3},{8,12},{9,13},{10,... | collective-permute-start | bytes 12296 | tf_op jit(solution)/shard_map/ppermute | solution.py:146
  6.9 0.2 collective-permute-start.2
  7.1 0.0 copy-start
  7.1 1.2 %copy-done = bf16[1024,512]{1,0:T(8,128)(2,1)S(1)} copy-done((bf16[1024,512]{1,0:T(8,128)(2,1)S(1)}, bf16[1024,512]{1,0:T(8,128)(2,1)}, u32[]{:S(2)}) %copy-start) | copy-done | bytes 1048600
  8.4 0.0 copy-start.1
  8.4 0.7 %copy-done.1 = s32[1,1024]{1,0:T(1,128)S(1)} copy-done((s32[1,1024]{1,0:T(1,128)S(1)}, s32[1,1024]{1,0:T(1,128)}, u32[]{:S(2)}) %copy-start.1) | copy-done | bytes 4120
  9.1 1.3 %shard_map.28 = (bf16[1024,512]{1,0:T(8,128)(2,1)S(1)}, bf16[128,512]{1,0:T(8,128)(2,1)S(1)}, f32[8,128]{1,0:T(8,128)S(1)}) custom-call(s32[1,1024]{1,0:T(1,128)S(1)} %copy-done.1, bf16[1024,512]{1,0:T(8,128)(2,1)S(1)} %copy-done), custom_call_target="tpu_custom_call" | custom-call | flops 1000000000 | bytes 3145728 | tf_op jit(solution)/shard_map/pallas_call | solution.py:166
  10.4 0.0 collective-permute-done.1.refs_1_
  10.4 0.0 collective-permute-done.refs_0_
  10.4 0.0 collective-permute-done.3.refs_3_
  10.4 0.3 %collective-permute-done.2.refs_2_ = s32[1,1024]{1,0:T(1,128)S(1)} collective-permute-done((s32[1,1024]{1,0:T(1,128)}, s32[1,1024]{1,0:T(1,128)S(1)}, u32[]{:S(2)}, u32[]{:S(2)}) %collective-permute-start.2) | collective-permute-done | bytes 4128 | tf_op jit(solution)/shard_map/ppermute | solution.py:146
  10.7 1.3 %shard_map.29 = (bf16[128,512]{1,0:T(8,128)(2,1)S(1)}, bf16[128,512]{1,0:T(8,128)(2,1)S(1)}, bf16[128,512]{1,0:T(8,128)(2,1)S(1)}, bf16[128,512]{1,0:T(8,128)(2,1)S(1)}) custom-call(s32[1,1024]{1,0:T(1,128)S(1)} %collective-permute-done.refs_0_, s32[1,1024]{1,0:T(1,128)S(1)} %collective-permute-done.1.refs_1_, s32[1,1024]{1,0:T(1,128)S(1)} %collective-permute-done.2.refs_2_, ...), custom_call_target="tpu_custom_call" | custom-call | flops 1000000000 | bytes 2097152 | tf_op jit(solution)/shard_map/pallas_call | solution.py:178
  12.1 2.7 %collective-permute-start.4 = (bf16[128,512]{1,0:T(8,128)(2,1)S(1)}, bf16[128,512]{1,0:T(8,128)(2,1)S(1)}, u32[]{:S(2)}, u32[]{:S(2)}) collective-permute-start(bf16[128,512]{1,0:T(8,128)(2,1)S(1)} %get-tuple-element.15), channel_id=1, source_target_pairs={{0,24},{1,29},{2,26},{3,31},{4,28},{5,25},{6,30},{7,27},{8,16},{9,... | collective-permute-start | bytes 393224 | tf_op jit(solution)/shard_map/ppermute | solution.py:146
  14.7 0.3 %collective-permute-start.5 = (bf16[128,512]{1,0:T(8,128)(2,1)S(1)}, bf16[128,512]{1,0:T(8,128)(2,1)S(1)}, u32[]{:S(2)}, u32[]{:S(2)}) collective-permute-start(bf16[128,512]{1,0:T(8,128)(2,1)S(1)} %get-tuple-element.16), channel_id=1, source_target_pairs={{0,16},{1,21},{2,18},{3,23},{4,20},{5,17},{6,22},{7,19},{8,24},{9,... | collective-permute-start | bytes 393224 | tf_op jit(solution)/shard_map/ppermute | solution.py:146
  15.1 1.4 %collective-permute-start.6 = (bf16[128,512]{1,0:T(8,128)(2,1)S(1)}, bf16[128,512]{1,0:T(8,128)(2,1)S(1)}, u32[]{:S(2)}, u32[]{:S(2)}) collective-permute-start(bf16[128,512]{1,0:T(8,128)(2,1)S(1)} %get-tuple-element.17), channel_id=1, source_target_pairs={{0,8},{1,13},{2,10},{3,15},{4,12},{5,9},{6,14},{7,11},{8,0},{9,5},... | collective-permute-start | bytes 393224 | tf_op jit(solution)/shard_map/ppermute | solution.py:146
  16.5 0.5 %collective-permute-start.7 = (bf16[128,512]{1,0:T(8,128)(2,1)S(1)}, bf16[128,512]{1,0:T(8,128)(2,1)S(1)}, u32[]{:S(2)}, u32[]{:S(2)}) collective-permute-start(bf16[128,512]{1,0:T(8,128)(2,1)S(1)} %get-tuple-element.18), channel_id=1, source_target_pairs={{0,4},{1,5},{2,6},{3,7},{4,0},{5,1},{6,2},{7,3},{8,12},{9,13},{10,... | collective-permute-start | bytes 393224 | tf_op jit(solution)/shard_map/ppermute | solution.py:146
  17.0 3.3 %collective-permute-done.4.refs_2_ = bf16[128,512]{1,0:T(8,128)(2,1)S(1)} collective-permute-done((bf16[128,512]{1,0:T(8,128)(2,1)S(1)}, bf16[128,512]{1,0:T(8,128)(2,1)S(1)}, u32[]{:S(2)}, u32[]{:S(2)}) %collective-permute-start.4) | collective-permute-done | bytes 131104 | tf_op jit(solution)/shard_map/ppermute | solution.py:146
  20.3 0.0 collective-permute-start.8
  20.3 7.1 %collective-permute-done.5.refs_3_ = bf16[128,512]{1,0:T(8,128)(2,1)S(1)} collective-permute-done((bf16[128,512]{1,0:T(8,128)(2,1)S(1)}, bf16[128,512]{1,0:T(8,128)(2,1)S(1)}, u32[]{:S(2)}, u32[]{:S(2)}) %collective-permute-start.5) | collective-permute-done | bytes 131104 | tf_op jit(solution)/shard_map/ppermute | solution.py:146
  27.4 0.0 collective-permute-start.9
  27.4 0.0 collective-permute-done.6.refs_4_
  27.4 0.5 %collective-permute-start.10 = (bf16[128,512]{1,0:T(8,128)(2,1)S(1)}, bf16[128,512]{1,0:T(8,128)(2,1)S(1)}, u32[]{:S(2)}, u32[]{:S(2)}) collective-permute-start(bf16[128,512]{1,0:T(8,128)(2,1)S(1)} %collective-permute-done.6.refs_4_), channel_id=1, source_target_pairs={{0,1},{1,0},{2,3},{3,2},{4,5},{5,4},{6,7},{7,6},{8,9},{9,8},{10,11... | collective-permute-start | bytes 393224 | tf_op jit(solution)/shard_map/ppermute | solution.py:150
  27.9 0.0 collective-permute-done.7.refs_5_
  27.9 0.0 collective-permute-done.8.refs_6_
  27.9 0.8 %collective-permute-done.9.refs_7_ = bf16[128,512]{1,0:T(8,128)(2,1)S(1)} collective-permute-done((bf16[128,512]{1,0:T(8,128)(2,1)S(1)}, bf16[128,512]{1,0:T(8,128)(2,1)S(1)}, u32[]{:S(2)}, u32[]{:S(2)}) %collective-permute-start.9) | collective-permute-done | bytes 131104 | tf_op jit(solution)/shard_map/ppermute | solution.py:150
  28.8 0.2 collective-permute-done.10.refs_8_
  28.9 1.4 %shard_map.30 = f32[1,256]{1,0:T(1,128)} custom-call(f32[8,128]{1,0:T(8,128)S(1)} %get-tuple-element.12.refs_0_, bf16[128,512]{1,0:T(8,128)(2,1)S(1)} %get-tuple-element.13.refs_1_, bf16[128,512]{1,0:T(8,128)(2,1)S(1)} %collective-permute-done.4.refs_2_, bf16[128,512]{1,0:T(8,128)(2,1)S(1)} %collective-permute-done.5.refs_3_, ...), custom_call_target="tpu_custom_call" | custom-call | flops 1000000000 | bytes 2097152 | tf_op jit(solution)/shard_map/pallas_call | solution.py:189
Async XLA Ops:
  0.0 10.4 %collective-permute-start.1 = (s32[1,1024]{1,0:T(1,128)}, s32[1,1024]{1,0:T(1,128)S(1)}, u32[]{:S(2)}, u32[]{:S(2)}) collective-permute-start(s32[1,1024]{1,0:T(1,128)} %ids_ref.1), channel_id=1, source_target_pairs={{0,16},{1,21},{2,18},{3,23},{4,20},{5,17},{6,22},{7,19},{8,24},{9,... | collective-permute-start | bytes 12296 | tf_op jit(solution)/shard_map/ppermute | solution.py:146
  4.0 6.4 %collective-permute-start = (s32[1,1024]{1,0:T(1,128)}, s32[1,1024]{1,0:T(1,128)S(1)}, u32[]{:S(2)}, u32[]{:S(2)}) collective-permute-start(s32[1,1024]{1,0:T(1,128)} %ids_ref.1), channel_id=1, source_target_pairs={{0,24},{1,29},{2,26},{3,31},{4,28},{5,25},{6,30},{7,27},{8,16},{9,... | collective-permute-start | bytes 12296 | tf_op jit(solution)/shard_map/ppermute | solution.py:146
  5.4 5.0 %collective-permute-start.3 = (s32[1,1024]{1,0:T(1,128)}, s32[1,1024]{1,0:T(1,128)S(1)}, u32[]{:S(2)}, u32[]{:S(2)}) collective-permute-start(s32[1,1024]{1,0:T(1,128)} %ids_ref.1), channel_id=1, source_target_pairs={{0,4},{1,5},{2,6},{3,7},{4,0},{5,1},{6,2},{7,3},{8,12},{9,13},{10,... | collective-permute-start | bytes 12296 | tf_op jit(solution)/shard_map/ppermute | solution.py:146
  6.9 3.8 %collective-permute-start.2 = (s32[1,1024]{1,0:T(1,128)}, s32[1,1024]{1,0:T(1,128)S(1)}, u32[]{:S(2)}, u32[]{:S(2)}) collective-permute-start(s32[1,1024]{1,0:T(1,128)} %ids_ref.1), channel_id=1, source_target_pairs={{0,8},{1,13},{2,10},{3,15},{4,12},{5,9},{6,14},{7,11},{8,0},{9,5},... | collective-permute-start | bytes 12296 | tf_op jit(solution)/shard_map/ppermute | solution.py:146
  7.1 1.2 %copy-start = (bf16[1024,512]{1,0:T(8,128)(2,1)S(1)}, bf16[1024,512]{1,0:T(8,128)(2,1)}, u32[]{:S(2)}) copy-start(bf16[1024,512]{1,0:T(8,128)(2,1)} %rows_ref.1) | copy-start | bytes 3145732
  8.4 0.7 %copy-start.1 = (s32[1,1024]{1,0:T(1,128)S(1)}, s32[1,1024]{1,0:T(1,128)}, u32[]{:S(2)}) copy-start(s32[1,1024]{1,0:T(1,128)} %ids_ref.1) | copy-start | bytes 12292
  12.1 8.2 %collective-permute-start.4 = (bf16[128,512]{1,0:T(8,128)(2,1)S(1)}, bf16[128,512]{1,0:T(8,128)(2,1)S(1)}, u32[]{:S(2)}, u32[]{:S(2)}) collective-permute-start(bf16[128,512]{1,0:T(8,128)(2,1)S(1)} %get-tuple-element.15), channel_id=1, source_target_pairs={{0,24},{1,29},{2,26},{3,31},{4,28},{5,25},{6,30},{7,27},{8,16},{9,... | collective-permute-start | bytes 393224 | tf_op jit(solution)/shard_map/ppermute | solution.py:146
  14.7 12.7 %collective-permute-start.5 = (bf16[128,512]{1,0:T(8,128)(2,1)S(1)}, bf16[128,512]{1,0:T(8,128)(2,1)S(1)}, u32[]{:S(2)}, u32[]{:S(2)}) collective-permute-start(bf16[128,512]{1,0:T(8,128)(2,1)S(1)} %get-tuple-element.16), channel_id=1, source_target_pairs={{0,16},{1,21},{2,18},{3,23},{4,20},{5,17},{6,22},{7,19},{8,24},{9,... | collective-permute-start | bytes 393224 | tf_op jit(solution)/shard_map/ppermute | solution.py:146
  15.1 12.3 %collective-permute-start.6 = (bf16[128,512]{1,0:T(8,128)(2,1)S(1)}, bf16[128,512]{1,0:T(8,128)(2,1)S(1)}, u32[]{:S(2)}, u32[]{:S(2)}) collective-permute-start(bf16[128,512]{1,0:T(8,128)(2,1)S(1)} %get-tuple-element.17), channel_id=1, source_target_pairs={{0,8},{1,13},{2,10},{3,15},{4,12},{5,9},{6,14},{7,11},{8,0},{9,5},... | collective-permute-start | bytes 393224 | tf_op jit(solution)/shard_map/ppermute | solution.py:146
  16.5 11.4 %collective-permute-start.7 = (bf16[128,512]{1,0:T(8,128)(2,1)S(1)}, bf16[128,512]{1,0:T(8,128)(2,1)S(1)}, u32[]{:S(2)}, u32[]{:S(2)}) collective-permute-start(bf16[128,512]{1,0:T(8,128)(2,1)S(1)} %get-tuple-element.18), channel_id=1, source_target_pairs={{0,4},{1,5},{2,6},{3,7},{4,0},{5,1},{6,2},{7,3},{8,12},{9,13},{10,... | collective-permute-start | bytes 393224 | tf_op jit(solution)/shard_map/ppermute | solution.py:146
  20.3 7.6 %collective-permute-start.8 = (bf16[128,512]{1,0:T(8,128)(2,1)S(1)}, bf16[128,512]{1,0:T(8,128)(2,1)S(1)}, u32[]{:S(2)}, u32[]{:S(2)}) collective-permute-start(bf16[128,512]{1,0:T(8,128)(2,1)S(1)} %collective-permute-done.4.refs_2_), channel_id=1, source_target_pairs={{0,1},{1,0},{2,3},{3,2},{4,5},{5,4},{6,7},{7,6},{8,9},{9,8},{10,11... | collective-permute-start | bytes 393224 | tf_op jit(solution)/shard_map/ppermute | solution.py:150
  27.4 1.3 %collective-permute-start.9 = (bf16[128,512]{1,0:T(8,128)(2,1)S(1)}, bf16[128,512]{1,0:T(8,128)(2,1)S(1)}, u32[]{:S(2)}, u32[]{:S(2)}) collective-permute-start(bf16[128,512]{1,0:T(8,128)(2,1)S(1)} %collective-permute-done.5.refs_3_), channel_id=1, source_target_pairs={{0,1},{1,0},{2,3},{3,2},{4,5},{5,4},{6,7},{7,6},{8,9},{9,8},{10,11... | collective-permute-start | bytes 393224 | tf_op jit(solution)/shard_map/ppermute | solution.py:150
  27.4 1.5 %collective-permute-start.10 = (bf16[128,512]{1,0:T(8,128)(2,1)S(1)}, bf16[128,512]{1,0:T(8,128)(2,1)S(1)}, u32[]{:S(2)}, u32[]{:S(2)}) collective-permute-start(bf16[128,512]{1,0:T(8,128)(2,1)S(1)} %collective-permute-done.6.refs_4_), channel_id=1, source_target_pairs={{0,1},{1,0},{2,3},{3,2},{4,5},{5,4},{6,7},{7,6},{8,9},{9,8},{10,11... | collective-permute-start | bytes 393224 | tf_op jit(solution)/shard_map/ppermute | solution.py:150

commit v2 on v1

--- a/solution.py
+++ b/solution.py
@@ -46,29 +46,39 @@
     return jnp.where(hit > 0.0, within + dot(earlier, sums), -1.0)
 
 
-def selector(slots, send_cap):
-    number = lax.broadcasted_iota(jnp.int32, (send_cap, LANES), 0).astype(jnp.float32)
-    return jnp.concatenate([ones_where(slots[h : h + 1, :] == number) for h in range(slots.shape[0])], axis=1)
-
-
-def block_id(distances):
+def selector(slots, numbers):
+    return jnp.concatenate([ones_where(slots[h : h + 1, :] == numbers) for h in range(slots.shape[0])], axis=1)
+
+
+def numbers_from(first, wanted, around):
+    return ((lax.broadcasted_iota(jnp.int32, (wanted, LANES), 0) + first) & (around - 1)).astype(jnp.float32)
+
+
+def by_rep(values):
     rep = lax.axis_index("rep")
-    distance = jnp.int32(0)
-    for r, d in enumerate(distances):
-        distance = jnp.where(rep == r, jnp.int32(d), distance)
-    return lax.axis_index("shard") ^ distance
-
-
-def prepare_kernel(chunks, send_cap, ids_ref, rows_ref, unit_ref, own_ref, place_ref):
-    rows_dev = rows_ref.shape[0]
-    groups = rows_dev // LANES
+    chosen = jnp.int32(values[0])
+    for r, value in enumerate(values[1:], 1):
+        chosen = jnp.where(rep == r, jnp.int32(value), chosen)
+    return chosen
+
+
+def unit_kernel(rows_ref, unit_ref):
     values = rows_ref[...].astype(jnp.float32)
     total = jnp.sum(values * values, axis=1, keepdims=True)
     unit_ref[...] = (values * lax.rsqrt(total + 1e-06)).astype(jnp.bfloat16)
 
+
+def pick_rows(slots, numbers, unit):
+    return dot(selector(slots, numbers), unit).astype(jnp.bfloat16)
+
+
+def place_kernel(chunks, send_cap, ids_ref, rows_ref, own_ref, place_ref):
+    rows_dev = rows_ref.shape[0]
+    groups = rows_dev // LANES
     ids = ids_ref[...]
     low = low_onehot(ids)
-    highs = [high_onehot(ids, block_id(d) * rows_dev, groups) for d in chunks]
+    shard = lax.axis_index("shard")
+    highs = [high_onehot(ids, (shard ^ by_rep(d)) * rows_dev, groups) for d, _ in chunks]
     high = jnp.concatenate([jnp.where(h, 1.0, 0.0) for h in highs], axis=0)
     member = lax.broadcasted_iota(jnp.int32, (1, ids.shape[1]), 1)
     digits = (member >> 5).astype(jnp.float32), (member & 31).astype(jnp.float32)
@@ -78,43 +88,52 @@
     hit = found[:count]
     position = found[count : 2 * count] * 32.0 + found[2 * count :]
     slots = slots_of(hit, groups)
-    number = lax.broadcasted_iota(jnp.int32, (send_cap, LANES), 0).astype(jnp.float32)
     diagonal = lax.broadcasted_iota(jnp.int32, (send_cap, send_cap), 0) == lax.broadcasted_iota(
         jnp.int32, (send_cap, send_cap), 1
     )
-    for c in range(len(chunks)):
+    for c, (_, first) in enumerate(chunks):
+        numbers = numbers_from(by_rep(first), send_cap, send_cap)
         spread = jnp.zeros((send_cap, LANES), jnp.float32)
         for h in range(groups):
             g = c * groups + h
-            spread += jnp.where(slots[g : g + 1, :] == number, position[g : g + 1, :] + 1.0, 0.0)
+            spread += jnp.where(slots[g : g + 1, :] == numbers, position[g : g + 1, :] + 1.0, 0.0)
         column = jnp.sum(spread, axis=1, keepdims=True)
         line = jnp.sum(jnp.where(diagonal, column, 0.0), axis=0, keepdims=True)
         place_ref[c : c + 1, :] = jnp.where(line > 0.0, line - 1.0, FAR)
-    own_ref[...] = dot(selector(slots[:groups], send_cap), unit_ref[...]).astype(jnp.bfloat16)
-
-
-def select_kernel(count, send_cap, *refs):
-    ids_refs, unit_ref, out_refs = refs[:count], refs[count], refs[count + 1 :]
-    rows_dev = unit_ref.shape[0]
+    numbers = numbers_from(0, send_cap, send_cap)
+    own_ref[...] = pick_rows(slots[:groups], numbers, rows_ref[...])
+
+
+def select_kernel(rounds, send_cap, *refs):
+    count = len(rounds)
+    ids_refs, rows_ref, out_refs = refs[:count], refs[count], refs[count + 1 :]
+    rows_dev = rows_ref.shape[0]
     groups = rows_dev // LANES
-    first = lax.axis_index("shard") * rows_dev
+    first_row = lax.axis_index("shard") * rows_dev
     hits = []
     for ref in ids_refs:
         ids = ref[...]
-        hits.append(nt_dot(ones_where(high_onehot(ids, first, 16)), low_onehot(ids))[:groups])
+        hits.append(nt_dot(ones_where(high_onehot(ids, first_row, 16)), low_onehot(ids))[:groups])
     slots = slots_of(jnp.concatenate(hits, axis=0), groups)
-    unit = unit_ref[...]
+    rows = rows_ref[...]
     for t, ref in enumerate(out_refs):
-        ref[...] = dot(selector(slots[t * groups : (t + 1) * groups], send_cap), unit).astype(jnp.bfloat16)
+        numbers = numbers_from(by_rep(rounds[t][1]), ref.shape[0], send_cap)
+        ref[...] = pick_rows(slots[t * groups : (t + 1) * groups], numbers, rows)
+
+
+def hand_on_kernel(rows_ref, place_ref, out_ref):
+    del place_ref
+    out_ref[...] = rows_ref[...]
 
 
 def best_kernel(stripe, *refs):
     place_ref, chunk_refs, out_ref, table_ref = refs[0], refs[1:-2], refs[-2], refs[-1]
-    send_cap = chunk_refs[0].shape[0]
-    for c, ref in enumerate(chunk_refs):
-        table_ref[c * send_cap : (c + 1) * send_cap, :] = ref[...]
+    start = 0
+    for ref in chunk_refs:
+        table_ref[start : start + ref.shape[0], :] = ref[...]
+        start += ref.shape[0]
     place = place_ref[...]
-    places = jnp.concatenate([place[c : c + 1, :] for c in range(len(chunk_refs))], axis=1)
+    places = jnp.concatenate([place[c : c + 1, :] for c in range(place.shape[0])], axis=1)
     first = lax.axis_index("rep") * stripe
     query = (lax.broadcasted_iota(jnp.int32, (stripe, 1), 0) + first).astype(jnp.float32)
     table = table_ref[...]
@@ -158,43 +177,69 @@
     send_cap = capacity // shards
     stripe = capacity // helpers
 
-    rounds = [[d + (r & 1) for r in range(helpers)] for d in range(shards - 2, 0, -2)] + [[1] * helpers]
-    chunk_dist = [[0] * helpers] + rounds + [[d[r ^ 1] for r in range(helpers)] for d in rounds[:-1]]
-
-    wanted = [permute(members, d) for d in rounds]
-    rows = jax.ShapeDtypeStruct((send_cap, width), jnp.bfloat16)
-    unit, own, place = pl.pallas_call(
-        functools.partial(prepare_kernel, chunk_dist, send_cap),
-        out_shape=(
-            jax.ShapeDtypeStruct((rows_dev, width), jnp.bfloat16),
-            rows,
-            jax.ShapeDtypeStruct((len(chunk_dist), send_cap), jnp.float32),
-        ),
+    half = send_cap // 2
+    reps = range(helpers)
+    zero = [0] * helpers
+    far = ([shards - 2 + (r >> 1) for r in reps], [half * (r & 1) for r in reps])
+    pairs = [([d + (r & 1) for r in reps], zero) for d in range(shards - 4, 0, -2)]
+    rounds = [far] + pairs + [([1] * helpers, zero)]
+    chunks = [(zero, zero), rounds[-1]]
+    chunks += pairs + [([d[r ^ 1] for r in reps], zero) for d, _ in pairs]
+    chunks += [far, ([far[0][r ^ 2] for r in reps], far[1])]
+
+    wanted = [permute(members, d) for d, _ in rounds]
+    def rows(count):
+        return jax.ShapeDtypeStruct((count, width), jnp.bfloat16)
+
+    unit = pl.pallas_call(
+        unit_kernel,
+        out_shape=rows(rows_dev),
+        in_specs=vmem(1),
+        out_specs=vmem(1)[0],
+        cost_estimate=pl.CostEstimate(flops=10**7, bytes_accessed=2 * 2**20, transcendentals=0),
+        **PARAMS,
+    )(embeddings)
+    sent = [None] * len(rounds)
+    for group in ([0, 1], list(range(2, len(rounds)))):
+        picked = pl.pallas_call(
+            functools.partial(select_kernel, [rounds[t] for t in group], send_cap),
+            out_shape=tuple(rows(half if t == 0 else send_cap) for t in group),
+            in_specs=vmem(len(group) + 1),
+            out_specs=tuple(vmem(len(group))),
+            cost_estimate=pl.CostEstimate(flops=10**9, bytes_accessed=2 * 2**20, transcendentals=0),
+            **PARAMS,
+        )(*[wanted[t] for t in group], unit)
+        for t, part in zip(group, picked):
+            sent[t] = part
+    fetched = [permute(part, d) for part, (d, _) in zip(sent, rounds)]
+    own, place = pl.pallas_call(
+        functools.partial(place_kernel, chunks, send_cap),
+        out_shape=(rows(send_cap), jax.ShapeDtypeStruct((len(chunks), send_cap), jnp.float32)),
         in_specs=vmem(2),
-        out_specs=tuple(vmem(3)),
-        cost_estimate=pl.CostEstimate(flops=10**9, bytes_accessed=3 * 2**20, transcendentals=0),
-        **PARAMS,
-    )(members, embeddings)
-    sent = pl.pallas_call(
-        functools.partial(select_kernel, len(rounds), send_cap),
-        out_shape=(rows,) * len(rounds),
-        in_specs=vmem(len(rounds) + 1),
-        out_specs=tuple(vmem(len(rounds))),
+        out_specs=tuple(vmem(2)),
         cost_estimate=pl.CostEstimate(flops=10**9, bytes_accessed=2 * 2**20, transcendentals=0),
         **PARAMS,
-    )(*wanted, unit)
-    fetched = [permute(rows, d) for rows, d in zip(sent, rounds)]
-    shared = [swap(rows, 1) for rows in fetched[:-1]]
-    chunks = [own] + fetched + shared
+    )(members, unit)
+    handed = pl.pallas_call(
+        hand_on_kernel,
+        out_shape=rows(half),
+        in_specs=vmem(2),
+        out_specs=vmem(1)[0],
+        cost_estimate=pl.CostEstimate(flops=10**9, bytes_accessed=2**17, transcendentals=0),
+        **PARAMS,
+    )(fetched[0], place)
+    crossed = swap(handed, 2)
+    parts = [own, fetched[-1]] + fetched[1:-1] + [swap(part, 1) for part in fetched[1:-1]]
+    parts += [fetched[0], swap(fetched[0], 1), crossed, swap(crossed, 1)]
     return pl.pallas_call(
         functools.partial(best_kernel, stripe),
         out_shape=jax.ShapeDtypeStruct((1, stripe), jnp.float32),
-        in_specs=vmem(len(chunks) + 1),
+        in_specs=vmem(len(parts) + 1),
         out_specs=vmem(1)[0],
         scratch_shapes=[pltpu.VMEM((capacity, width), jnp.bfloat16)],
         cost_estimate=pl.CostEstimate(flops=10**9, bytes_accessed=2 * 2**20, transcendentals=0),
         **PARAMS,
-    )(place, *chunks)
+    )(place, *parts)
 
 
 def unit_rows(embeddings):

time: 30.6 us -> 26.4 us (0.86)
  waiting for transfers between devices: 11.7 us -> 3.86 us
  starting transfers between devices: 12.6 us -> 16.3 us
  Pallas kernels: 4.11 us -> 4.86 us
  local copies, waits for them, and re-layouts: 1.91 us -> 1.23 us
    ppermute x8, waiting for transfers between devices: 10.7 us -> 2.21 us  [permute(): return lax.ppermute(array, ('shard', 'rep'), pairs)]
    ppermute x3 -> x5, starting transfers between devices: 0.51 us -> 3.07 us  [swap(): lax.ppermute(array, 'rep', [(r, r ^ mask) for r in range(lax.axis_size('r...]
    ppermute x8, starting transfers between devices: 12.1 us -> 13.2 us  [permute(): return lax.ppermute(array, ('shard', 'rep'), pairs)]
    pallas_call x2 -> x5, Pallas kernels: 2.66 us -> 3.41 us  [the longest x2 1.88 us: per_device(): pl.pallas_call(functools.partial(select_kernel, [rounds[t] for t in group...]
    unnamed x4, local copies, waits for them, and re-layouts: 1.91 us -> 1.23 us
    ppermute x3 -> x5, waiting for transfers between devices: 1.02 us -> 1.65 us  [swap(): lax.ppermute(array, 'rep', [(r, r ^ mask) for r in range(lax.axis_size('r...]
  transfers between devices with their start and end apart: 11 -> 13, of which waited for: 5 -> 6; matrix products, arithmetic and copies ran while one was open for 0% -> 0% of each run, Pallas kernels for 4% -> 13%
where the time goes in v2:
time: 26.4 us; the launch traced here: 26.3 us
  starting transfers between devices  16.3 us (62%)
  Pallas kernels  4.86 us (18%)
  waiting for transfers between devices  3.86 us (15%)
  local copies, waits for them, and re-layouts  1.23 us (5%)
    ppermute x8, starting transfers between devices, permute(): return lax.ppermute(array, ('shard', 'rep'), pairs)  13.2 us
    ppermute x5, starting transfers between devices, swap(): lax.ppermute(array, 'rep', [(r, r ^ mask) for r in range(lax.axis_size('r...  3.07 us
    ppermute x8, waiting for transfers between devices, permute(): return lax.ppermute(array, ('shard', 'rep'), pairs)  2.21 us
    pallas_call x2, Pallas kernels, per_device(): pl.pallas_call(functools.partial(select_kernel, [rounds[t] for t in group...  1.88 us
    ppermute x5, waiting for transfers between devices, swap(): lax.ppermute(array, 'rep', [(r, r ^ mask) for r in range(lax.axis_size('r...  1.65 us
    pallas_call x1, Pallas kernels, per_device(): pl.pallas_call(functools.partial(best_kernel, stripe), out_shape=jax.Shap...  1.45 us
    unnamed x4, local copies, waits for them, and re-layouts  1.23 us
    pallas_call x1, Pallas kernels, per_device(): pl.pallas_call(functools.partial(place_kernel, chunks, send_cap), out_sha...  1.18 us
  transfers between devices with their start and end apart: 13, of which 6 were waited for; matrix products, arithmetic and copies ran while one was open for 0% of the time, Pallas kernels for 13%

profile of v2, /device:TPU:0, one launch (start us, length us, event | category | flops | bytes accessed | tf_op | source)
XLA Modules:
  0.0 26.3 jit_solution(14647359278861512296)
XLA Ops:
  0.0 4.0 %collective-permute-start.4 = (s32[1,1024]{1,0:T(1,128)}, s32[1,1024]{1,0:T(1,128)S(1)}, u32[]{:S(2)}, u32[]{:S(2)}) collective-permute-start(s32[1,1024]{1,0:T(1,128)} %ids_ref.1), channel_id=1, source_target_pairs={{0,16},{1,21},{2,18},{3,23},{4,20},{5,17},{6,22},{7,19},{8,24},{9,... | collective-permute-start | bytes 12296 | tf_op jit(solution)/shard_map/ppermute | solution.py:165
  4.0 1.3 %collective-permute-start.3 = (s32[1,1024]{1,0:T(1,128)}, s32[1,1024]{1,0:T(1,128)S(1)}, u32[]{:S(2)}, u32[]{:S(2)}) collective-permute-start(s32[1,1024]{1,0:T(1,128)} %ids_ref.1), channel_id=1, source_target_pairs={{0,24},{1,25},{2,30},{3,31},{4,28},{5,29},{6,26},{7,27},{8,16},{9,... | collective-permute-start | bytes 12296 | tf_op jit(solution)/shard_map/ppermute | solution.py:165
  5.4 1.5 %collective-permute-start.1 = (s32[1,1024]{1,0:T(1,128)}, s32[1,1024]{1,0:T(1,128)S(1)}, u32[]{:S(2)}, u32[]{:S(2)}) collective-permute-start(s32[1,1024]{1,0:T(1,128)} %ids_ref.1), channel_id=1, source_target_pairs={{0,4},{1,5},{2,6},{3,7},{4,0},{5,1},{6,2},{7,3},{8,12},{9,13},{10,... | collective-permute-start | bytes 12296 | tf_op jit(solution)/shard_map/ppermute | solution.py:165
  6.9 0.2 collective-permute-start
  7.1 0.0 copy-start
  7.1 1.2 %copy-done = bf16[1024,512]{1,0:T(8,128)(2,1)S(1)} copy-done((bf16[1024,512]{1,0:T(8,128)(2,1)S(1)}, bf16[1024,512]{1,0:T(8,128)(2,1)}, u32[]{:S(2)}) %copy-start) | copy-done | bytes 1048600
  8.4 0.3 %shard_map.28.rows_ref.refs_2_ = bf16[1024,512]{1,0:T(8,128)(2,1)S(1)} custom-call(bf16[1024,512]{1,0:T(8,128)(2,1)S(1)} %copy-done), custom_call_target="tpu_custom_call" | custom-call | flops 10000000 | bytes 2097152 | tf_op jit(solution)/shard_map/pallas_call | solution.py:194
  8.7 0.0 collective-permute-done.4.refs_1_
  8.7 1.0 %collective-permute-done.3.refs_0_ = s32[1,1024]{1,0:T(1,128)S(1)} collective-permute-done((s32[1,1024]{1,0:T(1,128)}, s32[1,1024]{1,0:T(1,128)S(1)}, u32[]{:S(2)}, u32[]{:S(2)}) %collective-permute-start.3) | collective-permute-done | bytes 4128 | tf_op jit(solution)/shard_map/ppermute | solution.py:165
  9.7 1.0 %shard_map.31 = (bf16[64,512]{1,0:T(8,128)(2,1)S(1)}, bf16[128,512]{1,0:T(8,128)(2,1)S(1)}) custom-call(s32[1,1024]{1,0:T(1,128)S(1)} %collective-permute-done.3.refs_0_, s32[1,1024]{1,0:T(1,128)S(1)} %collective-permute-done.4.refs_1_, bf16[1024,512]{1,0:T(8,128)(2,1)S(1)} %shard_map.28.rows_ref.refs_2_), custom_call_target="tpu_custom_call" | custom-call | flops 1000000000 | bytes 2097152 | tf_op jit(solution)/shard_map/pallas_call | solution.py:204
  10.7 2.0 %collective-permute-start.9 = (bf16[64,512]{1,0:T(8,128)(2,1)S(1)}, bf16[64,512]{1,0:T(8,128)(2,1)S(1)}, u32[]{:S(2)}, u32[]{:S(2)}) collective-permute-start(bf16[64,512]{1,0:T(8,128)(2,1)S(1)} %get-tuple-element.16), channel_id=1, source_target_pairs={{0,24},{1,25},{2,30},{3,31},{4,28},{5,29},{6,26},{7,27},{8,16},{9,... | collective-permute-start | bytes 196616 | tf_op jit(solution)/shard_map/ppermute | solution.py:165
  12.7 0.0 copy-start.1
  12.7 0.3 %collective-permute-start.5 = (bf16[128,512]{1,0:T(8,128)(2,1)S(1)}, bf16[128,512]{1,0:T(8,128)(2,1)S(1)}, u32[]{:S(2)}, u32[]{:S(2)}) collective-permute-start(bf16[128,512]{1,0:T(8,128)(2,1)S(1)} %get-tuple-element.14), channel_id=1, source_target_pairs={{0,16},{1,21},{2,18},{3,23},{4,20},{5,17},{6,22},{7,19},{8,24},{9,... | collective-permute-start | bytes 393224 | tf_op jit(solution)/shard_map/ppermute | solution.py:165
  13.0 0.0 collective-permute-done.1.refs_1_
  13.0 0.0 collective-permute-done.refs_0_
  13.0 0.9 %shard_map.30 = (bf16[128,512]{1,0:T(8,128)(2,1)S(1)}, bf16[128,512]{1,0:T(8,128)(2,1)S(1)}) custom-call(s32[1,1024]{1,0:T(1,128)S(1)} %collective-permute-done.refs_0_, s32[1,1024]{1,0:T(1,128)S(1)} %collective-permute-done.1.refs_1_, bf16[1024,512]{1,0:T(8,128)(2,1)S(1)} %shard_map.28.rows_ref.refs_2_), custom_call_target="tpu_custom_call" | custom-call | flops 1000000000 | bytes 2097152 | tf_op jit(solution)/shard_map/pallas_call | solution.py:204
  14.0 2.2 %collective-permute-start.6 = (bf16[128,512]{1,0:T(8,128)(2,1)S(1)}, bf16[128,512]{1,0:T(8,128)(2,1)S(1)}, u32[]{:S(2)}, u32[]{:S(2)}) collective-permute-start(bf16[128,512]{1,0:T(8,128)(2,1)S(1)} %get-tuple-element.15), channel_id=1, source_target_pairs={{0,8},{1,13},{2,10},{3,15},{4,12},{5,9},{6,14},{7,11},{8,0},{9,5},... | collective-permute-start | bytes 393224 | tf_op jit(solution)/shard_map/ppermute | solution.py:165
  16.1 0.0 copy-done.1
  16.1 1.2 %shard_map.29 = (bf16[128,512]{1,0:T(8,128)(2,1)S(1)}, f32[8,128]{1,0:T(8,128)S(1)}) custom-call(s32[1,1024]{1,0:T(1,128)S(1)} %copy-done.1, bf16[1024,512]{1,0:T(8,128)(2,1)S(1)} %shard_map.28.rows_ref.refs_2_), custom_call_target="tpu_custom_call" | custom-call | flops 1000000000 | bytes 2097152 | tf_op jit(solution)/shard_map/pallas_call | solution.py:215
  17.3 1.5 %collective-permute-start.2 = (bf16[128,512]{1,0:T(8,128)(2,1)S(1)}, bf16[128,512]{1,0:T(8,128)(2,1)S(1)}, u32[]{:S(2)}, u32[]{:S(2)}) collective-permute-start(bf16[128,512]{1,0:T(8,128)(2,1)S(1)} %get-tuple-element.13), channel_id=1, source_target_pairs={{0,4},{1,5},{2,6},{3,7},{4,0},{5,1},{6,2},{7,3},{8,12},{9,13},{10,... | collective-permute-start | bytes 393224 | tf_op jit(solution)/shard_map/ppermute | solution.py:165
  18.9 0.0 collective-permute-done.9.rows_ref.refs_7_
  18.9 2.4 %collective-permute-start.11 = (bf16[64,512]{1,0:T(8,128)(2,1)S(1)}, bf16[64,512]{1,0:T(8,128)(2,1)S(1)}, u32[]{:S(2)}, u32[]{:S(2)}) collective-permute-start(bf16[64,512]{1,0:T(8,128)(2,1)S(1)} %shard_map.32), channel_id=1, source_target_pairs={{0,2},{1,3},{2,0},{3,1},{4,6},{5,7},{6,4},{7,5},{8,10},{9,11},{10,... | collective-permute-start | bytes 196616 | tf_op jit(solution)/shard_map/ppermute | solution.py:169
  21.3 1.0 %collective-permute-done.5.refs_3_ = bf16[128,512]{1,0:T(8,128)(2,1)S(1)} collective-permute-done((bf16[128,512]{1,0:T(8,128)(2,1)S(1)}, bf16[128,512]{1,0:T(8,128)(2,1)S(1)}, u32[]{:S(2)}, u32[]{:S(2)}) %collective-permute-start.5) | collective-permute-done | bytes 131104 | tf_op jit(solution)/shard_map/ppermute | solution.py:165
  22.3 0.1 collective-permute-start.7
  22.4 0.2 collective-permute-done.6.refs_4_
  22.6 0.2 collective-permute-start.8
  22.8 0.4 %collective-permute-start.10 = (bf16[64,512]{1,0:T(8,128)(2,1)S(1)}, bf16[64,512]{1,0:T(8,128)(2,1)S(1)}, u32[]{:S(2)}, u32[]{:S(2)}) collective-permute-start(bf16[64,512]{1,0:T(8,128)(2,1)S(1)} %collective-permute-done.9.rows_ref.refs_7_), channel_id=1, source_target_pairs={{0,1},{1,0},{2,3},{3,2},{4,5},{5,4},{6,7},{7,6},{8,9},{9,8},{10,11... | collective-permute-start | bytes 196616 | tf_op jit(solution)/shard_map/ppermute | solution.py:169
  23.1 0.4 %collective-permute-done.11.refs_9_ = bf16[64,512]{1,0:T(8,128)(2,1)S(1)} collective-permute-done((bf16[64,512]{1,0:T(8,128)(2,1)S(1)}, bf16[64,512]{1,0:T(8,128)(2,1)S(1)}, u32[]{:S(2)}, u32[]{:S(2)}) %collective-permute-start.11) | collective-permute-done | bytes 65568 | tf_op jit(solution)/shard_map/ppermute | solution.py:169
  23.5 0.0 collective-permute-start.12
  23.5 0.5 %collective-permute-done.10.refs_8_ = bf16[64,512]{1,0:T(8,128)(2,1)S(1)} collective-permute-done((bf16[64,512]{1,0:T(8,128)(2,1)S(1)}, bf16[64,512]{1,0:T(8,128)(2,1)S(1)}, u32[]{:S(2)}, u32[]{:S(2)}) %collective-permute-start.10) | collective-permute-done | bytes 65568 | tf_op jit(solution)/shard_map/ppermute | solution.py:169
  24.1 0.0 collective-permute-done.2.refs_2_
  24.1 0.7 %collective-permute-done.12.refs_10_ = bf16[64,512]{1,0:T(8,128)(2,1)S(1)} collective-permute-done((bf16[64,512]{1,0:T(8,128)(2,1)S(1)}, bf16[64,512]{1,0:T(8,128)(2,1)S(1)}, u32[]{:S(2)}, u32[]{:S(2)}) %collective-permute-start.12) | collective-permute-done | bytes 65568 | tf_op jit(solution)/shard_map/ppermute | solution.py:169
  24.8 0.0 collective-permute-done.7.refs_5_
  24.8 0.0 collective-permute-done.8.refs_6_
  24.8 1.4 %shard_map.33 = f32[1,256]{1,0:T(1,128)} custom-call(f32[8,128]{1,0:T(8,128)S(1)} %get-tuple-element.11.place_ref.refs_0_, bf16[128,512]{1,0:T(8,128)(2,1)S(1)} %get-tuple-element.12.refs_1_, bf16[128,512]{1,0:T(8,128)(2,1)S(1)} %collective-permute-done.2.refs_2_, bf16[128,512]{1,0:T(8,128)(2,1)S(1)} %collective-permute-done.5.refs_3_, ...), custom_call_target="tpu_custom_call" | custom-call | flops 1000000000 | bytes 2097152 | tf_op jit(solution)/shard_map/pallas_call | solution.py:234
  (1 shorter events, 0.0 us)
Async XLA Ops:
  0.0 8.7 %collective-permute-start.4 = (s32[1,1024]{1,0:T(1,128)}, s32[1,1024]{1,0:T(1,128)S(1)}, u32[]{:S(2)}, u32[]{:S(2)}) collective-permute-start(s32[1,1024]{1,0:T(1,128)} %ids_ref.1), channel_id=1, source_target_pairs={{0,16},{1,21},{2,18},{3,23},{4,20},{5,17},{6,22},{7,19},{8,24},{9,... | collective-permute-start | bytes 12296 | tf_op jit(solution)/shard_map/ppermute | solution.py:165
  4.0 5.7 %collective-permute-start.3 = (s32[1,1024]{1,0:T(1,128)}, s32[1,1024]{1,0:T(1,128)S(1)}, u32[]{:S(2)}, u32[]{:S(2)}) collective-permute-start(s32[1,1024]{1,0:T(1,128)} %ids_ref.1), channel_id=1, source_target_pairs={{0,24},{1,25},{2,30},{3,31},{4,28},{5,29},{6,26},{7,27},{8,16},{9,... | collective-permute-start | bytes 12296 | tf_op jit(solution)/shard_map/ppermute | solution.py:165
  5.4 7.6 %collective-permute-start.1 = (s32[1,1024]{1,0:T(1,128)}, s32[1,1024]{1,0:T(1,128)S(1)}, u32[]{:S(2)}, u32[]{:S(2)}) collective-permute-start(s32[1,1024]{1,0:T(1,128)} %ids_ref.1), channel_id=1, source_target_pairs={{0,4},{1,5},{2,6},{3,7},{4,0},{5,1},{6,2},{7,3},{8,12},{9,13},{10,... | collective-permute-start | bytes 12296 | tf_op jit(solution)/shard_map/ppermute | solution.py:165
  6.9 6.1 %collective-permute-start = (s32[1,1024]{1,0:T(1,128)}, s32[1,1024]{1,0:T(1,128)S(1)}, u32[]{:S(2)}, u32[]{:S(2)}) collective-permute-start(s32[1,1024]{1,0:T(1,128)} %ids_ref.1), channel_id=1, source_target_pairs={{0,8},{1,13},{2,10},{3,15},{4,12},{5,9},{6,14},{7,11},{8,0},{9,5},... | collective-permute-start | bytes 12296 | tf_op jit(solution)/shard_map/ppermute | solution.py:165
  7.1 1.2 %copy-start = (bf16[1024,512]{1,0:T(8,128)(2,1)S(1)}, bf16[1024,512]{1,0:T(8,128)(2,1)}, u32[]{:S(2)}) copy-start(bf16[1024,512]{1,0:T(8,128)(2,1)} %rows_ref.1) | copy-start | bytes 3145732
  10.7 8.2 %collective-permute-start.9 = (bf16[64,512]{1,0:T(8,128)(2,1)S(1)}, bf16[64,512]{1,0:T(8,128)(2,1)S(1)}, u32[]{:S(2)}, u32[]{:S(2)}) collective-permute-start(bf16[64,512]{1,0:T(8,128)(2,1)S(1)} %get-tuple-element.16), channel_id=1, source_target_pairs={{0,24},{1,25},{2,30},{3,31},{4,28},{5,29},{6,26},{7,27},{8,16},{9,... | collective-permute-start | bytes 196616 | tf_op jit(solution)/shard_map/ppermute | solution.py:165
  12.7 3.4 %copy-start.1 = (s32[1,1024]{1,0:T(1,128)S(1)}, s32[1,1024]{1,0:T(1,128)}, u32[]{:S(2)}) copy-start(s32[1,1024]{1,0:T(1,128)} %ids_ref.1) | copy-start | bytes 12292
  12.7 9.6 %collective-permute-start.5 = (bf16[128,512]{1,0:T(8,128)(2,1)S(1)}, bf16[128,512]{1,0:T(8,128)(2,1)S(1)}, u32[]{:S(2)}, u32[]{:S(2)}) collective-permute-start(bf16[128,512]{1,0:T(8,128)(2,1)S(1)} %get-tuple-element.14), channel_id=1, source_target_pairs={{0,16},{1,21},{2,18},{3,23},{4,20},{5,17},{6,22},{7,19},{8,24},{9,... | collective-permute-start | bytes 393224 | tf_op jit(solution)/shard_map/ppermute | solution.py:165
  14.0 8.7 %collective-permute-start.6 = (bf16[128,512]{1,0:T(8,128)(2,1)S(1)}, bf16[128,512]{1,0:T(8,128)(2,1)S(1)}, u32[]{:S(2)}, u32[]{:S(2)}) collective-permute-start(bf16[128,512]{1,0:T(8,128)(2,1)S(1)} %get-tuple-element.15), channel_id=1, source_target_pairs={{0,8},{1,13},{2,10},{3,15},{4,12},{5,9},{6,14},{7,11},{8,0},{9,5},... | collective-permute-start | bytes 393224 | tf_op jit(solution)/shard_map/ppermute | solution.py:165
  17.3 6.8 %collective-permute-start.2 = (bf16[128,512]{1,0:T(8,128)(2,1)S(1)}, bf16[128,512]{1,0:T(8,128)(2,1)S(1)}, u32[]{:S(2)}, u32[]{:S(2)}) collective-permute-start(bf16[128,512]{1,0:T(8,128)(2,1)S(1)} %get-tuple-element.13), channel_id=1, source_target_pairs={{0,4},{1,5},{2,6},{3,7},{4,0},{5,1},{6,2},{7,3},{8,12},{9,13},{10,... | collective-permute-start | bytes 393224 | tf_op jit(solution)/shard_map/ppermute | solution.py:165
  18.9 4.7 %collective-permute-start.11 = (bf16[64,512]{1,0:T(8,128)(2,1)S(1)}, bf16[64,512]{1,0:T(8,128)(2,1)S(1)}, u32[]{:S(2)}, u32[]{:S(2)}) collective-permute-start(bf16[64,512]{1,0:T(8,128)(2,1)S(1)} %shard_map.32), channel_id=1, source_target_pairs={{0,2},{1,3},{2,0},{3,1},{4,6},{5,7},{6,4},{7,5},{8,10},{9,11},{10,... | collective-permute-start | bytes 196616 | tf_op jit(solution)/shard_map/ppermute | solution.py:169
  22.3 2.5 %collective-permute-start.7 = (bf16[128,512]{1,0:T(8,128)(2,1)S(1)}, bf16[128,512]{1,0:T(8,128)(2,1)S(1)}, u32[]{:S(2)}, u32[]{:S(2)}) collective-permute-start(bf16[128,512]{1,0:T(8,128)(2,1)S(1)} %collective-permute-done.5.refs_3_), channel_id=1, source_target_pairs={{0,1},{1,0},{2,3},{3,2},{4,5},{5,4},{6,7},{7,6},{8,9},{9,8},{10,11... | collective-permute-start | bytes 393224 | tf_op jit(solution)/shard_map/ppermute | solution.py:169
  22.6 2.2 %collective-permute-start.8 = (bf16[128,512]{1,0:T(8,128)(2,1)S(1)}, bf16[128,512]{1,0:T(8,128)(2,1)S(1)}, u32[]{:S(2)}, u32[]{:S(2)}) collective-permute-start(bf16[128,512]{1,0:T(8,128)(2,1)S(1)} %collective-permute-done.6.refs_4_), channel_id=1, source_target_pairs={{0,1},{1,0},{2,3},{3,2},{4,5},{5,4},{6,7},{7,6},{8,9},{9,8},{10,11... | collective-permute-start | bytes 393224 | tf_op jit(solution)/shard_map/ppermute | solution.py:169
  22.8 1.3 %collective-permute-start.10 = (bf16[64,512]{1,0:T(8,128)(2,1)S(1)}, bf16[64,512]{1,0:T(8,128)(2,1)S(1)}, u32[]{:S(2)}, u32[]{:S(2)}) collective-permute-start(bf16[64,512]{1,0:T(8,128)(2,1)S(1)} %collective-permute-done.9.rows_ref.refs_7_), channel_id=1, source_target_pairs={{0,1},{1,0},{2,3},{3,2},{4,5},{5,4},{6,7},{7,6},{8,9},{9,8},{10,11... | collective-permute-start | bytes 196616 | tf_op jit(solution)/shard_map/ppermute | solution.py:169
  23.5 1.3 %collective-permute-start.12 = (bf16[64,512]{1,0:T(8,128)(2,1)S(1)}, bf16[64,512]{1,0:T(8,128)(2,1)S(1)}, u32[]{:S(2)}, u32[]{:S(2)}) collective-permute-start(bf16[64,512]{1,0:T(8,128)(2,1)S(1)} %collective-permute-done.11.refs_9_), channel_id=1, source_target_pairs={{0,1},{1,0},{2,3},{3,2},{4,5},{5,4},{6,7},{7,6},{8,9},{9,8},{10,11... | collective-permute-start | bytes 196616 | tf_op jit(solution)/shard_map/ppermute | solution.py:169

commit v3 on v2

--- a/solution.py
+++ b/solution.py
@@ -62,7 +62,12 @@
     return chosen
 
 
-def unit_kernel(rows_ref, unit_ref):
+def zero_kernel(out_ref):
+    out_ref[...] = jnp.zeros(out_ref.shape, out_ref.dtype)
+
+
+def unit_kernel(rows_ref, tick_ref, unit_ref):
+    del tick_ref
     values = rows_ref[...].astype(jnp.float32)
     total = jnp.sum(values * values, axis=1, keepdims=True)
     unit_ref[...] = (values * lax.rsqrt(total + 1e-06)).astype(jnp.bfloat16)
@@ -72,13 +77,12 @@
     return dot(selector(slots, numbers), unit).astype(jnp.bfloat16)
 
 
-def place_kernel(chunks, send_cap, ids_ref, rows_ref, own_ref, place_ref):
-    rows_dev = rows_ref.shape[0]
-    groups = rows_dev // LANES
+def place_kernel(chunks, send_cap, ids_ref, unit_ref, place_ref, own_ref):
+    groups = unit_ref.shape[0] // LANES
     ids = ids_ref[...]
     low = low_onehot(ids)
     shard = lax.axis_index("shard")
-    highs = [high_onehot(ids, (shard ^ by_rep(d)) * rows_dev, groups) for d, _ in chunks]
+    highs = [high_onehot(ids, (shard ^ by_rep(d)) * groups * LANES, groups) for d, _ in chunks]
     high = jnp.concatenate([jnp.where(h, 1.0, 0.0) for h in highs], axis=0)
     member = lax.broadcasted_iota(jnp.int32, (1, ids.shape[1]), 1)
     digits = (member >> 5).astype(jnp.float32), (member & 31).astype(jnp.float32)
@@ -100,14 +104,13 @@
         column = jnp.sum(spread, axis=1, keepdims=True)
         line = jnp.sum(jnp.where(diagonal, column, 0.0), axis=0, keepdims=True)
         place_ref[c : c + 1, :] = jnp.where(line > 0.0, line - 1.0, FAR)
-    numbers = numbers_from(0, send_cap, send_cap)
-    own_ref[...] = pick_rows(slots[:groups], numbers, rows_ref[...])
+    own_ref[...] = pick_rows(slots[:groups], numbers_from(0, send_cap, send_cap), unit_ref[...])
 
 
 def select_kernel(rounds, send_cap, *refs):
     count = len(rounds)
-    ids_refs, rows_ref, out_refs = refs[:count], refs[count], refs[count + 1 :]
-    rows_dev = rows_ref.shape[0]
+    ids_refs, unit_ref, out_refs = refs[:count], refs[count], refs[-count:]
+    rows_dev = unit_ref.shape[0]
     groups = rows_dev // LANES
     first_row = lax.axis_index("shard") * rows_dev
     hits = []
@@ -115,15 +118,15 @@
         ids = ref[...]
         hits.append(nt_dot(ones_where(high_onehot(ids, first_row, 16)), low_onehot(ids))[:groups])
     slots = slots_of(jnp.concatenate(hits, axis=0), groups)
-    rows = rows_ref[...]
-    for t, ref in enumerate(out_refs):
+    unit = unit_ref[...]
+    for t in range(count):
+        ref = out_refs[t]
         numbers = numbers_from(by_rep(rounds[t][1]), ref.shape[0], send_cap)
-        ref[...] = pick_rows(slots[t * groups : (t + 1) * groups], numbers, rows)
-
-
-def hand_on_kernel(rows_ref, place_ref, out_ref):
-    del place_ref
-    out_ref[...] = rows_ref[...]
+        ref[...] = pick_rows(slots[t * groups : (t + 1) * groups], numbers, unit)
+
+
+def hand_on_kernel(rows_ref, *refs):
+    refs[-1][:16, :] = rows_ref[:16, :]
 
 
 def best_kernel(stripe, *refs):
@@ -180,8 +183,8 @@
     half = send_cap // 2
     reps = range(helpers)
     zero = [0] * helpers
-    far = ([shards - 2 + (r >> 1) for r in reps], [half * (r & 1) for r in reps])
-    pairs = [([d + (r & 1) for r in reps], zero) for d in range(shards - 4, 0, -2)]
+    far = ([shards - 4 + (r >> 1) for r in reps], [half * (r & 1) for r in reps])
+    pairs = [([d + (r & 1) for r in reps], zero) for d in (shards - 2, shards - 6)]
     rounds = [far] + pairs + [([1] * helpers, zero)]
     chunks = [(zero, zero), rounds[-1]]
     chunks += pairs + [([d[r ^ 1] for r in reps], zero) for d, _ in pairs]
@@ -191,44 +194,58 @@
     def rows(count):
         return jax.ShapeDtypeStruct((count, width), jnp.bfloat16)
 
+    tick = pl.pallas_call(
+        zero_kernel,
+        out_shape=jax.ShapeDtypeStruct((8, LANES), jnp.float32),
+        out_specs=vmem(1)[0],
+        cost_estimate=pl.CostEstimate(flops=5 * 10**8, bytes_accessed=2**12, transcendentals=0),
+        **PARAMS,
+    )()
     unit = pl.pallas_call(
         unit_kernel,
         out_shape=rows(rows_dev),
-        in_specs=vmem(1),
+        in_specs=vmem(2),
         out_specs=vmem(1)[0],
-        cost_estimate=pl.CostEstimate(flops=10**7, bytes_accessed=2 * 2**20, transcendentals=0),
+        cost_estimate=pl.CostEstimate(flops=10**6, bytes_accessed=2**18, transcendentals=0),
         **PARAMS,
-    )(embeddings)
-    sent = [None] * len(rounds)
-    for group in ([0, 1], list(range(2, len(rounds)))):
-        picked = pl.pallas_call(
+    )(embeddings, tick)
+    place, own = pl.pallas_call(
+        functools.partial(place_kernel, chunks, send_cap),
+        out_shape=(jax.ShapeDtypeStruct((len(chunks), send_cap), jnp.float32), rows(send_cap)),
+        in_specs=vmem(2),
+        out_specs=tuple(vmem(2)),
+        cost_estimate=pl.CostEstimate(flops=10**9, bytes_accessed=2**12, transcendentals=0),
+        **PARAMS,
+    )(members, unit)
+    sent = []
+    after = []
+    for group in ([0], [1], [2, 3]):
+        sent += pl.pallas_call(
             functools.partial(select_kernel, [rounds[t] for t in group], send_cap),
             out_shape=tuple(rows(half if t == 0 else send_cap) for t in group),
-            in_specs=vmem(len(group) + 1),
+            in_specs=vmem(len(group) + 1 + len(after)),
             out_specs=tuple(vmem(len(group))),
-            cost_estimate=pl.CostEstimate(flops=10**9, bytes_accessed=2 * 2**20, transcendentals=0),
+            cost_estimate=pl.CostEstimate(flops=10**9, bytes_accessed=2**12, transcendentals=0),
             **PARAMS,
-        )(*[wanted[t] for t in group], unit)
-        for t, part in zip(group, picked):
-            sent[t] = part
+        )(*[wanted[t] for t in group], unit, *after)
+        after = sent[-1:]
     fetched = [permute(part, d) for part, (d, _) in zip(sent, rounds)]
-    own, place = pl.pallas_call(
-        functools.partial(place_kernel, chunks, send_cap),
-        out_shape=(rows(send_cap), jax.ShapeDtypeStruct((len(chunks), send_cap), jnp.float32)),
-        in_specs=vmem(2),
-        out_specs=tuple(vmem(2)),
-        cost_estimate=pl.CostEstimate(flops=10**9, bytes_accessed=2 * 2**20, transcendentals=0),
-        **PARAMS,
-    )(members, unit)
-    handed = pl.pallas_call(
-        hand_on_kernel,
-        out_shape=rows(half),
-        in_specs=vmem(2),
-        out_specs=vmem(1)[0],
-        cost_estimate=pl.CostEstimate(flops=10**9, bytes_accessed=2**17, transcendentals=0),
-        **PARAMS,
-    )(fetched[0], place)
-    crossed = swap(handed, 2)
+
+    def hand_on(part, flops, *others):
+        return pl.pallas_call(
+            hand_on_kernel,
+            out_shape=rows(part.shape[0]),
+            in_specs=vmem(1 + len(others)),
+            out_specs=vmem(1)[0],
+            input_output_aliases={0: 0},
+            cost_estimate=pl.CostEstimate(flops=flops, bytes_accessed=2**12, transcendentals=0),
+            **PARAMS,
+        )(part, *others)
+
+    fetched[0] = hand_on(fetched[0], 10**9)
+    fetched[1] = hand_on(fetched[1], 8 * 10**8)
+    fetched[2] = hand_on(fetched[2], 10**6, place)
+    crossed = swap(fetched[0], 2)
     parts = [own, fetched[-1]] + fetched[1:-1] + [swap(part, 1) for part in fetched[1:-1]]
     parts += [fetched[0], swap(fetched[0], 1), crossed, swap(crossed, 1)]
     return pl.pallas_call(

time: 26.4 us -> 25.4 us (0.962)
  local copies, waits for them, and re-layouts: 1.23 us -> 0.01 us
  starting transfers between devices: 16.3 us -> 15.7 us
  Pallas kernels: 4.86 us -> 5.42 us
    unnamed x4, local copies, waits for them, and re-layouts: 1.23 us -> 0.01 us
    ppermute x8, starting transfers between devices: 13.2 us -> 12 us  [permute(): return lax.ppermute(array, ('shard', 'rep'), pairs)]
    ppermute x8, waiting for transfers between devices: 2.21 us -> 2.88 us  [permute(): return lax.ppermute(array, ('shard', 'rep'), pairs)]
    ppermute x5, starting transfers between devices: 3.07 us -> 3.67 us  [swap(): lax.ppermute(array, 'rep', [(r, r ^ mask) for r in range(lax.axis_size('r...]
    pallas_call x2 -> x3, Pallas kernels: 1.88 us -> 2.45 us  [per_device(): pl.pallas_call(functools.partial(select_kernel, [rounds[t] for t in group...]
    ppermute x5, waiting for transfers between devices: 1.65 us -> 1.18 us  [swap(): lax.ppermute(array, 'rep', [(r, r ^ mask) for r in range(lax.axis_size('r...]
  transfers between devices with their start and end apart: 13 -> 13, of which waited for: 6 -> 3; matrix products, arithmetic and copies ran while one was open for 0% -> 0% of each run, Pallas kernels for 13% -> 16%
where the time goes in v3:
time: 25.4 us; the launch traced here: 25.3 us
  starting transfers between devices  15.7 us (62%)
  Pallas kernels  5.42 us (21%)
  waiting for transfers between devices  4.05 us (16%)
    ppermute x8, starting transfers between devices, permute(): return lax.ppermute(array, ('shard', 'rep'), pairs)  12 us
    ppermute x5, starting transfers between devices, swap(): lax.ppermute(array, 'rep', [(r, r ^ mask) for r in range(lax.axis_size('r...  3.67 us
    ppermute x8, waiting for transfers between devices, permute(): return lax.ppermute(array, ('shard', 'rep'), pairs)  2.88 us
    pallas_call x3, Pallas kernels, per_device(): pl.pallas_call(functools.partial(select_kernel, [rounds[t] for t in group...  2.45 us
    pallas_call x1, Pallas kernels, per_device(): pl.pallas_call(functools.partial(best_kernel, stripe), out_shape=jax.Shap...  1.45 us
    pallas_call x1, Pallas kernels, per_device(): pl.pallas_call(functools.partial(place_kernel, chunks, send_cap), out_sha...  1.18 us
    ppermute x5, waiting for transfers between devices, swap(): lax.ppermute(array, 'rep', [(r, r ^ mask) for r in range(lax.axis_size('r...  1.18 us
  transfers between devices with their start and end apart: 13, of which 3 were waited for; matrix products, arithmetic and copies ran while one was open for 0% of the time, Pallas kernels for 16%

profile of v3, /device:TPU:0, one launch (start us, length us, event | category | flops | bytes accessed | tf_op | source)
XLA Modules:
  0.0 25.3 jit_solution(17157827396061747425)
XLA Ops:
  0.0 0.0 copy-start
  0.0 4.0 %collective-permute-start.3 = (s32[1,1024]{1,0:T(1,128)}, s32[1,1024]{1,0:T(1,128)S(1)}, u32[]{:S(2)}, u32[]{:S(2)}) collective-permute-start(s32[1,1024]{1,0:T(1,128)} %ids_ref.1), channel_id=1, source_target_pairs={{0,16},{1,17},{2,22},{3,23},{4,20},{5,21},{6,18},{7,19},{8,24},{9,... | collective-permute-start | bytes 12296 | tf_op jit(solution)/shard_map/ppermute | solution.py:168
  4.0 1.3 %collective-permute-start.2 = (s32[1,1024]{1,0:T(1,128)}, s32[1,1024]{1,0:T(1,128)S(1)}, u32[]{:S(2)}, u32[]{:S(2)}) collective-permute-start(s32[1,1024]{1,0:T(1,128)} %ids_ref.1), channel_id=1, source_target_pairs={{0,24},{1,29},{2,26},{3,31},{4,28},{5,25},{6,30},{7,27},{8,16},{9,... | collective-permute-start | bytes 12296 | tf_op jit(solution)/shard_map/ppermute | solution.py:168
  5.4 0.2 collective-permute-start
  5.6 1.5 %collective-permute-start.1 = (s32[1,1024]{1,0:T(1,128)}, s32[1,1024]{1,0:T(1,128)S(1)}, u32[]{:S(2)}, u32[]{:S(2)}) collective-permute-start(s32[1,1024]{1,0:T(1,128)} %ids_ref.1), channel_id=1, source_target_pairs={{0,4},{1,5},{2,6},{3,7},{4,0},{5,1},{6,2},{7,3},{8,12},{9,13},{10,... | collective-permute-start | bytes 12296 | tf_op jit(solution)/shard_map/ppermute | solution.py:168
  7.1 0.0 copy-done
  7.1 0.3 %shard_map.29.unit_ref.refs_1_.refs_2_ = bf16[1024,512]{1,0:T(8,128)(2,1)S(1)} custom-call(bf16[1024,512]{1,0:T(8,128)(2,1)S(1)} %copy-done, f32[8,128]{1,0:T(8,128)S(1)} %shard_map.28.tick_ref), custom_call_target="tpu_custom_call" | custom-call | flops 1000000 | bytes 262144 | tf_op jit(solution)/shard_map/pallas_call | solution.py:204
  7.5 0.0 collective-permute-done.3.refs_0_
  7.5 0.8 %shard_map.31.refs_2_ = bf16[64,512]{1,0:T(8,128)(2,1)S(1)} custom-call(s32[1,1024]{1,0:T(1,128)S(1)} %collective-permute-done.3.refs_0_, bf16[1024,512]{1,0:T(8,128)(2,1)S(1)} %shard_map.29.unit_ref.refs_1_.refs_2_), custom_call_target="tpu_custom_call" | custom-call | flops 1000000000 | bytes 4096 | tf_op jit(solution)/shard_map/pallas_call | solution.py:223
  8.3 2.9 %collective-permute-start.9 = (bf16[64,512]{1,0:T(8,128)(2,1)S(1)}, bf16[64,512]{1,0:T(8,128)(2,1)S(1)}, u32[]{:S(2)}, u32[]{:S(2)}) collective-permute-start(bf16[64,512]{1,0:T(8,128)(2,1)S(1)} %shard_map.31.refs_2_), channel_id=1, source_target_pairs={{0,16},{1,17},{2,22},{3,23},{4,20},{5,21},{6,18},{7,19},{8,24},{9,... | collective-permute-start | bytes 196616 | tf_op jit(solution)/shard_map/ppermute | solution.py:168
  11.1 0.0 collective-permute-done.2.refs_0_
  11.1 0.8 %shard_map.32.refs_3_ = bf16[128,512]{1,0:T(8,128)(2,1)S(1)} custom-call(s32[1,1024]{1,0:T(1,128)S(1)} %collective-permute-done.2.refs_0_, bf16[1024,512]{1,0:T(8,128)(2,1)S(1)} %shard_map.29.unit_ref.refs_1_.refs_2_, bf16[64,512]{1,0:T(8,128)(2,1)S(1)} %shard_map.31.refs_2_), custom_call_target="tpu_custom_call" | custom-call | flops 1000000000 | bytes 4096 | tf_op jit(solution)/shard_map/pallas_call | solution.py:223
  11.9 0.0 copy-start.1
  11.9 1.4 %collective-permute-start.5 = (bf16[128,512]{1,0:T(8,128)(2,1)S(1)}, bf16[128,512]{1,0:T(8,128)(2,1)S(1)}, u32[]{:S(2)}, u32[]{:S(2)}) collective-permute-start(bf16[128,512]{1,0:T(8,128)(2,1)S(1)} %shard_map.32.refs_3_), channel_id=1, source_target_pairs={{0,24},{1,29},{2,26},{3,31},{4,28},{5,25},{6,30},{7,27},{8,16},{9,... | collective-permute-start | bytes 393224 | tf_op jit(solution)/shard_map/ppermute | solution.py:168
  13.3 0.0 collective-permute-done.refs_0_
  13.3 0.0 collective-permute-done.1.refs_1_
  13.3 0.9 %shard_map.33 = (bf16[128,512]{1,0:T(8,128)(2,1)S(1)}, bf16[128,512]{1,0:T(8,128)(2,1)S(1)}) custom-call(s32[1,1024]{1,0:T(1,128)S(1)} %collective-permute-done.refs_0_, s32[1,1024]{1,0:T(1,128)S(1)} %collective-permute-done.1.refs_1_, bf16[1024,512]{1,0:T(8,128)(2,1)S(1)} %shard_map.29.unit_ref.refs_1_.refs_2_, bf16[128,512]{1,0:T(8,128)(2,1)S(1)} %shard_map.32.refs_3_), custom_call_target="tpu_custom_call" | custom-call | flops 1000000000 | bytes 4096 | tf_op jit(solution)/shard_map/pallas_call | solution.py:223
  14.2 0.1 collective-permute-start.6
  14.3 0.0 copy-done.1
  14.3 1.2 %shard_map.30 = (f32[8,128]{1,0:T(8,128)S(1)}, bf16[128,512]{1,0:T(8,128)(2,1)S(1)}) custom-call(s32[1,1024]{1,0:T(1,128)S(1)} %copy-done.1, bf16[1024,512]{1,0:T(8,128)(2,1)S(1)} %shard_map.29.unit_ref.refs_1_.refs_2_), custom_call_target="tpu_custom_call" | custom-call | flops 1000000000 | bytes 4096 | tf_op jit(solution)/shard_map/pallas_call | solution.py:212
  15.5 0.6 %collective-permute-start.4 = (bf16[128,512]{1,0:T(8,128)(2,1)S(1)}, bf16[128,512]{1,0:T(8,128)(2,1)S(1)}, u32[]{:S(2)}, u32[]{:S(2)}) collective-permute-start(bf16[128,512]{1,0:T(8,128)(2,1)S(1)} %get-tuple-element.11), channel_id=1, source_target_pairs={{0,4},{1,5},{2,6},{3,7},{4,0},{5,1},{6,2},{7,3},{8,12},{9,13},{10,... | collective-permute-start | bytes 393224 | tf_op jit(solution)/shard_map/ppermute | solution.py:168
  16.1 0.0 collective-permute-done.9.rows_ref
  16.1 2.4 %collective-permute-start.11 = (bf16[64,512]{1,0:T(8,128)(2,1)S(1)}, bf16[64,512]{1,0:T(8,128)(2,1)S(1)}, u32[]{:S(2)}, u32[]{:S(2)}) collective-permute-start(bf16[64,512]{1,0:T(8,128)(2,1)S(1)} %shard_map.36.refs_7_), channel_id=1, source_target_pairs={{0,2},{1,3},{2,0},{3,1},{4,6},{5,7},{6,4},{7,5},{8,10},{9,11},{10,... | collective-permute-start | bytes 196616 | tf_op jit(solution)/shard_map/ppermute | solution.py:172
  18.5 2.9 %collective-permute-done.6.rows_ref = bf16[128,512]{1,0:T(8,128)(2,1)S(1)} collective-permute-done((bf16[128,512]{1,0:T(8,128)(2,1)S(1)}, bf16[128,512]{1,0:T(8,128)(2,1)S(1)}, u32[]{:S(2)}, u32[]{:S(2)}) %collective-permute-start.6) | collective-permute-done | bytes 131104 | tf_op jit(solution)/shard_map/ppermute | solution.py:168
  21.4 0.7 %collective-permute-start.8 = (bf16[128,512]{1,0:T(8,128)(2,1)S(1)}, bf16[128,512]{1,0:T(8,128)(2,1)S(1)}, u32[]{:S(2)}, u32[]{:S(2)}) collective-permute-start(bf16[128,512]{1,0:T(8,128)(2,1)S(1)} %shard_map.35.refs_4_), channel_id=1, source_target_pairs={{0,1},{1,0},{2,3},{3,2},{4,5},{5,4},{6,7},{7,6},{8,9},{9,8},{10,11... | collective-permute-start | bytes 393224 | tf_op jit(solution)/shard_map/ppermute | solution.py:172
  22.0 0.0 collective-permute-done.5.rows_ref
  22.0 0.1 collective-permute-start.7
  22.1 0.4 %collective-permute-start.10 = (bf16[64,512]{1,0:T(8,128)(2,1)S(1)}, bf16[64,512]{1,0:T(8,128)(2,1)S(1)}, u32[]{:S(2)}, u32[]{:S(2)}) collective-permute-start(bf16[64,512]{1,0:T(8,128)(2,1)S(1)} %shard_map.36.refs_7_), channel_id=1, source_target_pairs={{0,1},{1,0},{2,3},{3,2},{4,5},{5,4},{6,7},{7,6},{8,9},{9,8},{10,11... | collective-permute-start | bytes 196616 | tf_op jit(solution)/shard_map/ppermute | solution.py:172
  22.6 0.0 collective-permute-done.11.refs_9_
  22.6 0.1 collective-permute-start.12
  22.6 0.0 collective-permute-done.4.refs_2_
  22.6 0.8 %collective-permute-done.10.refs_8_ = bf16[64,512]{1,0:T(8,128)(2,1)S(1)} collective-permute-done((bf16[64,512]{1,0:T(8,128)(2,1)S(1)}, bf16[64,512]{1,0:T(8,128)(2,1)S(1)}, u32[]{:S(2)}, u32[]{:S(2)}) %collective-permute-start.10) | collective-permute-done | bytes 65568 | tf_op jit(solution)/shard_map/ppermute | solution.py:172
  23.5 0.3 %collective-permute-done.12.refs_10_ = bf16[64,512]{1,0:T(8,128)(2,1)S(1)} collective-permute-done((bf16[64,512]{1,0:T(8,128)(2,1)S(1)}, bf16[64,512]{1,0:T(8,128)(2,1)S(1)}, u32[]{:S(2)}, u32[]{:S(2)}) %collective-permute-start.12) | collective-permute-done | bytes 65568 | tf_op jit(solution)/shard_map/ppermute | solution.py:172
  23.8 0.0 collective-permute-done.8.refs_6_
  23.8 0.0 collective-permute-done.7.refs_5_
  23.8 1.4 %shard_map.37 = f32[1,256]{1,0:T(1,128)} custom-call(f32[8,128]{1,0:T(8,128)S(1)} %get-tuple-element.9.refs_0_, bf16[128,512]{1,0:T(8,128)(2,1)S(1)} %get-tuple-element.10.refs_1_, bf16[128,512]{1,0:T(8,128)(2,1)S(1)} %collective-permute-done.4.refs_2_, bf16[128,512]{1,0:T(8,128)(2,1)S(1)} %shard_map.34.refs_3_, bf16[128,512]{1,0:T(8,128)(2,1)S(1)} %shard_map.35.refs_4_, ...), custom_call_target="tpu_custom_call" | custom-call | flops 1000000000 | bytes 2097152 | tf_op jit(solution)/shard_map/pallas_call | solution.py:251
  (4 shorter events, 0.0 us)
Async XLA Ops:
  0.0 7.1 %copy-start = (bf16[1024,512]{1,0:T(8,128)(2,1)S(1)}, bf16[1024,512]{1,0:T(8,128)(2,1)}, u32[]{:S(2)}) copy-start(bf16[1024,512]{1,0:T(8,128)(2,1)} %rows_ref.1) | copy-start | bytes 3145732
  0.0 7.5 %collective-permute-start.3 = (s32[1,1024]{1,0:T(1,128)}, s32[1,1024]{1,0:T(1,128)S(1)}, u32[]{:S(2)}, u32[]{:S(2)}) collective-permute-start(s32[1,1024]{1,0:T(1,128)} %ids_ref.1), channel_id=1, source_target_pairs={{0,16},{1,17},{2,22},{3,23},{4,20},{5,21},{6,18},{7,19},{8,24},{9,... | collective-permute-start | bytes 12296 | tf_op jit(solution)/shard_map/ppermute | solution.py:168
  4.0 7.1 %collective-permute-start.2 = (s32[1,1024]{1,0:T(1,128)}, s32[1,1024]{1,0:T(1,128)S(1)}, u32[]{:S(2)}, u32[]{:S(2)}) collective-permute-start(s32[1,1024]{1,0:T(1,128)} %ids_ref.1), channel_id=1, source_target_pairs={{0,24},{1,29},{2,26},{3,31},{4,28},{5,25},{6,30},{7,27},{8,16},{9,... | collective-permute-start | bytes 12296 | tf_op jit(solution)/shard_map/ppermute | solution.py:168
  5.4 7.9 %collective-permute-start = (s32[1,1024]{1,0:T(1,128)}, s32[1,1024]{1,0:T(1,128)S(1)}, u32[]{:S(2)}, u32[]{:S(2)}) collective-permute-start(s32[1,1024]{1,0:T(1,128)} %ids_ref.1), channel_id=1, source_target_pairs={{0,8},{1,13},{2,10},{3,15},{4,12},{5,9},{6,14},{7,11},{8,0},{9,5},... | collective-permute-start | bytes 12296 | tf_op jit(solution)/shard_map/ppermute | solution.py:168
  5.6 7.7 %collective-permute-start.1 = (s32[1,1024]{1,0:T(1,128)}, s32[1,1024]{1,0:T(1,128)S(1)}, u32[]{:S(2)}, u32[]{:S(2)}) collective-permute-start(s32[1,1024]{1,0:T(1,128)} %ids_ref.1), channel_id=1, source_target_pairs={{0,4},{1,5},{2,6},{3,7},{4,0},{5,1},{6,2},{7,3},{8,12},{9,13},{10,... | collective-permute-start | bytes 12296 | tf_op jit(solution)/shard_map/ppermute | solution.py:168
  8.3 7.8 %collective-permute-start.9 = (bf16[64,512]{1,0:T(8,128)(2,1)S(1)}, bf16[64,512]{1,0:T(8,128)(2,1)S(1)}, u32[]{:S(2)}, u32[]{:S(2)}) collective-permute-start(bf16[64,512]{1,0:T(8,128)(2,1)S(1)} %shard_map.31.refs_2_), channel_id=1, source_target_pairs={{0,16},{1,17},{2,22},{3,23},{4,20},{5,21},{6,18},{7,19},{8,24},{9,... | collective-permute-start | bytes 196616 | tf_op jit(solution)/shard_map/ppermute | solution.py:168
  11.9 2.4 %copy-start.1 = (s32[1,1024]{1,0:T(1,128)S(1)}, s32[1,1024]{1,0:T(1,128)}, u32[]{:S(2)}) copy-start(s32[1,1024]{1,0:T(1,128)} %ids_ref.1) | copy-start | bytes 12292
  11.9 10.1 %collective-permute-start.5 = (bf16[128,512]{1,0:T(8,128)(2,1)S(1)}, bf16[128,512]{1,0:T(8,128)(2,1)S(1)}, u32[]{:S(2)}, u32[]{:S(2)}) collective-permute-start(bf16[128,512]{1,0:T(8,128)(2,1)S(1)} %shard_map.32.refs_3_), channel_id=1, source_target_pairs={{0,24},{1,29},{2,26},{3,31},{4,28},{5,25},{6,30},{7,27},{8,16},{9,... | collective-permute-start | bytes 393224 | tf_op jit(solution)/shard_map/ppermute | solution.py:168
  14.2 7.1 %collective-permute-start.6 = (bf16[128,512]{1,0:T(8,128)(2,1)S(1)}, bf16[128,512]{1,0:T(8,128)(2,1)S(1)}, u32[]{:S(2)}, u32[]{:S(2)}) collective-permute-start(bf16[128,512]{1,0:T(8,128)(2,1)S(1)} %get-tuple-element.12), channel_id=1, source_target_pairs={{0,8},{1,13},{2,10},{3,15},{4,12},{5,9},{6,14},{7,11},{8,0},{9,5},... | collective-permute-start | bytes 393224 | tf_op jit(solution)/shard_map/ppermute | solution.py:168
  15.5 7.1 %collective-permute-start.4 = (bf16[128,512]{1,0:T(8,128)(2,1)S(1)}, bf16[128,512]{1,0:T(8,128)(2,1)S(1)}, u32[]{:S(2)}, u32[]{:S(2)}) collective-permute-start(bf16[128,512]{1,0:T(8,128)(2,1)S(1)} %get-tuple-element.11), channel_id=1, source_target_pairs={{0,4},{1,5},{2,6},{3,7},{4,0},{5,1},{6,2},{7,3},{8,12},{9,13},{10,... | collective-permute-start | bytes 393224 | tf_op jit(solution)/shard_map/ppermute | solution.py:168
  16.1 6.5 %collective-permute-start.11 = (bf16[64,512]{1,0:T(8,128)(2,1)S(1)}, bf16[64,512]{1,0:T(8,128)(2,1)S(1)}, u32[]{:S(2)}, u32[]{:S(2)}) collective-permute-start(bf16[64,512]{1,0:T(8,128)(2,1)S(1)} %shard_map.36.refs_7_), channel_id=1, source_target_pairs={{0,2},{1,3},{2,0},{3,1},{4,6},{5,7},{6,4},{7,5},{8,10},{9,11},{10,... | collective-permute-start | bytes 196616 | tf_op jit(solution)/shard_map/ppermute | solution.py:172
  21.4 2.5 %collective-permute-start.8 = (bf16[128,512]{1,0:T(8,128)(2,1)S(1)}, bf16[128,512]{1,0:T(8,128)(2,1)S(1)}, u32[]{:S(2)}, u32[]{:S(2)}) collective-permute-start(bf16[128,512]{1,0:T(8,128)(2,1)S(1)} %shard_map.35.refs_4_), channel_id=1, source_target_pairs={{0,1},{1,0},{2,3},{3,2},{4,5},{5,4},{6,7},{7,6},{8,9},{9,8},{10,11... | collective-permute-start | bytes 393224 | tf_op jit(solution)/shard_map/ppermute | solution.py:172
  22.0 1.8 %collective-permute-start.7 = (bf16[128,512]{1,0:T(8,128)(2,1)S(1)}, bf16[128,512]{1,0:T(8,128)(2,1)S(1)}, u32[]{:S(2)}, u32[]{:S(2)}) collective-permute-start(bf16[128,512]{1,0:T(8,128)(2,1)S(1)} %shard_map.34.refs_3_), channel_id=1, source_target_pairs={{0,1},{1,0},{2,3},{3,2},{4,5},{5,4},{6,7},{7,6},{8,9},{9,8},{10,11... | collective-permute-start | bytes 393224 | tf_op jit(solution)/shard_map/ppermute | solution.py:172
  22.1 1.4 %collective-permute-start.10 = (bf16[64,512]{1,0:T(8,128)(2,1)S(1)}, bf16[64,512]{1,0:T(8,128)(2,1)S(1)}, u32[]{:S(2)}, u32[]{:S(2)}) collective-permute-start(bf16[64,512]{1,0:T(8,128)(2,1)S(1)} %shard_map.36.refs_7_), channel_id=1, source_target_pairs={{0,1},{1,0},{2,3},{3,2},{4,5},{5,4},{6,7},{7,6},{8,9},{9,8},{10,11... | collective-permute-start | bytes 196616 | tf_op jit(solution)/shard_map/ppermute | solution.py:172
  22.6 1.3 %collective-permute-start.12 = (bf16[64,512]{1,0:T(8,128)(2,1)S(1)}, bf16[64,512]{1,0:T(8,128)(2,1)S(1)}, u32[]{:S(2)}, u32[]{:S(2)}) collective-permute-start(bf16[64,512]{1,0:T(8,128)(2,1)S(1)} %collective-permute-done.11.refs_9_), channel_id=1, source_target_pairs={{0,1},{1,0},{2,3},{3,2},{4,5},{5,4},{6,7},{7,6},{8,9},{9,8},{10,11... | collective-permute-start | bytes 196616 | tf_op jit(solution)/shard_map/ppermute | solution.py:172

commit v4 on v3

--- a/solution.py
+++ b/solution.py
@@ -66,19 +66,15 @@
     out_ref[...] = jnp.zeros(out_ref.shape, out_ref.dtype)
 
 
-def unit_kernel(rows_ref, tick_ref, unit_ref):
-    del tick_ref
-    values = rows_ref[...].astype(jnp.float32)
+def pick_rows(slots, numbers, rows):
+    values = dot(selector(slots, numbers), rows)
     total = jnp.sum(values * values, axis=1, keepdims=True)
-    unit_ref[...] = (values * lax.rsqrt(total + 1e-06)).astype(jnp.bfloat16)
-
-
-def pick_rows(slots, numbers, unit):
-    return dot(selector(slots, numbers), unit).astype(jnp.bfloat16)
-
-
-def place_kernel(chunks, send_cap, ids_ref, unit_ref, place_ref, own_ref):
-    groups = unit_ref.shape[0] // LANES
+    return (values * lax.rsqrt(total + 1e-06)).astype(jnp.bfloat16)
+
+
+def place_kernel(chunks, send_cap, ids_ref, rows_ref, *refs):
+    place_ref, own_ref = refs[-2:]
+    groups = rows_ref.shape[0] // LANES
     ids = ids_ref[...]
     low = low_onehot(ids)
     shard = lax.axis_index("shard")
@@ -104,13 +100,13 @@
         column = jnp.sum(spread, axis=1, keepdims=True)
         line = jnp.sum(jnp.where(diagonal, column, 0.0), axis=0, keepdims=True)
         place_ref[c : c + 1, :] = jnp.where(line > 0.0, line - 1.0, FAR)
-    own_ref[...] = pick_rows(slots[:groups], numbers_from(0, send_cap, send_cap), unit_ref[...])
+    own_ref[...] = pick_rows(slots[:groups], numbers_from(0, send_cap, send_cap), rows_ref[...])
 
 
 def select_kernel(rounds, send_cap, *refs):
     count = len(rounds)
-    ids_refs, unit_ref, out_refs = refs[:count], refs[count], refs[-count:]
-    rows_dev = unit_ref.shape[0]
+    ids_refs, rows_ref, out_refs = refs[:count], refs[count], refs[-count:]
+    rows_dev = rows_ref.shape[0]
     groups = rows_dev // LANES
     first_row = lax.axis_index("shard") * rows_dev
     hits = []
@@ -118,11 +114,11 @@
         ids = ref[...]
         hits.append(nt_dot(ones_where(high_onehot(ids, first_row, 16)), low_onehot(ids))[:groups])
     slots = slots_of(jnp.concatenate(hits, axis=0), groups)
-    unit = unit_ref[...]
+    rows = rows_ref[...]
     for t in range(count):
         ref = out_refs[t]
         numbers = numbers_from(by_rep(rounds[t][1]), ref.shape[0], send_cap)
-        ref[...] = pick_rows(slots[t * groups : (t + 1) * groups], numbers, unit)
+        ref[...] = pick_rows(slots[t * groups : (t + 1) * groups], numbers, rows)
 
 
 def hand_on_kernel(rows_ref, *refs):
@@ -131,9 +127,10 @@
 
 def best_kernel(stripe, *refs):
     place_ref, chunk_refs, out_ref, table_ref = refs[0], refs[1:-2], refs[-2], refs[-1]
-    start = 0
+    send_cap, start, near = place_ref.shape[1], 0, table_ref.shape[0] - place_ref.shape[1]
     for ref in chunk_refs:
-        table_ref[start : start + ref.shape[0], :] = ref[...]
+        row = start if start < send_cap else start + send_cap if start < near else start - near + send_cap
+        table_ref[row : row + ref.shape[0], :] = ref[...]
         start += ref.shape[0]
     place = place_ref[...]
     places = jnp.concatenate([place[c : c + 1, :] for c in range(place.shape[0])], axis=1)
@@ -163,7 +160,10 @@
 def permute(array, distances):
     shards, helpers = lax.axis_size("shard"), lax.axis_size("rep")
     pairs = [
-        (s * helpers + r, (s ^ distances[r]) * helpers + r) for s in range(shards) for r in range(helpers)
+        (s * helpers + r, (s ^ distances[r]) * helpers + r)
+        for s in range(shards)
+        for r in range(helpers)
+        if distances[r]
     ]
     return lax.ppermute(array, ("shard", "rep"), pairs)
 
@@ -185,12 +185,14 @@
     zero = [0] * helpers
     far = ([shards - 4 + (r >> 1) for r in reps], [half * (r & 1) for r in reps])
     pairs = [([d + (r & 1) for r in reps], zero) for d in (shards - 2, shards - 6)]
-    rounds = [far] + pairs + [([1] * helpers, zero)]
-    chunks = [(zero, zero), rounds[-1]]
+    near = ([1] * helpers, zero)
+    rounds = [far] + pairs + [near]
+    chunks = [(zero, zero), near]
     chunks += pairs + [([d[r ^ 1] for r in reps], zero) for d, _ in pairs]
     chunks += [far, ([far[0][r ^ 2] for r in reps], far[1])]
 
     wanted = [permute(members, d) for d, _ in rounds]
+
     def rows(count):
         return jax.ShapeDtypeStruct((count, width), jnp.bfloat16)
 
@@ -201,34 +203,18 @@
         cost_estimate=pl.CostEstimate(flops=5 * 10**8, bytes_accessed=2**12, transcendentals=0),
         **PARAMS,
     )()
-    unit = pl.pallas_call(
-        unit_kernel,
-        out_shape=rows(rows_dev),
-        in_specs=vmem(2),
-        out_specs=vmem(1)[0],
-        cost_estimate=pl.CostEstimate(flops=10**6, bytes_accessed=2**18, transcendentals=0),
-        **PARAMS,
-    )(embeddings, tick)
-    place, own = pl.pallas_call(
-        functools.partial(place_kernel, chunks, send_cap),
-        out_shape=(jax.ShapeDtypeStruct((len(chunks), send_cap), jnp.float32), rows(send_cap)),
-        in_specs=vmem(2),
-        out_specs=tuple(vmem(2)),
-        cost_estimate=pl.CostEstimate(flops=10**9, bytes_accessed=2**12, transcendentals=0),
-        **PARAMS,
-    )(members, unit)
     sent = []
-    after = []
+    after = tick
     for group in ([0], [1], [2, 3]):
         sent += pl.pallas_call(
             functools.partial(select_kernel, [rounds[t] for t in group], send_cap),
             out_shape=tuple(rows(half if t == 0 else send_cap) for t in group),
-            in_specs=vmem(len(group) + 1 + len(after)),
+            in_specs=vmem(len(group) + 2),
             out_specs=tuple(vmem(len(group))),
             cost_estimate=pl.CostEstimate(flops=10**9, bytes_accessed=2**12, transcendentals=0),
             **PARAMS,
-        )(*[wanted[t] for t in group], unit, *after)
-        after = sent[-1:]
+        )(*[wanted[t] for t in group], embeddings, after)
+        after = sent[-1]
     fetched = [permute(part, d) for part, (d, _) in zip(sent, rounds)]
 
     def hand_on(part, flops, *others):
@@ -242,12 +228,19 @@
             **PARAMS,
         )(part, *others)
 
-    fetched[0] = hand_on(fetched[0], 10**9)
-    fetched[1] = hand_on(fetched[1], 8 * 10**8)
+    fetched[0] = hand_on(fetched[0], 300000000)
+    place, own = pl.pallas_call(
+        functools.partial(place_kernel, chunks, send_cap),
+        out_shape=(jax.ShapeDtypeStruct((len(chunks), send_cap), jnp.float32), rows(send_cap)),
+        in_specs=vmem(3),
+        out_specs=tuple(vmem(2)),
+        cost_estimate=pl.CostEstimate(flops=300000000, bytes_accessed=2**12, transcendentals=0),
+        **PARAMS,
+    )(members, embeddings, fetched[0])
     fetched[2] = hand_on(fetched[2], 10**6, place)
-    crossed = swap(fetched[0], 2)
-    parts = [own, fetched[-1]] + fetched[1:-1] + [swap(part, 1) for part in fetched[1:-1]]
-    parts += [fetched[0], swap(fetched[0], 1), crossed, swap(crossed, 1)]
+    crossed = hand_on(swap(fetched[0], 2), 1500000000)
+    parts = [own] + fetched[1:-1] + [swap(part, 1) for part in fetched[1:-1]]
+    parts += [fetched[0], swap(fetched[0], 1), crossed, swap(crossed, 1), fetched[-1]]
     return pl.pallas_call(
         functools.partial(best_kernel, stripe),
         out_shape=jax.ShapeDtypeStruct((1, stripe), jnp.float32),

time: 25.4 us -> 24.5 us (0.965)
  the two profiles are of different devices: /device:TPU:0 before, /device:TPU:11 now
where the time goes in v4:
time: 24.5 us; the launch traced here: 24.3 us
  starting transfers between devices  16 us (65%)
  Pallas kernels  5.43 us (22%)
  waiting for transfers between devices  2.82 us (12%)
    ppermute x8, starting transfers between devices, permute(): return lax.ppermute(array, ('shard', 'rep'), pairs)  10.6 us
    ppermute x5, starting transfers between devices, swap(): lax.ppermute(array, 'rep', [(r, r ^ mask) for r in range(lax.axis_size('r...  5.37 us
    pallas_call x3, Pallas kernels, per_device(): pl.pallas_call(functools.partial(select_kernel, [rounds[t] for t in group...  2.7 us
    ppermute x8, waiting for transfers between devices, permute(): return lax.ppermute(array, ('shard', 'rep'), pairs)  1.63 us
    pallas_call x1, Pallas kernels, per_device(): pl.pallas_call(functools.partial(best_kernel, stripe), out_shape=jax.Shap...  1.45 us
    pallas_call x1, Pallas kernels, per_device(): pl.pallas_call(functools.partial(place_kernel, chunks, send_cap), out_sha...  1.27 us
    ppermute x5, waiting for transfers between devices, swap(): lax.ppermute(array, 'rep', [(r, r ^ mask) for r in range(lax.axis_size('r...  1.19 us
  transfers between devices with their start and end apart: 13, of which 2 were waited for; matrix products, arithmetic and copies ran while one was open for 0% of the time, Pallas kernels for 16%

profile of v4, /device:TPU:11, one launch (start us, length us, event | category | flops | bytes accessed | tf_op | source)
XLA Modules:
  0.0 24.3 jit_solution(12902963248376997155)
XLA Ops:
  0.0 0.0 copy-start
  0.0 3.3 %collective-permute-start = (s32[1,1024]{1,0:T(1,128)}, s32[1,1024]{1,0:T(1,128)S(1)}, u32[]{:S(2)}, u32[]{:S(2)}) collective-permute-start(s32[1,1024]{1,0:T(1,128)} %ids_ref.1), channel_id=1, source_target_pairs={{0,16},{1,17},{2,22},{3,23},{4,20},{5,21},{6,18},{7,19},{8,24},{9,... | collective-permute-start | bytes 12296 | tf_op jit(solution)/shard_map/ppermute | solution.py:168
  3.3 0.0 collective-permute-start.2
  3.3 2.1 %collective-permute-start.4 = (s32[1,1024]{1,0:T(1,128)}, s32[1,1024]{1,0:T(1,128)S(1)}, u32[]{:S(2)}, u32[]{:S(2)}) collective-permute-start(s32[1,1024]{1,0:T(1,128)} %ids_ref.1), channel_id=1, source_target_pairs={{0,8},{1,13},{2,10},{3,15},{4,12},{5,9},{6,14},{7,11},{8,0},{9,5},... | collective-permute-start | bytes 12296 | tf_op jit(solution)/shard_map/ppermute | solution.py:168
  5.4 0.3 %collective-permute-start.5 = (s32[1,1024]{1,0:T(1,128)}, s32[1,1024]{1,0:T(1,128)S(1)}, u32[]{:S(2)}, u32[]{:S(2)}) collective-permute-start(s32[1,1024]{1,0:T(1,128)} %ids_ref.1), channel_id=1, source_target_pairs={{0,4},{1,5},{2,6},{3,7},{4,0},{5,1},{6,2},{7,3},{8,12},{9,13},{10,... | collective-permute-start | bytes 12296 | tf_op jit(solution)/shard_map/ppermute | solution.py:168
  5.7 0.0 collective-permute-done.refs_0_
  5.7 0.0 copy-done
  5.7 0.8 %shard_map.29.refs_2_ = bf16[64,512]{1,0:T(8,128)(2,1)S(1)} custom-call(s32[1,1024]{1,0:T(1,128)S(1)} %collective-permute-done.refs_0_, bf16[1024,512]{1,0:T(8,128)(2,1)S(1)} %copy-done, f32[8,128]{1,0:T(8,128)S(1)} %shard_map.28.refs_2_), custom_call_target="tpu_custom_call" | custom-call | flops 1000000000 | bytes 4096 | tf_op jit(solution)/shard_map/pallas_call | solution.py:209
  6.6 2.4 %collective-permute-start.1 = (bf16[64,512]{1,0:T(8,128)(2,1)S(1)}, bf16[64,512]{1,0:T(8,128)(2,1)S(1)}, u32[]{:S(2)}, u32[]{:S(2)}) collective-permute-start(bf16[64,512]{1,0:T(8,128)(2,1)S(1)} %shard_map.29.refs_2_), channel_id=1, source_target_pairs={{0,16},{1,17},{2,22},{3,23},{4,20},{5,21},{6,18},{7,19},{8,24},{9,... | collective-permute-start | bytes 196616 | tf_op jit(solution)/shard_map/ppermute | solution.py:168
  8.9 0.0 collective-permute-done.2.refs_0_
  8.9 0.9 %shard_map.32.refs_3_ = bf16[128,512]{1,0:T(8,128)(2,1)S(1)} custom-call(s32[1,1024]{1,0:T(1,128)S(1)} %collective-permute-done.2.refs_0_, bf16[1024,512]{1,0:T(8,128)(2,1)S(1)} %copy-done, bf16[64,512]{1,0:T(8,128)(2,1)S(1)} %shard_map.29.refs_2_), custom_call_target="tpu_custom_call" | custom-call | flops 1000000000 | bytes 4096 | tf_op jit(solution)/shard_map/pallas_call | solution.py:209
  9.8 0.0 collective-permute-done.4.refs_0_
  9.8 0.0 collective-permute-done.5.refs_1_
  9.8 1.0 %shard_map.33 = (bf16[128,512]{1,0:T(8,128)(2,1)S(1)}, bf16[128,512]{1,0:T(8,128)(2,1)S(1)}) custom-call(s32[1,1024]{1,0:T(1,128)S(1)} %collective-permute-done.4.refs_0_, s32[1,1024]{1,0:T(1,128)S(1)} %collective-permute-done.5.refs_1_, bf16[1024,512]{1,0:T(8,128)(2,1)S(1)} %copy-done, bf16[128,512]{1,0:T(8,128)(2,1)S(1)} %shard_map.32.refs_3_), custom_call_target="tpu_custom_call" | custom-call | flops 1000000000 | bytes 4096 | tf_op jit(solution)/shard_map/pallas_call | solution.py:209
  10.8 1.1 %collective-permute-start.6 = (bf16[128,512]{1,0:T(8,128)(2,1)S(1)}, bf16[128,512]{1,0:T(8,128)(2,1)S(1)}, u32[]{:S(2)}, u32[]{:S(2)}) collective-permute-start(bf16[128,512]{1,0:T(8,128)(2,1)S(1)} %get-tuple-element.11), channel_id=1, source_target_pairs={{0,8},{1,13},{2,10},{3,15},{4,12},{5,9},{6,14},{7,11},{8,0},{9,5},... | collective-permute-start | bytes 393224 | tf_op jit(solution)/shard_map/ppermute | solution.py:168
  11.9 1.1 %collective-permute-start.3 = (bf16[128,512]{1,0:T(8,128)(2,1)S(1)}, bf16[128,512]{1,0:T(8,128)(2,1)S(1)}, u32[]{:S(2)}, u32[]{:S(2)}) collective-permute-start(bf16[128,512]{1,0:T(8,128)(2,1)S(1)} %shard_map.32.refs_3_), channel_id=1, source_target_pairs={{0,24},{1,29},{2,26},{3,31},{4,28},{5,25},{6,30},{7,27},{8,16},{9,... | collective-permute-start | bytes 393224 | tf_op jit(solution)/shard_map/ppermute | solution.py:168
  13.0 0.0 collective-permute-done.1.rows_ref
  13.0 0.0 copy-start.1
  13.0 0.1 collective-permute-start.10
  13.1 0.4 %collective-permute-start.12 = (bf16[128,512]{1,0:T(8,128)(2,1)S(1)}, bf16[128,512]{1,0:T(8,128)(2,1)S(1)}, u32[]{:S(2)}, u32[]{:S(2)}) collective-permute-start(bf16[128,512]{1,0:T(8,128)(2,1)S(1)} %get-tuple-element.12), channel_id=1, source_target_pairs={{0,4},{1,5},{2,6},{3,7},{4,0},{5,1},{6,2},{7,3},{8,12},{9,13},{10,... | collective-permute-start | bytes 393224 | tf_op jit(solution)/shard_map/ppermute | solution.py:168
  13.5 1.7 %collective-permute-start.9 = (bf16[64,512]{1,0:T(8,128)(2,1)S(1)}, bf16[64,512]{1,0:T(8,128)(2,1)S(1)}, u32[]{:S(2)}, u32[]{:S(2)}) collective-permute-start(bf16[64,512]{1,0:T(8,128)(2,1)S(1)} %shard_map.30.refs_0_.refs_6_), channel_id=1, source_target_pairs={{0,1},{1,0},{2,3},{3,2},{4,5},{5,4},{6,7},{7,6},{8,9},{9,8},{10,11... | collective-permute-start | bytes 196616 | tf_op jit(solution)/shard_map/ppermute | solution.py:172
  15.1 0.0 copy-done.1
  15.1 1.3 %shard_map.31 = (f32[8,128]{1,0:T(8,128)S(1)}, bf16[128,512]{1,0:T(8,128)(2,1)S(1)}) custom-call(s32[1,1024]{1,0:T(1,128)S(1)} %copy-done.1, bf16[1024,512]{1,0:T(8,128)(2,1)S(1)} %copy-done, bf16[64,512]{1,0:T(8,128)(2,1)S(1)} %shard_map.30.refs_0_.refs_6_), custom_call_target="tpu_custom_call" | custom-call | flops 300000000 | bytes 4096 | tf_op jit(solution)/shard_map/pallas_call | solution.py:232
  16.4 0.0 collective-permute-done.6.rows_ref
  16.4 1.7 %collective-permute-start.8 = (bf16[128,512]{1,0:T(8,128)(2,1)S(1)}, bf16[128,512]{1,0:T(8,128)(2,1)S(1)}, u32[]{:S(2)}, u32[]{:S(2)}) collective-permute-start(bf16[128,512]{1,0:T(8,128)(2,1)S(1)} %shard_map.34.refs_3_), channel_id=1, source_target_pairs={{0,1},{1,0},{2,3},{3,2},{4,5},{5,4},{6,7},{7,6},{8,9},{9,8},{10,11... | collective-permute-start | bytes 393224 | tf_op jit(solution)/shard_map/ppermute | solution.py:172
  18.2 1.6 %collective-permute-done.3.refs_2_ = bf16[128,512]{1,0:T(8,128)(2,1)S(1)} collective-permute-done((bf16[128,512]{1,0:T(8,128)(2,1)S(1)}, bf16[128,512]{1,0:T(8,128)(2,1)S(1)}, u32[]{:S(2)}, u32[]{:S(2)}) %collective-permute-start.3) | collective-permute-done | bytes 131104 | tf_op jit(solution)/shard_map/ppermute | solution.py:168
  19.8 1.8 %collective-permute-start.7 = (bf16[128,512]{1,0:T(8,128)(2,1)S(1)}, bf16[128,512]{1,0:T(8,128)(2,1)S(1)}, u32[]{:S(2)}, u32[]{:S(2)}) collective-permute-start(bf16[128,512]{1,0:T(8,128)(2,1)S(1)} %collective-permute-done.3.refs_2_), channel_id=1, source_target_pairs={{0,1},{1,0},{2,3},{3,2},{4,5},{5,4},{6,7},{7,6},{8,9},{9,8},{10,11... | collective-permute-start | bytes 393224 | tf_op jit(solution)/shard_map/ppermute | solution.py:172
  21.6 0.0 collective-permute-done.10.rows_ref
  21.6 0.1 collective-permute-start.11
  21.7 0.0 collective-permute-done.9.refs_7_
  21.7 0.0 collective-permute-done.12.refs_10_
  21.7 1.2 %collective-permute-done.11.refs_9_ = bf16[64,512]{1,0:T(8,128)(2,1)S(1)} collective-permute-done((bf16[64,512]{1,0:T(8,128)(2,1)S(1)}, bf16[64,512]{1,0:T(8,128)(2,1)S(1)}, u32[]{:S(2)}, u32[]{:S(2)}) %collective-permute-start.11) | collective-permute-done | bytes 65568 | tf_op jit(solution)/shard_map/ppermute | solution.py:172
  22.9 0.0 collective-permute-done.8.refs_5_
  22.9 0.0 collective-permute-done.7.refs_4_
  22.9 1.4 %shard_map.36 = f32[1,256]{1,0:T(1,128)} custom-call(f32[8,128]{1,0:T(8,128)S(1)} %get-tuple-element.9.refs_0_, bf16[128,512]{1,0:T(8,128)(2,1)S(1)} %get-tuple-element.10.refs_1_, bf16[128,512]{1,0:T(8,128)(2,1)S(1)} %collective-permute-done.3.refs_2_, bf16[128,512]{1,0:T(8,128)(2,1)S(1)} %shard_map.34.refs_3_, ...), custom_call_target="tpu_custom_call" | custom-call | flops 1000000000 | bytes 2097152 | tf_op jit(solution)/shard_map/pallas_call | solution.py:244
  (4 shorter events, 0.0 us)
Async XLA Ops:
  0.0 5.7 %copy-start = (bf16[1024,512]{1,0:T(8,128)(2,1)S(1)}, bf16[1024,512]{1,0:T(8,128)(2,1)}, u32[]{:S(2)}) copy-start(bf16[1024,512]{1,0:T(8,128)(2,1)} %refs_2_.1) | copy-start | bytes 3145732
  0.0 5.7 %collective-permute-start = (s32[1,1024]{1,0:T(1,128)}, s32[1,1024]{1,0:T(1,128)S(1)}, u32[]{:S(2)}, u32[]{:S(2)}) collective-permute-start(s32[1,1024]{1,0:T(1,128)} %ids_ref.1), channel_id=1, source_target_pairs={{0,16},{1,17},{2,22},{3,23},{4,20},{5,21},{6,18},{7,19},{8,24},{9,... | collective-permute-start | bytes 12296 | tf_op jit(solution)/shard_map/ppermute | solution.py:168
  3.3 5.6 %collective-permute-start.2 = (s32[1,1024]{1,0:T(1,128)}, s32[1,1024]{1,0:T(1,128)S(1)}, u32[]{:S(2)}, u32[]{:S(2)}) collective-permute-start(s32[1,1024]{1,0:T(1,128)} %ids_ref.1), channel_id=1, source_target_pairs={{0,24},{1,29},{2,26},{3,31},{4,28},{5,25},{6,30},{7,27},{8,16},{9,... | collective-permute-start | bytes 12296 | tf_op jit(solution)/shard_map/ppermute | solution.py:168
  3.3 6.5 %collective-permute-start.4 = (s32[1,1024]{1,0:T(1,128)}, s32[1,1024]{1,0:T(1,128)S(1)}, u32[]{:S(2)}, u32[]{:S(2)}) collective-permute-start(s32[1,1024]{1,0:T(1,128)} %ids_ref.1), channel_id=1, source_target_pairs={{0,8},{1,13},{2,10},{3,15},{4,12},{5,9},{6,14},{7,11},{8,0},{9,5},... | collective-permute-start | bytes 12296 | tf_op jit(solution)/shard_map/ppermute | solution.py:168
  5.4 4.4 %collective-permute-start.5 = (s32[1,1024]{1,0:T(1,128)}, s32[1,1024]{1,0:T(1,128)S(1)}, u32[]{:S(2)}, u32[]{:S(2)}) collective-permute-start(s32[1,1024]{1,0:T(1,128)} %ids_ref.1), channel_id=1, source_target_pairs={{0,4},{1,5},{2,6},{3,7},{4,0},{5,1},{6,2},{7,3},{8,12},{9,13},{10,... | collective-permute-start | bytes 12296 | tf_op jit(solution)/shard_map/ppermute | solution.py:168
  6.6 6.5 %collective-permute-start.1 = (bf16[64,512]{1,0:T(8,128)(2,1)S(1)}, bf16[64,512]{1,0:T(8,128)(2,1)S(1)}, u32[]{:S(2)}, u32[]{:S(2)}) collective-permute-start(bf16[64,512]{1,0:T(8,128)(2,1)S(1)} %shard_map.29.refs_2_), channel_id=1, source_target_pairs={{0,16},{1,17},{2,22},{3,23},{4,20},{5,21},{6,18},{7,19},{8,24},{9,... | collective-permute-start | bytes 196616 | tf_op jit(solution)/shard_map/ppermute | solution.py:168
  10.8 5.6 %collective-permute-start.6 = (bf16[128,512]{1,0:T(8,128)(2,1)S(1)}, bf16[128,512]{1,0:T(8,128)(2,1)S(1)}, u32[]{:S(2)}, u32[]{:S(2)}) collective-permute-start(bf16[128,512]{1,0:T(8,128)(2,1)S(1)} %get-tuple-element.11), channel_id=1, source_target_pairs={{0,8},{1,13},{2,10},{3,15},{4,12},{5,9},{6,14},{7,11},{8,0},{9,5},... | collective-permute-start | bytes 393224 | tf_op jit(solution)/shard_map/ppermute | solution.py:168
  11.9 7.9 %collective-permute-start.3 = (bf16[128,512]{1,0:T(8,128)(2,1)S(1)}, bf16[128,512]{1,0:T(8,128)(2,1)S(1)}, u32[]{:S(2)}, u32[]{:S(2)}) collective-permute-start(bf16[128,512]{1,0:T(8,128)(2,1)S(1)} %shard_map.32.refs_3_), channel_id=1, source_target_pairs={{0,24},{1,29},{2,26},{3,31},{4,28},{5,25},{6,30},{7,27},{8,16},{9,... | collective-permute-start | bytes 393224 | tf_op jit(solution)/shard_map/ppermute | solution.py:168
  13.0 2.1 %copy-start.1 = (s32[1,1024]{1,0:T(1,128)S(1)}, s32[1,1024]{1,0:T(1,128)}, u32[]{:S(2)}) copy-start(s32[1,1024]{1,0:T(1,128)} %ids_ref.1) | copy-start | bytes 12292
  13.0 8.6 %collective-permute-start.10 = (bf16[64,512]{1,0:T(8,128)(2,1)S(1)}, bf16[64,512]{1,0:T(8,128)(2,1)S(1)}, u32[]{:S(2)}, u32[]{:S(2)}) collective-permute-start(bf16[64,512]{1,0:T(8,128)(2,1)S(1)} %shard_map.30.refs_0_.refs_6_), channel_id=1, source_target_pairs={{0,2},{1,3},{2,0},{3,1},{4,6},{5,7},{6,4},{7,5},{8,10},{9,11},{10,... | collective-permute-start | bytes 196616 | tf_op jit(solution)/shard_map/ppermute | solution.py:172
  13.1 8.6 %collective-permute-start.12 = (bf16[128,512]{1,0:T(8,128)(2,1)S(1)}, bf16[128,512]{1,0:T(8,128)(2,1)S(1)}, u32[]{:S(2)}, u32[]{:S(2)}) collective-permute-start(bf16[128,512]{1,0:T(8,128)(2,1)S(1)} %get-tuple-element.12), channel_id=1, source_target_pairs={{0,4},{1,5},{2,6},{3,7},{4,0},{5,1},{6,2},{7,3},{8,12},{9,13},{10,... | collective-permute-start | bytes 393224 | tf_op jit(solution)/shard_map/ppermute | solution.py:168
  13.5 8.2 %collective-permute-start.9 = (bf16[64,512]{1,0:T(8,128)(2,1)S(1)}, bf16[64,512]{1,0:T(8,128)(2,1)S(1)}, u32[]{:S(2)}, u32[]{:S(2)}) collective-permute-start(bf16[64,512]{1,0:T(8,128)(2,1)S(1)} %shard_map.30.refs_0_.refs_6_), channel_id=1, source_target_pairs={{0,1},{1,0},{2,3},{3,2},{4,5},{5,4},{6,7},{7,6},{8,9},{9,8},{10,11... | collective-permute-start | bytes 196616 | tf_op jit(solution)/shard_map/ppermute | solution.py:172
  16.4 6.4 %collective-permute-start.8 = (bf16[128,512]{1,0:T(8,128)(2,1)S(1)}, bf16[128,512]{1,0:T(8,128)(2,1)S(1)}, u32[]{:S(2)}, u32[]{:S(2)}) collective-permute-start(bf16[128,512]{1,0:T(8,128)(2,1)S(1)} %shard_map.34.refs_3_), channel_id=1, source_target_pairs={{0,1},{1,0},{2,3},{3,2},{4,5},{5,4},{6,7},{7,6},{8,9},{9,8},{10,11... | collective-permute-start | bytes 393224 | tf_op jit(solution)/shard_map/ppermute | solution.py:172
  19.8 3.1 %collective-permute-start.7 = (bf16[128,512]{1,0:T(8,128)(2,1)S(1)}, bf16[128,512]{1,0:T(8,128)(2,1)S(1)}, u32[]{:S(2)}, u32[]{:S(2)}) collective-permute-start(bf16[128,512]{1,0:T(8,128)(2,1)S(1)} %collective-permute-done.3.refs_2_), channel_id=1, source_target_pairs={{0,1},{1,0},{2,3},{3,2},{4,5},{5,4},{6,7},{7,6},{8,9},{9,8},{10,11... | collective-permute-start | bytes 393224 | tf_op jit(solution)/shard_map/ppermute | solution.py:172
  21.6 1.3 %collective-permute-start.11 = (bf16[64,512]{1,0:T(8,128)(2,1)S(1)}, bf16[64,512]{1,0:T(8,128)(2,1)S(1)}, u32[]{:S(2)}, u32[]{:S(2)}) collective-permute-start(bf16[64,512]{1,0:T(8,128)(2,1)S(1)} %shard_map.35.refs_8_), channel_id=1, source_target_pairs={{0,1},{1,0},{2,3},{3,2},{4,5},{5,4},{6,7},{7,6},{8,9},{9,8},{10,11... | collective-permute-start | bytes 196616 | tf_op jit(solution)/shard_map/ppermute | solution.py:172

commit v5 on v4

--- a/solution.py
+++ b/solution.py
@@ -27,23 +27,19 @@
     return ones_where(lax.broadcasted_iota(jnp.int32, (LANES, ids.shape[1]), 0) == (ids & (LANES - 1)))
 
 
-def high_onehot(ids, first_row, groups):
+def high_marks(ids, first_row, groups):
     high = (ids - first_row) >> 7
-    return lax.broadcasted_iota(jnp.int32, (groups, ids.shape[1]), 0) == high
-
-
-def slots_of(hit, groups):
-    total = hit.shape[0]
-    marks = hit.astype(jnp.bfloat16)
-    before = ones_where(
-        lax.broadcasted_iota(jnp.int32, (LANES, LANES), 0) < lax.broadcasted_iota(jnp.int32, (LANES, LANES), 1)
-    )
-    within = dot(marks, before)
-    sums = dot(marks, jnp.ones((LANES, LANES), jnp.bfloat16)).astype(jnp.bfloat16)
-    row = lax.broadcasted_iota(jnp.int32, (total, total), 0)
-    col = lax.broadcasted_iota(jnp.int32, (total, total), 1)
-    earlier = ones_where((col < row) & (col // groups == row // groups))
-    return jnp.where(hit > 0.0, within + dot(earlier, sums), -1.0)
+    row = lax.broadcasted_iota(jnp.int32, (2 * groups, ids.shape[1]), 0)
+    high = jnp.where(high < 0, groups, high)
+    return jnp.where(row < groups, jnp.where(high == row, 1.0, 0.0), jnp.where(high < row - groups, 1.0, 0.0))
+
+
+def slots_of(found, groups):
+    row = lax.broadcasted_iota(jnp.int32, (LANES, 2 * LANES), 0)
+    col = lax.broadcasted_iota(jnp.int32, (LANES, 2 * LANES), 1)
+    counts = dot(found.astype(jnp.bfloat16), ones_where((row < col) | (col >= LANES)))
+    slots = counts[:groups, :LANES] + counts[groups:, LANES:]
+    return jnp.where(found[:groups] > 0.0, slots, -1.0)
 
 
 def selector(slots, numbers):
@@ -78,16 +74,15 @@
     ids = ids_ref[...]
     low = low_onehot(ids)
     shard = lax.axis_index("shard")
-    highs = [high_onehot(ids, (shard ^ by_rep(d)) * groups * LANES, groups) for d, _ in chunks]
-    high = jnp.concatenate([jnp.where(h, 1.0, 0.0) for h in highs], axis=0)
+    highs = [high_marks(ids, (shard ^ by_rep(d)) * groups * LANES, groups) for d, _ in chunks]
+    here = jnp.concatenate([high[:groups] for high in highs], axis=0)
+    count = here.shape[0]
     member = lax.broadcasted_iota(jnp.int32, (1, ids.shape[1]), 1)
     digits = (member >> 5).astype(jnp.float32), (member & 31).astype(jnp.float32)
-    marks = jnp.concatenate([high, high * digits[0], high * digits[1]], axis=0).astype(jnp.bfloat16)
-    found = nt_dot(marks, low)
-    count = high.shape[0]
-    hit = found[:count]
-    position = found[count : 2 * count] * 32.0 + found[2 * count :]
-    slots = slots_of(hit, groups)
+    marks = [here] + [high[groups:] for high in highs] + [here * digits[0], here * digits[1]]
+    found = nt_dot(jnp.concatenate(marks, axis=0).astype(jnp.bfloat16), low)
+    slots = slots_of(found[: 2 * count], count)
+    position = found[2 * count : 3 * count] * 32.0 + found[3 * count :]
     diagonal = lax.broadcasted_iota(jnp.int32, (send_cap, send_cap), 0) == lax.broadcasted_iota(
         jnp.int32, (send_cap, send_cap), 1
     )
@@ -112,8 +107,9 @@
     hits = []
     for ref in ids_refs:
         ids = ref[...]
-        hits.append(nt_dot(ones_where(high_onehot(ids, first_row, 16)), low_onehot(ids))[:groups])
-    slots = slots_of(jnp.concatenate(hits, axis=0), groups)
+        hits.append(nt_dot(high_marks(ids, first_row, groups).astype(jnp.bfloat16), low_onehot(ids)))
+    hits = [hit[:groups] for hit in hits] + [hit[groups:] for hit in hits]
+    slots = slots_of(jnp.concatenate(hits, axis=0), count * groups)
     rows = rows_ref[...]
     for t in range(count):
         ref = out_refs[t]

time: 24.5 us -> 24.1 us (0.984)
  the two profiles are of different devices: /device:TPU:11 before, /device:TPU:0 now
where the time goes in v5:
time: 24.1 us; the launch traced here: 23.7 us
  starting transfers between devices  16.4 us (68%)
  Pallas kernels  4.96 us (21%)
  waiting for transfers between devices  2.18 us (9%)
    ppermute x8, starting transfers between devices, permute(): return lax.ppermute(array, ('shard', 'rep'), pairs)  12.8 us
    ppermute x5, starting transfers between devices, swap(): lax.ppermute(array, 'rep', [(r, r ^ mask) for r in range(lax.axis_size('r...  3.6 us
    pallas_call x3, Pallas kernels, per_device(): pl.pallas_call(functools.partial(select_kernel, [rounds[t] for t in group...  2.27 us
    ppermute x8, waiting for transfers between devices, permute(): return lax.ppermute(array, ('shard', 'rep'), pairs)  2.16 us
    pallas_call x1, Pallas kernels, per_device(): pl.pallas_call(functools.partial(best_kernel, stripe), out_shape=jax.Shap...  1.45 us
    pallas_call x1, Pallas kernels, per_device(): pl.pallas_call(functools.partial(place_kernel, chunks, send_cap), out_sha...  1.23 us
  transfers between devices with their start and end apart: 13, of which 2 were waited for; matrix products, arithmetic and copies ran while one was open for 0% of the time, Pallas kernels for 15%

profile of v5, /device:TPU:0, one launch (start us, length us, event | category | flops | bytes accessed | tf_op | source)
XLA Modules:
  0.0 23.7 jit_solution(15857732823734892555)
XLA Ops:
  0.0 0.0 copy-start
  0.0 4.0 %collective-permute-start = (s32[1,1024]{1,0:T(1,128)}, s32[1,1024]{1,0:T(1,128)S(1)}, u32[]{:S(2)}, u32[]{:S(2)}) collective-permute-start(s32[1,1024]{1,0:T(1,128)} %ids_ref.1), channel_id=1, source_target_pairs={{0,16},{1,17},{2,22},{3,23},{4,20},{5,21},{6,18},{7,19},{8,24},{9,... | collective-permute-start | bytes 12296 | tf_op jit(solution)/shard_map/ppermute | solution.py:164
  4.0 1.3 %collective-permute-start.2 = (s32[1,1024]{1,0:T(1,128)}, s32[1,1024]{1,0:T(1,128)S(1)}, u32[]{:S(2)}, u32[]{:S(2)}) collective-permute-start(s32[1,1024]{1,0:T(1,128)} %ids_ref.1), channel_id=1, source_target_pairs={{0,24},{1,29},{2,26},{3,31},{4,28},{5,25},{6,30},{7,27},{8,16},{9,... | collective-permute-start | bytes 12296 | tf_op jit(solution)/shard_map/ppermute | solution.py:164
  5.4 0.2 collective-permute-start.4
  5.6 1.5 %collective-permute-start.5 = (s32[1,1024]{1,0:T(1,128)}, s32[1,1024]{1,0:T(1,128)S(1)}, u32[]{:S(2)}, u32[]{:S(2)}) collective-permute-start(s32[1,1024]{1,0:T(1,128)} %ids_ref.1), channel_id=1, source_target_pairs={{0,4},{1,5},{2,6},{3,7},{4,0},{5,1},{6,2},{7,3},{8,12},{9,13},{10,... | collective-permute-start | bytes 12296 | tf_op jit(solution)/shard_map/ppermute | solution.py:164
  7.1 0.0 collective-permute-done.refs_0_
  7.1 0.0 copy-done
  7.1 0.7 %shard_map.29.refs_2_ = bf16[64,512]{1,0:T(8,128)(2,1)S(1)} custom-call(s32[1,1024]{1,0:T(1,128)S(1)} %collective-permute-done.refs_0_, bf16[1024,512]{1,0:T(8,128)(2,1)S(1)} %copy-done, f32[8,128]{1,0:T(8,128)S(1)} %shard_map.28.refs_2_), custom_call_target="tpu_custom_call" | custom-call | flops 1000000000 | bytes 4096 | tf_op jit(solution)/shard_map/pallas_call | solution.py:205
  7.8 2.9 %collective-permute-start.1 = (bf16[64,512]{1,0:T(8,128)(2,1)S(1)}, bf16[64,512]{1,0:T(8,128)(2,1)S(1)}, u32[]{:S(2)}, u32[]{:S(2)}) collective-permute-start(bf16[64,512]{1,0:T(8,128)(2,1)S(1)} %shard_map.29.refs_2_), channel_id=1, source_target_pairs={{0,16},{1,17},{2,22},{3,23},{4,20},{5,21},{6,18},{7,19},{8,24},{9,... | collective-permute-start | bytes 196616 | tf_op jit(solution)/shard_map/ppermute | solution.py:164
  10.7 0.0 collective-permute-done.2.refs_0_
  10.7 0.7 %shard_map.32.refs_3_ = bf16[128,512]{1,0:T(8,128)(2,1)S(1)} custom-call(s32[1,1024]{1,0:T(1,128)S(1)} %collective-permute-done.2.refs_0_, bf16[1024,512]{1,0:T(8,128)(2,1)S(1)} %copy-done, bf16[64,512]{1,0:T(8,128)(2,1)S(1)} %shard_map.29.refs_2_), custom_call_target="tpu_custom_call" | custom-call | flops 1000000000 | bytes 4096 | tf_op jit(solution)/shard_map/pallas_call | solution.py:205
  11.4 0.0 collective-permute-done.4.refs_0_
  11.4 0.0 collective-permute-done.5.refs_1_
  11.5 0.9 %shard_map.33 = (bf16[128,512]{1,0:T(8,128)(2,1)S(1)}, bf16[128,512]{1,0:T(8,128)(2,1)S(1)}) custom-call(s32[1,1024]{1,0:T(1,128)S(1)} %collective-permute-done.4.refs_0_, s32[1,1024]{1,0:T(1,128)S(1)} %collective-permute-done.5.refs_1_, bf16[1024,512]{1,0:T(8,128)(2,1)S(1)} %copy-done, bf16[128,512]{1,0:T(8,128)(2,1)S(1)} %shard_map.32.refs_3_), custom_call_target="tpu_custom_call" | custom-call | flops 1000000000 | bytes 4096 | tf_op jit(solution)/shard_map/pallas_call | solution.py:205
  12.3 0.7 %collective-permute-start.6 = (bf16[128,512]{1,0:T(8,128)(2,1)S(1)}, bf16[128,512]{1,0:T(8,128)(2,1)S(1)}, u32[]{:S(2)}, u32[]{:S(2)}) collective-permute-start(bf16[128,512]{1,0:T(8,128)(2,1)S(1)} %get-tuple-element.11), channel_id=1, source_target_pairs={{0,8},{1,13},{2,10},{3,15},{4,12},{5,9},{6,14},{7,11},{8,0},{9,5},... | collective-permute-start | bytes 393224 | tf_op jit(solution)/shard_map/ppermute | solution.py:164
  13.1 1.6 %collective-permute-start.3 = (bf16[128,512]{1,0:T(8,128)(2,1)S(1)}, bf16[128,512]{1,0:T(8,128)(2,1)S(1)}, u32[]{:S(2)}, u32[]{:S(2)}) collective-permute-start(bf16[128,512]{1,0:T(8,128)(2,1)S(1)} %shard_map.32.refs_3_), channel_id=1, source_target_pairs={{0,24},{1,29},{2,26},{3,31},{4,28},{5,25},{6,30},{7,27},{8,16},{9,... | collective-permute-start | bytes 393224 | tf_op jit(solution)/shard_map/ppermute | solution.py:164
  14.7 0.0 collective-permute-done.1.rows_ref
  14.7 0.0 copy-start.1
  14.7 2.5 %collective-permute-start.10 = (bf16[64,512]{1,0:T(8,128)(2,1)S(1)}, bf16[64,512]{1,0:T(8,128)(2,1)S(1)}, u32[]{:S(2)}, u32[]{:S(2)}) collective-permute-start(bf16[64,512]{1,0:T(8,128)(2,1)S(1)} %shard_map.30.refs_0_.refs_6_), channel_id=1, source_target_pairs={{0,2},{1,3},{2,0},{3,1},{4,6},{5,7},{6,4},{7,5},{8,10},{9,11},{10,... | collective-permute-start | bytes 196616 | tf_op jit(solution)/shard_map/ppermute | solution.py:168
  17.2 0.5 %collective-permute-start.12 = (bf16[128,512]{1,0:T(8,128)(2,1)S(1)}, bf16[128,512]{1,0:T(8,128)(2,1)S(1)}, u32[]{:S(2)}, u32[]{:S(2)}) collective-permute-start(bf16[128,512]{1,0:T(8,128)(2,1)S(1)} %get-tuple-element.12), channel_id=1, source_target_pairs={{0,4},{1,5},{2,6},{3,7},{4,0},{5,1},{6,2},{7,3},{8,12},{9,13},{10,... | collective-permute-start | bytes 393224 | tf_op jit(solution)/shard_map/ppermute | solution.py:164
  17.7 0.0 collective-permute-start.9
  17.7 0.0 copy-done.1
  17.7 1.2 %shard_map.31 = (f32[8,128]{1,0:T(8,128)S(1)}, bf16[128,512]{1,0:T(8,128)(2,1)S(1)}) custom-call(s32[1,1024]{1,0:T(1,128)S(1)} %copy-done.1, bf16[1024,512]{1,0:T(8,128)(2,1)S(1)} %copy-done, bf16[64,512]{1,0:T(8,128)(2,1)S(1)} %shard_map.30.refs_0_.refs_6_), custom_call_target="tpu_custom_call" | custom-call | flops 300000000 | bytes 4096 | tf_op jit(solution)/shard_map/pallas_call | solution.py:228
  18.9 0.0 collective-permute-done.6.rows_ref
  19.0 0.6 %collective-permute-start.8 = (bf16[128,512]{1,0:T(8,128)(2,1)S(1)}, bf16[128,512]{1,0:T(8,128)(2,1)S(1)}, u32[]{:S(2)}, u32[]{:S(2)}) collective-permute-start(bf16[128,512]{1,0:T(8,128)(2,1)S(1)} %shard_map.34.refs_3_), channel_id=1, source_target_pairs={{0,1},{1,0},{2,3},{3,2},{4,5},{5,4},{6,7},{7,6},{8,9},{9,8},{10,11... | collective-permute-start | bytes 393224 | tf_op jit(solution)/shard_map/ppermute | solution.py:168
  19.5 1.1 %collective-permute-done.3.refs_2_ = bf16[128,512]{1,0:T(8,128)(2,1)S(1)} collective-permute-done((bf16[128,512]{1,0:T(8,128)(2,1)S(1)}, bf16[128,512]{1,0:T(8,128)(2,1)S(1)}, u32[]{:S(2)}, u32[]{:S(2)}) %collective-permute-start.3) | collective-permute-done | bytes 131104 | tf_op jit(solution)/shard_map/ppermute | solution.py:164
  20.7 0.0 collective-permute-start.7
  20.7 0.0 collective-permute-done.10.rows_ref
  20.7 0.5 %collective-permute-start.11 = (bf16[64,512]{1,0:T(8,128)(2,1)S(1)}, bf16[64,512]{1,0:T(8,128)(2,1)S(1)}, u32[]{:S(2)}, u32[]{:S(2)}) collective-permute-start(bf16[64,512]{1,0:T(8,128)(2,1)S(1)} %shard_map.35.refs_8_), channel_id=1, source_target_pairs={{0,1},{1,0},{2,3},{3,2},{4,5},{5,4},{6,7},{7,6},{8,9},{9,8},{10,11... | collective-permute-start | bytes 196616 | tf_op jit(solution)/shard_map/ppermute | solution.py:168
  21.2 0.0 collective-permute-done.9.refs_7_
  21.2 1.0 %collective-permute-done.12.refs_10_ = bf16[128,512]{1,0:T(8,128)(2,1)S(1)} collective-permute-done((bf16[128,512]{1,0:T(8,128)(2,1)S(1)}, bf16[128,512]{1,0:T(8,128)(2,1)S(1)}, u32[]{:S(2)}, u32[]{:S(2)}) %collective-permute-start.12) | collective-permute-done | bytes 131104 | tf_op jit(solution)/shard_map/ppermute | solution.py:164
  22.2 0.0 collective-permute-done.11.refs_9_
  22.2 0.0 collective-permute-done.8.refs_5_
  22.2 0.0 collective-permute-done.7.refs_4_
  22.2 1.4 %shard_map.36 = f32[1,256]{1,0:T(1,128)} custom-call(f32[8,128]{1,0:T(8,128)S(1)} %get-tuple-element.9.refs_0_, bf16[128,512]{1,0:T(8,128)(2,1)S(1)} %get-tuple-element.10.refs_1_, bf16[128,512]{1,0:T(8,128)(2,1)S(1)} %collective-permute-done.3.refs_2_, bf16[128,512]{1,0:T(8,128)(2,1)S(1)} %shard_map.34.refs_3_, ...), custom_call_target="tpu_custom_call" | custom-call | flops 1000000000 | bytes 2097152 | tf_op jit(solution)/shard_map/pallas_call | solution.py:240
  (4 shorter events, 0.0 us)
Async XLA Ops:
  0.0 7.1 %copy-start = (bf16[1024,512]{1,0:T(8,128)(2,1)S(1)}, bf16[1024,512]{1,0:T(8,128)(2,1)}, u32[]{:S(2)}) copy-start(bf16[1024,512]{1,0:T(8,128)(2,1)} %refs_2_.1) | copy-start | bytes 3145732
  0.0 7.1 %collective-permute-start = (s32[1,1024]{1,0:T(1,128)}, s32[1,1024]{1,0:T(1,128)S(1)}, u32[]{:S(2)}, u32[]{:S(2)}) collective-permute-start(s32[1,1024]{1,0:T(1,128)} %ids_ref.1), channel_id=1, source_target_pairs={{0,16},{1,17},{2,22},{3,23},{4,20},{5,21},{6,18},{7,19},{8,24},{9,... | collective-permute-start | bytes 12296 | tf_op jit(solution)/shard_map/ppermute | solution.py:164
  4.0 6.7 %collective-permute-start.2 = (s32[1,1024]{1,0:T(1,128)}, s32[1,1024]{1,0:T(1,128)S(1)}, u32[]{:S(2)}, u32[]{:S(2)}) collective-permute-start(s32[1,1024]{1,0:T(1,128)} %ids_ref.1), channel_id=1, source_target_pairs={{0,24},{1,29},{2,26},{3,31},{4,28},{5,25},{6,30},{7,27},{8,16},{9,... | collective-permute-start | bytes 12296 | tf_op jit(solution)/shard_map/ppermute | solution.py:164
  5.4 6.0 %collective-permute-start.4 = (s32[1,1024]{1,0:T(1,128)}, s32[1,1024]{1,0:T(1,128)S(1)}, u32[]{:S(2)}, u32[]{:S(2)}) collective-permute-start(s32[1,1024]{1,0:T(1,128)} %ids_ref.1), channel_id=1, source_target_pairs={{0,8},{1,13},{2,10},{3,15},{4,12},{5,9},{6,14},{7,11},{8,0},{9,5},... | collective-permute-start | bytes 12296 | tf_op jit(solution)/shard_map/ppermute | solution.py:164
  5.6 5.8 %collective-permute-start.5 = (s32[1,1024]{1,0:T(1,128)}, s32[1,1024]{1,0:T(1,128)S(1)}, u32[]{:S(2)}, u32[]{:S(2)}) collective-permute-start(s32[1,1024]{1,0:T(1,128)} %ids_ref.1), channel_id=1, source_target_pairs={{0,4},{1,5},{2,6},{3,7},{4,0},{5,1},{6,2},{7,3},{8,12},{9,13},{10,... | collective-permute-start | bytes 12296 | tf_op jit(solution)/shard_map/ppermute | solution.py:164
  7.8 6.9 %collective-permute-start.1 = (bf16[64,512]{1,0:T(8,128)(2,1)S(1)}, bf16[64,512]{1,0:T(8,128)(2,1)S(1)}, u32[]{:S(2)}, u32[]{:S(2)}) collective-permute-start(bf16[64,512]{1,0:T(8,128)(2,1)S(1)} %shard_map.29.refs_2_), channel_id=1, source_target_pairs={{0,16},{1,17},{2,22},{3,23},{4,20},{5,21},{6,18},{7,19},{8,24},{9,... | collective-permute-start | bytes 196616 | tf_op jit(solution)/shard_map/ppermute | solution.py:164
  12.3 6.6 %collective-permute-start.6 = (bf16[128,512]{1,0:T(8,128)(2,1)S(1)}, bf16[128,512]{1,0:T(8,128)(2,1)S(1)}, u32[]{:S(2)}, u32[]{:S(2)}) collective-permute-start(bf16[128,512]{1,0:T(8,128)(2,1)S(1)} %get-tuple-element.11), channel_id=1, source_target_pairs={{0,8},{1,13},{2,10},{3,15},{4,12},{5,9},{6,14},{7,11},{8,0},{9,5},... | collective-permute-start | bytes 393224 | tf_op jit(solution)/shard_map/ppermute | solution.py:164
  13.1 7.6 %collective-permute-start.3 = (bf16[128,512]{1,0:T(8,128)(2,1)S(1)}, bf16[128,512]{1,0:T(8,128)(2,1)S(1)}, u32[]{:S(2)}, u32[]{:S(2)}) collective-permute-start(bf16[128,512]{1,0:T(8,128)(2,1)S(1)} %shard_map.32.refs_3_), channel_id=1, source_target_pairs={{0,24},{1,29},{2,26},{3,31},{4,28},{5,25},{6,30},{7,27},{8,16},{9,... | collective-permute-start | bytes 393224 | tf_op jit(solution)/shard_map/ppermute | solution.py:164
  14.7 3.0 %copy-start.1 = (s32[1,1024]{1,0:T(1,128)S(1)}, s32[1,1024]{1,0:T(1,128)}, u32[]{:S(2)}) copy-start(s32[1,1024]{1,0:T(1,128)} %ids_ref.1) | copy-start | bytes 12292
  14.7 6.0 %collective-permute-start.10 = (bf16[64,512]{1,0:T(8,128)(2,1)S(1)}, bf16[64,512]{1,0:T(8,128)(2,1)S(1)}, u32[]{:S(2)}, u32[]{:S(2)}) collective-permute-start(bf16[64,512]{1,0:T(8,128)(2,1)S(1)} %shard_map.30.refs_0_.refs_6_), channel_id=1, source_target_pairs={{0,2},{1,3},{2,0},{3,1},{4,6},{5,7},{6,4},{7,5},{8,10},{9,11},{10,... | collective-permute-start | bytes 196616 | tf_op jit(solution)/shard_map/ppermute | solution.py:168
  17.2 5.0 %collective-permute-start.12 = (bf16[128,512]{1,0:T(8,128)(2,1)S(1)}, bf16[128,512]{1,0:T(8,128)(2,1)S(1)}, u32[]{:S(2)}, u32[]{:S(2)}) collective-permute-start(bf16[128,512]{1,0:T(8,128)(2,1)S(1)} %get-tuple-element.12), channel_id=1, source_target_pairs={{0,4},{1,5},{2,6},{3,7},{4,0},{5,1},{6,2},{7,3},{8,12},{9,13},{10,... | collective-permute-start | bytes 393224 | tf_op jit(solution)/shard_map/ppermute | solution.py:164
  17.7 3.5 %collective-permute-start.9 = (bf16[64,512]{1,0:T(8,128)(2,1)S(1)}, bf16[64,512]{1,0:T(8,128)(2,1)S(1)}, u32[]{:S(2)}, u32[]{:S(2)}) collective-permute-start(bf16[64,512]{1,0:T(8,128)(2,1)S(1)} %shard_map.30.refs_0_.refs_6_), channel_id=1, source_target_pairs={{0,1},{1,0},{2,3},{3,2},{4,5},{5,4},{6,7},{7,6},{8,9},{9,8},{10,11... | collective-permute-start | bytes 196616 | tf_op jit(solution)/shard_map/ppermute | solution.py:168
  19.0 3.2 %collective-permute-start.8 = (bf16[128,512]{1,0:T(8,128)(2,1)S(1)}, bf16[128,512]{1,0:T(8,128)(2,1)S(1)}, u32[]{:S(2)}, u32[]{:S(2)}) collective-permute-start(bf16[128,512]{1,0:T(8,128)(2,1)S(1)} %shard_map.34.refs_3_), channel_id=1, source_target_pairs={{0,1},{1,0},{2,3},{3,2},{4,5},{5,4},{6,7},{7,6},{8,9},{9,8},{10,11... | collective-permute-start | bytes 393224 | tf_op jit(solution)/shard_map/ppermute | solution.py:168
  20.7 1.5 %collective-permute-start.7 = (bf16[128,512]{1,0:T(8,128)(2,1)S(1)}, bf16[128,512]{1,0:T(8,128)(2,1)S(1)}, u32[]{:S(2)}, u32[]{:S(2)}) collective-permute-start(bf16[128,512]{1,0:T(8,128)(2,1)S(1)} %collective-permute-done.3.refs_2_), channel_id=1, source_target_pairs={{0,1},{1,0},{2,3},{3,2},{4,5},{5,4},{6,7},{7,6},{8,9},{9,8},{10,11... | collective-permute-start | bytes 393224 | tf_op jit(solution)/shard_map/ppermute | solution.py:168
  20.7 1.5 %collective-permute-start.11 = (bf16[64,512]{1,0:T(8,128)(2,1)S(1)}, bf16[64,512]{1,0:T(8,128)(2,1)S(1)}, u32[]{:S(2)}, u32[]{:S(2)}) collective-permute-start(bf16[64,512]{1,0:T(8,128)(2,1)S(1)} %shard_map.35.refs_8_), channel_id=1, source_target_pairs={{0,1},{1,0},{2,3},{3,2},{4,5},{5,4},{6,7},{7,6},{8,9},{9,8},{10,11... | collective-permute-start | bytes 196616 | tf_op jit(solution)/shard_map/ppermute | solution.py:168

commit v6 on v5

--- a/solution.py
+++ b/solution.py
@@ -62,10 +62,13 @@
     out_ref[...] = jnp.zeros(out_ref.shape, out_ref.dtype)
 
 
-def pick_rows(slots, numbers, rows):
-    values = dot(selector(slots, numbers), rows)
+def scaled(values):
     total = jnp.sum(values * values, axis=1, keepdims=True)
     return (values * lax.rsqrt(total + 1e-06)).astype(jnp.bfloat16)
+
+
+def pick_rows(slots, numbers, rows):
+    return scaled(dot(selector(slots, numbers), rows))
 
 
 def place_kernel(chunks, send_cap, ids_ref, rows_ref, *refs):
@@ -110,11 +113,15 @@
         hits.append(nt_dot(high_marks(ids, first_row, groups).astype(jnp.bfloat16), low_onehot(ids)))
     hits = [hit[:groups] for hit in hits] + [hit[groups:] for hit in hits]
     slots = slots_of(jnp.concatenate(hits, axis=0), count * groups)
-    rows = rows_ref[...]
-    for t in range(count):
-        ref = out_refs[t]
+    marks = []
+    for t, ref in enumerate(out_refs):
         numbers = numbers_from(by_rep(rounds[t][1]), ref.shape[0], send_cap)
-        ref[...] = pick_rows(slots[t * groups : (t + 1) * groups], numbers, rows)
+        marks.append(selector(slots[t * groups : (t + 1) * groups], numbers))
+    picked = scaled(dot(jnp.concatenate(marks, axis=0), rows_ref[...]))
+    start = 0
+    for ref in out_refs:
+        ref[...] = picked[start : start + ref.shape[0], :]
+        start += ref.shape[0]
 
 
 def hand_on_kernel(rows_ref, *refs):

time: 24.1 us -> 24 us (level)
  no operation moved by 1% of the time
where the time goes in v6:
time: 24 us; the launch traced here: 23.7 us
  starting transfers between devices  16.4 us (68%)
  Pallas kernels  4.95 us (21%)
  waiting for transfers between devices  2.18 us (9%)
    ppermute x8, starting transfers between devices, permute(): return lax.ppermute(array, ('shard', 'rep'), pairs)  12.8 us
    ppermute x5, starting transfers between devices, swap(): lax.ppermute(array, 'rep', [(r, r ^ mask) for r in range(lax.axis_size('r...  3.59 us
    pallas_call x3, Pallas kernels, per_device(): pl.pallas_call(functools.partial(select_kernel, [rounds[t] for t in group...  2.26 us
    ppermute x8, waiting for transfers between devices, permute(): return lax.ppermute(array, ('shard', 'rep'), pairs)  2.16 us
    pallas_call x1, Pallas kernels, per_device(): pl.pallas_call(functools.partial(best_kernel, stripe), out_shape=jax.Shap...  1.45 us
    pallas_call x1, Pallas kernels, per_device(): pl.pallas_call(functools.partial(place_kernel, chunks, send_cap), out_sha...  1.23 us
  transfers between devices with their start and end apart: 13, of which 2 were waited for; matrix products, arithmetic and copies ran while one was open for 0% of the time, Pallas kernels for 15%

profile of v6, /device:TPU:0, one launch (start us, length us, event | category | flops | bytes accessed | tf_op | source)
XLA Modules:
  0.0 23.7 jit_solution(9764723558010194492)
XLA Ops:
  0.0 0.0 copy-start
  0.0 4.0 %collective-permute-start = (s32[1,1024]{1,0:T(1,128)}, s32[1,1024]{1,0:T(1,128)S(1)}, u32[]{:S(2)}, u32[]{:S(2)}) collective-permute-start(s32[1,1024]{1,0:T(1,128)} %ids_ref.1), channel_id=1, source_target_pairs={{0,16},{1,17},{2,22},{3,23},{4,20},{5,21},{6,18},{7,19},{8,24},{9,... | collective-permute-start | bytes 12296 | tf_op jit(solution)/shard_map/ppermute | solution.py:171
  4.0 1.3 %collective-permute-start.2 = (s32[1,1024]{1,0:T(1,128)}, s32[1,1024]{1,0:T(1,128)S(1)}, u32[]{:S(2)}, u32[]{:S(2)}) collective-permute-start(s32[1,1024]{1,0:T(1,128)} %ids_ref.1), channel_id=1, source_target_pairs={{0,24},{1,29},{2,26},{3,31},{4,28},{5,25},{6,30},{7,27},{8,16},{9,... | collective-permute-start | bytes 12296 | tf_op jit(solution)/shard_map/ppermute | solution.py:171
  5.4 0.2 collective-permute-start.4
  5.6 1.5 %collective-permute-start.5 = (s32[1,1024]{1,0:T(1,128)}, s32[1,1024]{1,0:T(1,128)S(1)}, u32[]{:S(2)}, u32[]{:S(2)}) collective-permute-start(s32[1,1024]{1,0:T(1,128)} %ids_ref.1), channel_id=1, source_target_pairs={{0,4},{1,5},{2,6},{3,7},{4,0},{5,1},{6,2},{7,3},{8,12},{9,13},{10,... | collective-permute-start | bytes 12296 | tf_op jit(solution)/shard_map/ppermute | solution.py:171
  7.1 0.0 collective-permute-done.refs_0_
  7.1 0.0 copy-done
  7.1 0.7 %shard_map.29.refs_2_ = bf16[64,512]{1,0:T(8,128)(2,1)S(1)} custom-call(s32[1,1024]{1,0:T(1,128)S(1)} %collective-permute-done.refs_0_, bf16[1024,512]{1,0:T(8,128)(2,1)S(1)} %copy-done, f32[8,128]{1,0:T(8,128)S(1)} %shard_map.28.refs_2_), custom_call_target="tpu_custom_call" | custom-call | flops 1000000000 | bytes 4096 | tf_op jit(solution)/shard_map/pallas_call | solution.py:212
  7.8 2.9 %collective-permute-start.1 = (bf16[64,512]{1,0:T(8,128)(2,1)S(1)}, bf16[64,512]{1,0:T(8,128)(2,1)S(1)}, u32[]{:S(2)}, u32[]{:S(2)}) collective-permute-start(bf16[64,512]{1,0:T(8,128)(2,1)S(1)} %shard_map.29.refs_2_), channel_id=1, source_target_pairs={{0,16},{1,17},{2,22},{3,23},{4,20},{5,21},{6,18},{7,19},{8,24},{9,... | collective-permute-start | bytes 196616 | tf_op jit(solution)/shard_map/ppermute | solution.py:171
  10.7 0.0 collective-permute-done.2.refs_0_
  10.7 0.7 %shard_map.32.refs_3_ = bf16[128,512]{1,0:T(8,128)(2,1)S(1)} custom-call(s32[1,1024]{1,0:T(1,128)S(1)} %collective-permute-done.2.refs_0_, bf16[1024,512]{1,0:T(8,128)(2,1)S(1)} %copy-done, bf16[64,512]{1,0:T(8,128)(2,1)S(1)} %shard_map.29.refs_2_), custom_call_target="tpu_custom_call" | custom-call | flops 1000000000 | bytes 4096 | tf_op jit(solution)/shard_map/pallas_call | solution.py:212
  11.4 0.0 collective-permute-done.4.refs_0_
  11.4 0.0 collective-permute-done.5.refs_1_
  11.5 0.9 %shard_map.33 = (bf16[128,512]{1,0:T(8,128)(2,1)S(1)}, bf16[128,512]{1,0:T(8,128)(2,1)S(1)}) custom-call(s32[1,1024]{1,0:T(1,128)S(1)} %collective-permute-done.4.refs_0_, s32[1,1024]{1,0:T(1,128)S(1)} %collective-permute-done.5.refs_1_, bf16[1024,512]{1,0:T(8,128)(2,1)S(1)} %copy-done, bf16[128,512]{1,0:T(8,128)(2,1)S(1)} %shard_map.32.refs_3_), custom_call_target="tpu_custom_call" | custom-call | flops 1000000000 | bytes 4096 | tf_op jit(solution)/shard_map/pallas_call | solution.py:212
  12.3 0.7 %collective-permute-start.6 = (bf16[128,512]{1,0:T(8,128)(2,1)S(1)}, bf16[128,512]{1,0:T(8,128)(2,1)S(1)}, u32[]{:S(2)}, u32[]{:S(2)}) collective-permute-start(bf16[128,512]{1,0:T(8,128)(2,1)S(1)} %get-tuple-element.11), channel_id=1, source_target_pairs={{0,8},{1,13},{2,10},{3,15},{4,12},{5,9},{6,14},{7,11},{8,0},{9,5},... | collective-permute-start | bytes 393224 | tf_op jit(solution)/shard_map/ppermute | solution.py:171
  13.1 1.6 %collective-permute-start.3 = (bf16[128,512]{1,0:T(8,128)(2,1)S(1)}, bf16[128,512]{1,0:T(8,128)(2,1)S(1)}, u32[]{:S(2)}, u32[]{:S(2)}) collective-permute-start(bf16[128,512]{1,0:T(8,128)(2,1)S(1)} %shard_map.32.refs_3_), channel_id=1, source_target_pairs={{0,24},{1,29},{2,26},{3,31},{4,28},{5,25},{6,30},{7,27},{8,16},{9,... | collective-permute-start | bytes 393224 | tf_op jit(solution)/shard_map/ppermute | solution.py:171
  14.7 0.0 collective-permute-done.1.rows_ref
  14.7 0.0 copy-start.1
  14.7 2.5 %collective-permute-start.10 = (bf16[64,512]{1,0:T(8,128)(2,1)S(1)}, bf16[64,512]{1,0:T(8,128)(2,1)S(1)}, u32[]{:S(2)}, u32[]{:S(2)}) collective-permute-start(bf16[64,512]{1,0:T(8,128)(2,1)S(1)} %shard_map.30.refs_0_.refs_6_), channel_id=1, source_target_pairs={{0,2},{1,3},{2,0},{3,1},{4,6},{5,7},{6,4},{7,5},{8,10},{9,11},{10,... | collective-permute-start | bytes 196616 | tf_op jit(solution)/shard_map/ppermute | solution.py:175
  17.2 0.5 %collective-permute-start.12 = (bf16[128,512]{1,0:T(8,128)(2,1)S(1)}, bf16[128,512]{1,0:T(8,128)(2,1)S(1)}, u32[]{:S(2)}, u32[]{:S(2)}) collective-permute-start(bf16[128,512]{1,0:T(8,128)(2,1)S(1)} %get-tuple-element.12), channel_id=1, source_target_pairs={{0,4},{1,5},{2,6},{3,7},{4,0},{5,1},{6,2},{7,3},{8,12},{9,13},{10,... | collective-permute-start | bytes 393224 | tf_op jit(solution)/shard_map/ppermute | solution.py:171
  17.7 0.0 collective-permute-start.9
  17.7 0.0 copy-done.1
  17.7 1.2 %shard_map.31 = (f32[8,128]{1,0:T(8,128)S(1)}, bf16[128,512]{1,0:T(8,128)(2,1)S(1)}) custom-call(s32[1,1024]{1,0:T(1,128)S(1)} %copy-done.1, bf16[1024,512]{1,0:T(8,128)(2,1)S(1)} %copy-done, bf16[64,512]{1,0:T(8,128)(2,1)S(1)} %shard_map.30.refs_0_.refs_6_), custom_call_target="tpu_custom_call" | custom-call | flops 300000000 | bytes 4096 | tf_op jit(solution)/shard_map/pallas_call | solution.py:235
  18.9 0.0 collective-permute-done.6.rows_ref
  18.9 0.6 %collective-permute-start.8 = (bf16[128,512]{1,0:T(8,128)(2,1)S(1)}, bf16[128,512]{1,0:T(8,128)(2,1)S(1)}, u32[]{:S(2)}, u32[]{:S(2)}) collective-permute-start(bf16[128,512]{1,0:T(8,128)(2,1)S(1)} %shard_map.34.refs_3_), channel_id=1, source_target_pairs={{0,1},{1,0},{2,3},{3,2},{4,5},{5,4},{6,7},{7,6},{8,9},{9,8},{10,11... | collective-permute-start | bytes 393224 | tf_op jit(solution)/shard_map/ppermute | solution.py:175
  19.5 1.1 %collective-permute-done.3.refs_2_ = bf16[128,512]{1,0:T(8,128)(2,1)S(1)} collective-permute-done((bf16[128,512]{1,0:T(8,128)(2,1)S(1)}, bf16[128,512]{1,0:T(8,128)(2,1)S(1)}, u32[]{:S(2)}, u32[]{:S(2)}) %collective-permute-start.3) | collective-permute-done | bytes 131104 | tf_op jit(solution)/shard_map/ppermute | solution.py:171
  20.7 0.0 collective-permute-start.7
  20.7 0.0 collective-permute-done.10.rows_ref
  20.7 0.5 %collective-permute-start.11 = (bf16[64,512]{1,0:T(8,128)(2,1)S(1)}, bf16[64,512]{1,0:T(8,128)(2,1)S(1)}, u32[]{:S(2)}, u32[]{:S(2)}) collective-permute-start(bf16[64,512]{1,0:T(8,128)(2,1)S(1)} %shard_map.35.refs_8_), channel_id=1, source_target_pairs={{0,1},{1,0},{2,3},{3,2},{4,5},{5,4},{6,7},{7,6},{8,9},{9,8},{10,11... | collective-permute-start | bytes 196616 | tf_op jit(solution)/shard_map/ppermute | solution.py:175
  21.2 0.0 collective-permute-done.9.refs_7_
  21.2 1.0 %collective-permute-done.12.refs_10_ = bf16[128,512]{1,0:T(8,128)(2,1)S(1)} collective-permute-done((bf16[128,512]{1,0:T(8,128)(2,1)S(1)}, bf16[128,512]{1,0:T(8,128)(2,1)S(1)}, u32[]{:S(2)}, u32[]{:S(2)}) %collective-permute-start.12) | collective-permute-done | bytes 131104 | tf_op jit(solution)/shard_map/ppermute | solution.py:171
  22.2 0.0 collective-permute-done.11.refs_9_
  22.2 0.0 collective-permute-done.8.refs_5_
  22.2 0.0 collective-permute-done.7.refs_4_
  22.2 1.5 %shard_map.36 = f32[1,256]{1,0:T(1,128)} custom-call(f32[8,128]{1,0:T(8,128)S(1)} %get-tuple-element.9.refs_0_, bf16[128,512]{1,0:T(8,128)(2,1)S(1)} %get-tuple-element.10.refs_1_, bf16[128,512]{1,0:T(8,128)(2,1)S(1)} %collective-permute-done.3.refs_2_, bf16[128,512]{1,0:T(8,128)(2,1)S(1)} %shard_map.34.refs_3_, ...), custom_call_target="tpu_custom_call" | custom-call | flops 1000000000 | bytes 2097152 | tf_op jit(solution)/shard_map/pallas_call | solution.py:247
  (4 shorter events, 0.0 us)
Async XLA Ops:
  0.0 7.1 %copy-start = (bf16[1024,512]{1,0:T(8,128)(2,1)S(1)}, bf16[1024,512]{1,0:T(8,128)(2,1)}, u32[]{:S(2)}) copy-start(bf16[1024,512]{1,0:T(8,128)(2,1)} %refs_2_.1) | copy-start | bytes 3145732
  0.0 7.1 %collective-permute-start = (s32[1,1024]{1,0:T(1,128)}, s32[1,1024]{1,0:T(1,128)S(1)}, u32[]{:S(2)}, u32[]{:S(2)}) collective-permute-start(s32[1,1024]{1,0:T(1,128)} %ids_ref.1), channel_id=1, source_target_pairs={{0,16},{1,17},{2,22},{3,23},{4,20},{5,21},{6,18},{7,19},{8,24},{9,... | collective-permute-start | bytes 12296 | tf_op jit(solution)/shard_map/ppermute | solution.py:171
  4.0 6.7 %collective-permute-start.2 = (s32[1,1024]{1,0:T(1,128)}, s32[1,1024]{1,0:T(1,128)S(1)}, u32[]{:S(2)}, u32[]{:S(2)}) collective-permute-start(s32[1,1024]{1,0:T(1,128)} %ids_ref.1), channel_id=1, source_target_pairs={{0,24},{1,29},{2,26},{3,31},{4,28},{5,25},{6,30},{7,27},{8,16},{9,... | collective-permute-start | bytes 12296 | tf_op jit(solution)/shard_map/ppermute | solution.py:171
  5.4 6.0 %collective-permute-start.4 = (s32[1,1024]{1,0:T(1,128)}, s32[1,1024]{1,0:T(1,128)S(1)}, u32[]{:S(2)}, u32[]{:S(2)}) collective-permute-start(s32[1,1024]{1,0:T(1,128)} %ids_ref.1), channel_id=1, source_target_pairs={{0,8},{1,13},{2,10},{3,15},{4,12},{5,9},{6,14},{7,11},{8,0},{9,5},... | collective-permute-start | bytes 12296 | tf_op jit(solution)/shard_map/ppermute | solution.py:171
  5.6 5.8 %collective-permute-start.5 = (s32[1,1024]{1,0:T(1,128)}, s32[1,1024]{1,0:T(1,128)S(1)}, u32[]{:S(2)}, u32[]{:S(2)}) collective-permute-start(s32[1,1024]{1,0:T(1,128)} %ids_ref.1), channel_id=1, source_target_pairs={{0,4},{1,5},{2,6},{3,7},{4,0},{5,1},{6,2},{7,3},{8,12},{9,13},{10,... | collective-permute-start | bytes 12296 | tf_op jit(solution)/shard_map/ppermute | solution.py:171
  7.8 6.8 %collective-permute-start.1 = (bf16[64,512]{1,0:T(8,128)(2,1)S(1)}, bf16[64,512]{1,0:T(8,128)(2,1)S(1)}, u32[]{:S(2)}, u32[]{:S(2)}) collective-permute-start(bf16[64,512]{1,0:T(8,128)(2,1)S(1)} %shard_map.29.refs_2_), channel_id=1, source_target_pairs={{0,16},{1,17},{2,22},{3,23},{4,20},{5,21},{6,18},{7,19},{8,24},{9,... | collective-permute-start | bytes 196616 | tf_op jit(solution)/shard_map/ppermute | solution.py:171
  12.3 6.6 %collective-permute-start.6 = (bf16[128,512]{1,0:T(8,128)(2,1)S(1)}, bf16[128,512]{1,0:T(8,128)(2,1)S(1)}, u32[]{:S(2)}, u32[]{:S(2)}) collective-permute-start(bf16[128,512]{1,0:T(8,128)(2,1)S(1)} %get-tuple-element.11), channel_id=1, source_target_pairs={{0,8},{1,13},{2,10},{3,15},{4,12},{5,9},{6,14},{7,11},{8,0},{9,5},... | collective-permute-start | bytes 393224 | tf_op jit(solution)/shard_map/ppermute | solution.py:171
  13.1 7.6 %collective-permute-start.3 = (bf16[128,512]{1,0:T(8,128)(2,1)S(1)}, bf16[128,512]{1,0:T(8,128)(2,1)S(1)}, u32[]{:S(2)}, u32[]{:S(2)}) collective-permute-start(bf16[128,512]{1,0:T(8,128)(2,1)S(1)} %shard_map.32.refs_3_), channel_id=1, source_target_pairs={{0,24},{1,29},{2,26},{3,31},{4,28},{5,25},{6,30},{7,27},{8,16},{9,... | collective-permute-start | bytes 393224 | tf_op jit(solution)/shard_map/ppermute | solution.py:171
  14.7 3.0 %copy-start.1 = (s32[1,1024]{1,0:T(1,128)S(1)}, s32[1,1024]{1,0:T(1,128)}, u32[]{:S(2)}) copy-start(s32[1,1024]{1,0:T(1,128)} %ids_ref.1) | copy-start | bytes 12292
  14.7 6.0 %collective-permute-start.10 = (bf16[64,512]{1,0:T(8,128)(2,1)S(1)}, bf16[64,512]{1,0:T(8,128)(2,1)S(1)}, u32[]{:S(2)}, u32[]{:S(2)}) collective-permute-start(bf16[64,512]{1,0:T(8,128)(2,1)S(1)} %shard_map.30.refs_0_.refs_6_), channel_id=1, source_target_pairs={{0,2},{1,3},{2,0},{3,1},{4,6},{5,7},{6,4},{7,5},{8,10},{9,11},{10,... | collective-permute-start | bytes 196616 | tf_op jit(solution)/shard_map/ppermute | solution.py:175
  17.2 5.0 %collective-permute-start.12 = (bf16[128,512]{1,0:T(8,128)(2,1)S(1)}, bf16[128,512]{1,0:T(8,128)(2,1)S(1)}, u32[]{:S(2)}, u32[]{:S(2)}) collective-permute-start(bf16[128,512]{1,0:T(8,128)(2,1)S(1)} %get-tuple-element.12), channel_id=1, source_target_pairs={{0,4},{1,5},{2,6},{3,7},{4,0},{5,1},{6,2},{7,3},{8,12},{9,13},{10,... | collective-permute-start | bytes 393224 | tf_op jit(solution)/shard_map/ppermute | solution.py:171
  17.7 3.5 %collective-permute-start.9 = (bf16[64,512]{1,0:T(8,128)(2,1)S(1)}, bf16[64,512]{1,0:T(8,128)(2,1)S(1)}, u32[]{:S(2)}, u32[]{:S(2)}) collective-permute-start(bf16[64,512]{1,0:T(8,128)(2,1)S(1)} %shard_map.30.refs_0_.refs_6_), channel_id=1, source_target_pairs={{0,1},{1,0},{2,3},{3,2},{4,5},{5,4},{6,7},{7,6},{8,9},{9,8},{10,11... | collective-permute-start | bytes 196616 | tf_op jit(solution)/shard_map/ppermute | solution.py:175
  18.9 3.2 %collective-permute-start.8 = (bf16[128,512]{1,0:T(8,128)(2,1)S(1)}, bf16[128,512]{1,0:T(8,128)(2,1)S(1)}, u32[]{:S(2)}, u32[]{:S(2)}) collective-permute-start(bf16[128,512]{1,0:T(8,128)(2,1)S(1)} %shard_map.34.refs_3_), channel_id=1, source_target_pairs={{0,1},{1,0},{2,3},{3,2},{4,5},{5,4},{6,7},{7,6},{8,9},{9,8},{10,11... | collective-permute-start | bytes 393224 | tf_op jit(solution)/shard_map/ppermute | solution.py:175
  20.7 1.5 %collective-permute-start.7 = (bf16[128,512]{1,0:T(8,128)(2,1)S(1)}, bf16[128,512]{1,0:T(8,128)(2,1)S(1)}, u32[]{:S(2)}, u32[]{:S(2)}) collective-permute-start(bf16[128,512]{1,0:T(8,128)(2,1)S(1)} %collective-permute-done.3.refs_2_), channel_id=1, source_target_pairs={{0,1},{1,0},{2,3},{3,2},{4,5},{5,4},{6,7},{7,6},{8,9},{9,8},{10,11... | collective-permute-start | bytes 393224 | tf_op jit(solution)/shard_map/ppermute | solution.py:175
  20.7 1.5 %collective-permute-start.11 = (bf16[64,512]{1,0:T(8,128)(2,1)S(1)}, bf16[64,512]{1,0:T(8,128)(2,1)S(1)}, u32[]{:S(2)}, u32[]{:S(2)}) collective-permute-start(bf16[64,512]{1,0:T(8,128)(2,1)S(1)} %shard_map.35.refs_8_), channel_id=1, source_target_pairs={{0,1},{1,0},{2,3},{3,2},{4,5},{5,4},{6,7},{7,6},{8,9},{9,8},{10,11... | collective-permute-start | bytes 196616 | tf_op jit(solution)/shard_map/ppermute | solution.py:175

commit v7 on v5

--- a/solution.py
+++ b/solution.py
@@ -35,10 +35,10 @@
 
 
 def slots_of(found, groups):
-    row = lax.broadcasted_iota(jnp.int32, (LANES, 2 * LANES), 0)
-    col = lax.broadcasted_iota(jnp.int32, (LANES, 2 * LANES), 1)
-    counts = dot(found.astype(jnp.bfloat16), ones_where((row < col) | (col >= LANES)))
-    slots = counts[:groups, :LANES] + counts[groups:, LANES:]
+    row = lax.broadcasted_iota(jnp.int32, (LANES, LANES), 0)
+    col = lax.broadcasted_iota(jnp.int32, (LANES, LANES), 1)
+    within = dot(found[:groups].astype(jnp.bfloat16), ones_where(row < col))
+    slots = within + jnp.sum(found[groups:], axis=1, keepdims=True)
     return jnp.where(found[:groups] > 0.0, slots, -1.0)
 
 

time: 24.1 us -> 24 us (level)
  no operation moved by 1% of the time
where the time goes in v7:
time: 24 us; the launch traced here: 23.7 us
  starting transfers between devices  16.4 us (68%)
  Pallas kernels  4.94 us (21%)
  waiting for transfers between devices  2.19 us (9%)
    ppermute x8, starting transfers between devices, permute(): return lax.ppermute(array, ('shard', 'rep'), pairs)  12.8 us
    ppermute x5, starting transfers between devices, swap(): lax.ppermute(array, 'rep', [(r, r ^ mask) for r in range(lax.axis_size('r...  3.59 us
    pallas_call x3, Pallas kernels, per_device(): pl.pallas_call(functools.partial(select_kernel, [rounds[t] for t in group...  2.27 us
    ppermute x8, waiting for transfers between devices, permute(): return lax.ppermute(array, ('shard', 'rep'), pairs)  2.18 us
    pallas_call x1, Pallas kernels, per_device(): pl.pallas_call(functools.partial(best_kernel, stripe), out_shape=jax.Shap...  1.45 us
    pallas_call x1, Pallas kernels, per_device(): pl.pallas_call(functools.partial(place_kernel, chunks, send_cap), out_sha...  1.22 us
  transfers between devices with their start and end apart: 13, of which 2 were waited for; matrix products, arithmetic and copies ran while one was open for 0% of the time, Pallas kernels for 15%

profile of v7, /device:TPU:0, one launch (start us, length us, event | category | flops | bytes accessed | tf_op | source)
XLA Modules:
  0.0 23.7 jit_solution(9092930174967850643)
XLA Ops:
  0.0 0.0 copy-start
  0.0 4.0 %collective-permute-start = (s32[1,1024]{1,0:T(1,128)}, s32[1,1024]{1,0:T(1,128)S(1)}, u32[]{:S(2)}, u32[]{:S(2)}) collective-permute-start(s32[1,1024]{1,0:T(1,128)} %ids_ref.1), channel_id=1, source_target_pairs={{0,16},{1,17},{2,22},{3,23},{4,20},{5,21},{6,18},{7,19},{8,24},{9,... | collective-permute-start | bytes 12296 | tf_op jit(solution)/shard_map/ppermute | solution.py:164
  4.0 1.3 %collective-permute-start.2 = (s32[1,1024]{1,0:T(1,128)}, s32[1,1024]{1,0:T(1,128)S(1)}, u32[]{:S(2)}, u32[]{:S(2)}) collective-permute-start(s32[1,1024]{1,0:T(1,128)} %ids_ref.1), channel_id=1, source_target_pairs={{0,24},{1,29},{2,26},{3,31},{4,28},{5,25},{6,30},{7,27},{8,16},{9,... | collective-permute-start | bytes 12296 | tf_op jit(solution)/shard_map/ppermute | solution.py:164
  5.4 0.2 collective-permute-start.4
  5.6 1.5 %collective-permute-start.5 = (s32[1,1024]{1,0:T(1,128)}, s32[1,1024]{1,0:T(1,128)S(1)}, u32[]{:S(2)}, u32[]{:S(2)}) collective-permute-start(s32[1,1024]{1,0:T(1,128)} %ids_ref.1), channel_id=1, source_target_pairs={{0,4},{1,5},{2,6},{3,7},{4,0},{5,1},{6,2},{7,3},{8,12},{9,13},{10,... | collective-permute-start | bytes 12296 | tf_op jit(solution)/shard_map/ppermute | solution.py:164
  7.1 0.0 collective-permute-done.refs_0_
  7.1 0.0 copy-done
  7.1 0.7 %shard_map.29.refs_2_ = bf16[64,512]{1,0:T(8,128)(2,1)S(1)} custom-call(s32[1,1024]{1,0:T(1,128)S(1)} %collective-permute-done.refs_0_, bf16[1024,512]{1,0:T(8,128)(2,1)S(1)} %copy-done, f32[8,128]{1,0:T(8,128)S(1)} %shard_map.28.refs_2_), custom_call_target="tpu_custom_call" | custom-call | flops 1000000000 | bytes 4096 | tf_op jit(solution)/shard_map/pallas_call | solution.py:205
  7.8 2.9 %collective-permute-start.1 = (bf16[64,512]{1,0:T(8,128)(2,1)S(1)}, bf16[64,512]{1,0:T(8,128)(2,1)S(1)}, u32[]{:S(2)}, u32[]{:S(2)}) collective-permute-start(bf16[64,512]{1,0:T(8,128)(2,1)S(1)} %shard_map.29.refs_2_), channel_id=1, source_target_pairs={{0,16},{1,17},{2,22},{3,23},{4,20},{5,21},{6,18},{7,19},{8,24},{9,... | collective-permute-start | bytes 196616 | tf_op jit(solution)/shard_map/ppermute | solution.py:164
  10.7 0.0 collective-permute-done.2.refs_0_
  10.7 0.7 %shard_map.32.refs_3_ = bf16[128,512]{1,0:T(8,128)(2,1)S(1)} custom-call(s32[1,1024]{1,0:T(1,128)S(1)} %collective-permute-done.2.refs_0_, bf16[1024,512]{1,0:T(8,128)(2,1)S(1)} %copy-done, bf16[64,512]{1,0:T(8,128)(2,1)S(1)} %shard_map.29.refs_2_), custom_call_target="tpu_custom_call" | custom-call | flops 1000000000 | bytes 4096 | tf_op jit(solution)/shard_map/pallas_call | solution.py:205
  11.4 0.0 collective-permute-done.4.refs_0_
  11.4 0.0 collective-permute-done.5.refs_1_
  11.4 0.9 %shard_map.33 = (bf16[128,512]{1,0:T(8,128)(2,1)S(1)}, bf16[128,512]{1,0:T(8,128)(2,1)S(1)}) custom-call(s32[1,1024]{1,0:T(1,128)S(1)} %collective-permute-done.4.refs_0_, s32[1,1024]{1,0:T(1,128)S(1)} %collective-permute-done.5.refs_1_, bf16[1024,512]{1,0:T(8,128)(2,1)S(1)} %copy-done, bf16[128,512]{1,0:T(8,128)(2,1)S(1)} %shard_map.32.refs_3_), custom_call_target="tpu_custom_call" | custom-call | flops 1000000000 | bytes 4096 | tf_op jit(solution)/shard_map/pallas_call | solution.py:205
  12.3 0.7 %collective-permute-start.6 = (bf16[128,512]{1,0:T(8,128)(2,1)S(1)}, bf16[128,512]{1,0:T(8,128)(2,1)S(1)}, u32[]{:S(2)}, u32[]{:S(2)}) collective-permute-start(bf16[128,512]{1,0:T(8,128)(2,1)S(1)} %get-tuple-element.11), channel_id=1, source_target_pairs={{0,8},{1,13},{2,10},{3,15},{4,12},{5,9},{6,14},{7,11},{8,0},{9,5},... | collective-permute-start | bytes 393224 | tf_op jit(solution)/shard_map/ppermute | solution.py:164
  13.1 1.6 %collective-permute-start.3 = (bf16[128,512]{1,0:T(8,128)(2,1)S(1)}, bf16[128,512]{1,0:T(8,128)(2,1)S(1)}, u32[]{:S(2)}, u32[]{:S(2)}) collective-permute-start(bf16[128,512]{1,0:T(8,128)(2,1)S(1)} %shard_map.32.refs_3_), channel_id=1, source_target_pairs={{0,24},{1,29},{2,26},{3,31},{4,28},{5,25},{6,30},{7,27},{8,16},{9,... | collective-permute-start | bytes 393224 | tf_op jit(solution)/shard_map/ppermute | solution.py:164
  14.7 0.0 collective-permute-done.1.rows_ref
  14.7 0.0 copy-start.1
  14.7 2.5 %collective-permute-start.10 = (bf16[64,512]{1,0:T(8,128)(2,1)S(1)}, bf16[64,512]{1,0:T(8,128)(2,1)S(1)}, u32[]{:S(2)}, u32[]{:S(2)}) collective-permute-start(bf16[64,512]{1,0:T(8,128)(2,1)S(1)} %shard_map.30.refs_0_.refs_6_), channel_id=1, source_target_pairs={{0,2},{1,3},{2,0},{3,1},{4,6},{5,7},{6,4},{7,5},{8,10},{9,11},{10,... | collective-permute-start | bytes 196616 | tf_op jit(solution)/shard_map/ppermute | solution.py:168
  17.2 0.5 %collective-permute-start.12 = (bf16[128,512]{1,0:T(8,128)(2,1)S(1)}, bf16[128,512]{1,0:T(8,128)(2,1)S(1)}, u32[]{:S(2)}, u32[]{:S(2)}) collective-permute-start(bf16[128,512]{1,0:T(8,128)(2,1)S(1)} %get-tuple-element.12), channel_id=1, source_target_pairs={{0,4},{1,5},{2,6},{3,7},{4,0},{5,1},{6,2},{7,3},{8,12},{9,13},{10,... | collective-permute-start | bytes 393224 | tf_op jit(solution)/shard_map/ppermute | solution.py:164
  17.7 0.0 collective-permute-start.9
  17.7 0.0 copy-done.1
  17.7 1.2 %shard_map.31 = (f32[8,128]{1,0:T(8,128)S(1)}, bf16[128,512]{1,0:T(8,128)(2,1)S(1)}) custom-call(s32[1,1024]{1,0:T(1,128)S(1)} %copy-done.1, bf16[1024,512]{1,0:T(8,128)(2,1)S(1)} %copy-done, bf16[64,512]{1,0:T(8,128)(2,1)S(1)} %shard_map.30.refs_0_.refs_6_), custom_call_target="tpu_custom_call" | custom-call | flops 300000000 | bytes 4096 | tf_op jit(solution)/shard_map/pallas_call | solution.py:228
  18.9 0.0 collective-permute-done.6.rows_ref
  18.9 0.6 %collective-permute-start.8 = (bf16[128,512]{1,0:T(8,128)(2,1)S(1)}, bf16[128,512]{1,0:T(8,128)(2,1)S(1)}, u32[]{:S(2)}, u32[]{:S(2)}) collective-permute-start(bf16[128,512]{1,0:T(8,128)(2,1)S(1)} %shard_map.34.refs_3_), channel_id=1, source_target_pairs={{0,1},{1,0},{2,3},{3,2},{4,5},{5,4},{6,7},{7,6},{8,9},{9,8},{10,11... | collective-permute-start | bytes 393224 | tf_op jit(solution)/shard_map/ppermute | solution.py:168
  19.5 1.2 %collective-permute-done.3.refs_2_ = bf16[128,512]{1,0:T(8,128)(2,1)S(1)} collective-permute-done((bf16[128,512]{1,0:T(8,128)(2,1)S(1)}, bf16[128,512]{1,0:T(8,128)(2,1)S(1)}, u32[]{:S(2)}, u32[]{:S(2)}) %collective-permute-start.3) | collective-permute-done | bytes 131104 | tf_op jit(solution)/shard_map/ppermute | solution.py:164
  20.7 0.0 collective-permute-start.7
  20.7 0.0 collective-permute-done.10.rows_ref
  20.7 0.5 %collective-permute-start.11 = (bf16[64,512]{1,0:T(8,128)(2,1)S(1)}, bf16[64,512]{1,0:T(8,128)(2,1)S(1)}, u32[]{:S(2)}, u32[]{:S(2)}) collective-permute-start(bf16[64,512]{1,0:T(8,128)(2,1)S(1)} %shard_map.35.refs_8_), channel_id=1, source_target_pairs={{0,1},{1,0},{2,3},{3,2},{4,5},{5,4},{6,7},{7,6},{8,9},{9,8},{10,11... | collective-permute-start | bytes 196616 | tf_op jit(solution)/shard_map/ppermute | solution.py:168
  21.2 0.0 collective-permute-done.9.refs_7_
  21.2 1.0 %collective-permute-done.12.refs_10_ = bf16[128,512]{1,0:T(8,128)(2,1)S(1)} collective-permute-done((bf16[128,512]{1,0:T(8,128)(2,1)S(1)}, bf16[128,512]{1,0:T(8,128)(2,1)S(1)}, u32[]{:S(2)}, u32[]{:S(2)}) %collective-permute-start.12) | collective-permute-done | bytes 131104 | tf_op jit(solution)/shard_map/ppermute | solution.py:164
  22.2 0.0 collective-permute-done.11.refs_9_
  22.2 0.0 collective-permute-done.8.refs_5_
  22.2 0.0 collective-permute-done.7.refs_4_
  22.2 1.4 %shard_map.36 = f32[1,256]{1,0:T(1,128)} custom-call(f32[8,128]{1,0:T(8,128)S(1)} %get-tuple-element.9.refs_0_, bf16[128,512]{1,0:T(8,128)(2,1)S(1)} %get-tuple-element.10.refs_1_, bf16[128,512]{1,0:T(8,128)(2,1)S(1)} %collective-permute-done.3.refs_2_, bf16[128,512]{1,0:T(8,128)(2,1)S(1)} %shard_map.34.refs_3_, ...), custom_call_target="tpu_custom_call" | custom-call | flops 1000000000 | bytes 2097152 | tf_op jit(solution)/shard_map/pallas_call | solution.py:240
  (4 shorter events, 0.0 us)
Async XLA Ops:
  0.0 7.1 %copy-start = (bf16[1024,512]{1,0:T(8,128)(2,1)S(1)}, bf16[1024,512]{1,0:T(8,128)(2,1)}, u32[]{:S(2)}) copy-start(bf16[1024,512]{1,0:T(8,128)(2,1)} %refs_2_.1) | copy-start | bytes 3145732
  0.0 7.1 %collective-permute-start = (s32[1,1024]{1,0:T(1,128)}, s32[1,1024]{1,0:T(1,128)S(1)}, u32[]{:S(2)}, u32[]{:S(2)}) collective-permute-start(s32[1,1024]{1,0:T(1,128)} %ids_ref.1), channel_id=1, source_target_pairs={{0,16},{1,17},{2,22},{3,23},{4,20},{5,21},{6,18},{7,19},{8,24},{9,... | collective-permute-start | bytes 12296 | tf_op jit(solution)/shard_map/ppermute | solution.py:164
  4.0 6.6 %collective-permute-start.2 = (s32[1,1024]{1,0:T(1,128)}, s32[1,1024]{1,0:T(1,128)S(1)}, u32[]{:S(2)}, u32[]{:S(2)}) collective-permute-start(s32[1,1024]{1,0:T(1,128)} %ids_ref.1), channel_id=1, source_target_pairs={{0,24},{1,29},{2,26},{3,31},{4,28},{5,25},{6,30},{7,27},{8,16},{9,... | collective-permute-start | bytes 12296 | tf_op jit(solution)/shard_map/ppermute | solution.py:164
  5.4 6.0 %collective-permute-start.4 = (s32[1,1024]{1,0:T(1,128)}, s32[1,1024]{1,0:T(1,128)S(1)}, u32[]{:S(2)}, u32[]{:S(2)}) collective-permute-start(s32[1,1024]{1,0:T(1,128)} %ids_ref.1), channel_id=1, source_target_pairs={{0,8},{1,13},{2,10},{3,15},{4,12},{5,9},{6,14},{7,11},{8,0},{9,5},... | collective-permute-start | bytes 12296 | tf_op jit(solution)/shard_map/ppermute | solution.py:164
  5.6 5.8 %collective-permute-start.5 = (s32[1,1024]{1,0:T(1,128)}, s32[1,1024]{1,0:T(1,128)S(1)}, u32[]{:S(2)}, u32[]{:S(2)}) collective-permute-start(s32[1,1024]{1,0:T(1,128)} %ids_ref.1), channel_id=1, source_target_pairs={{0,4},{1,5},{2,6},{3,7},{4,0},{5,1},{6,2},{7,3},{8,12},{9,13},{10,... | collective-permute-start | bytes 12296 | tf_op jit(solution)/shard_map/ppermute | solution.py:164
  7.8 6.9 %collective-permute-start.1 = (bf16[64,512]{1,0:T(8,128)(2,1)S(1)}, bf16[64,512]{1,0:T(8,128)(2,1)S(1)}, u32[]{:S(2)}, u32[]{:S(2)}) collective-permute-start(bf16[64,512]{1,0:T(8,128)(2,1)S(1)} %shard_map.29.refs_2_), channel_id=1, source_target_pairs={{0,16},{1,17},{2,22},{3,23},{4,20},{5,21},{6,18},{7,19},{8,24},{9,... | collective-permute-start | bytes 196616 | tf_op jit(solution)/shard_map/ppermute | solution.py:164
  12.3 6.6 %collective-permute-start.6 = (bf16[128,512]{1,0:T(8,128)(2,1)S(1)}, bf16[128,512]{1,0:T(8,128)(2,1)S(1)}, u32[]{:S(2)}, u32[]{:S(2)}) collective-permute-start(bf16[128,512]{1,0:T(8,128)(2,1)S(1)} %get-tuple-element.11), channel_id=1, source_target_pairs={{0,8},{1,13},{2,10},{3,15},{4,12},{5,9},{6,14},{7,11},{8,0},{9,5},... | collective-permute-start | bytes 393224 | tf_op jit(solution)/shard_map/ppermute | solution.py:164
  13.1 7.6 %collective-permute-start.3 = (bf16[128,512]{1,0:T(8,128)(2,1)S(1)}, bf16[128,512]{1,0:T(8,128)(2,1)S(1)}, u32[]{:S(2)}, u32[]{:S(2)}) collective-permute-start(bf16[128,512]{1,0:T(8,128)(2,1)S(1)} %shard_map.32.refs_3_), channel_id=1, source_target_pairs={{0,24},{1,29},{2,26},{3,31},{4,28},{5,25},{6,30},{7,27},{8,16},{9,... | collective-permute-start | bytes 393224 | tf_op jit(solution)/shard_map/ppermute | solution.py:164
  14.7 3.0 %copy-start.1 = (s32[1,1024]{1,0:T(1,128)S(1)}, s32[1,1024]{1,0:T(1,128)}, u32[]{:S(2)}) copy-start(s32[1,1024]{1,0:T(1,128)} %ids_ref.1) | copy-start | bytes 12292
  14.7 6.0 %collective-permute-start.10 = (bf16[64,512]{1,0:T(8,128)(2,1)S(1)}, bf16[64,512]{1,0:T(8,128)(2,1)S(1)}, u32[]{:S(2)}, u32[]{:S(2)}) collective-permute-start(bf16[64,512]{1,0:T(8,128)(2,1)S(1)} %shard_map.30.refs_0_.refs_6_), channel_id=1, source_target_pairs={{0,2},{1,3},{2,0},{3,1},{4,6},{5,7},{6,4},{7,5},{8,10},{9,11},{10,... | collective-permute-start | bytes 196616 | tf_op jit(solution)/shard_map/ppermute | solution.py:168
  17.2 5.0 %collective-permute-start.12 = (bf16[128,512]{1,0:T(8,128)(2,1)S(1)}, bf16[128,512]{1,0:T(8,128)(2,1)S(1)}, u32[]{:S(2)}, u32[]{:S(2)}) collective-permute-start(bf16[128,512]{1,0:T(8,128)(2,1)S(1)} %get-tuple-element.12), channel_id=1, source_target_pairs={{0,4},{1,5},{2,6},{3,7},{4,0},{5,1},{6,2},{7,3},{8,12},{9,13},{10,... | collective-permute-start | bytes 393224 | tf_op jit(solution)/shard_map/ppermute | solution.py:164
  17.7 3.5 %collective-permute-start.9 = (bf16[64,512]{1,0:T(8,128)(2,1)S(1)}, bf16[64,512]{1,0:T(8,128)(2,1)S(1)}, u32[]{:S(2)}, u32[]{:S(2)}) collective-permute-start(bf16[64,512]{1,0:T(8,128)(2,1)S(1)} %shard_map.30.refs_0_.refs_6_), channel_id=1, source_target_pairs={{0,1},{1,0},{2,3},{3,2},{4,5},{5,4},{6,7},{7,6},{8,9},{9,8},{10,11... | collective-permute-start | bytes 196616 | tf_op jit(solution)/shard_map/ppermute | solution.py:168
  18.9 3.3 %collective-permute-start.8 = (bf16[128,512]{1,0:T(8,128)(2,1)S(1)}, bf16[128,512]{1,0:T(8,128)(2,1)S(1)}, u32[]{:S(2)}, u32[]{:S(2)}) collective-permute-start(bf16[128,512]{1,0:T(8,128)(2,1)S(1)} %shard_map.34.refs_3_), channel_id=1, source_target_pairs={{0,1},{1,0},{2,3},{3,2},{4,5},{5,4},{6,7},{7,6},{8,9},{9,8},{10,11... | collective-permute-start | bytes 393224 | tf_op jit(solution)/shard_map/ppermute | solution.py:168
  20.7 1.5 %collective-permute-start.7 = (bf16[128,512]{1,0:T(8,128)(2,1)S(1)}, bf16[128,512]{1,0:T(8,128)(2,1)S(1)}, u32[]{:S(2)}, u32[]{:S(2)}) collective-permute-start(bf16[128,512]{1,0:T(8,128)(2,1)S(1)} %collective-permute-done.3.refs_2_), channel_id=1, source_target_pairs={{0,1},{1,0},{2,3},{3,2},{4,5},{5,4},{6,7},{7,6},{8,9},{9,8},{10,11... | collective-permute-start | bytes 393224 | tf_op jit(solution)/shard_map/ppermute | solution.py:168
  20.7 1.5 %collective-permute-start.11 = (bf16[64,512]{1,0:T(8,128)(2,1)S(1)}, bf16[64,512]{1,0:T(8,128)(2,1)S(1)}, u32[]{:S(2)}, u32[]{:S(2)}) collective-permute-start(bf16[64,512]{1,0:T(8,128)(2,1)S(1)} %shard_map.35.refs_8_), channel_id=1, source_target_pairs={{0,1},{1,0},{2,3},{3,2},{4,5},{5,4},{6,7},{7,6},{8,9},{9,8},{10,11... | collective-permute-start | bytes 196616 | tf_op jit(solution)/shard_map/ppermute | solution.py:168

commit v8 on v5

--- a/solution.py
+++ b/solution.py
@@ -180,7 +180,7 @@
     reps = range(helpers)
     zero = [0] * helpers
     far = ([shards - 4 + (r >> 1) for r in reps], [half * (r & 1) for r in reps])
-    pairs = [([d + (r & 1) for r in reps], zero) for d in (shards - 2, shards - 6)]
+    pairs = [([shards - 2 + (r & 1) for r in reps], zero), ([shards - 6 + (r & 1 ^ 1 - (r >> 1)) for r in reps], zero)]
     near = ([1] * helpers, zero)
     rounds = [far] + pairs + [near]
     chunks = [(zero, zero), near]

time: 24.1 us -> 24.1 us (level)
  waiting for transfers between devices: 2.18 us -> 2.8 us
  starting transfers between devices: 16.4 us -> 15.9 us
    ppermute x5, starting transfers between devices: 3.6 us -> 2.19 us  [swap(): lax.ppermute(array, 'rep', [(r, r ^ mask) for r in range(lax.axis_size('r...]
    ppermute x8, starting transfers between devices: 12.8 us -> 13.7 us  [permute(): return lax.ppermute(array, ('shard', 'rep'), pairs)]
    ppermute x8, waiting for transfers between devices: 2.16 us -> 2.68 us  [permute(): return lax.ppermute(array, ('shard', 'rep'), pairs)]
  transfers between devices with their start and end apart: 13 -> 13, of which waited for: 2 -> 4; matrix products, arithmetic and copies ran while one was open for 0% -> 0% of each run, Pallas kernels for 15% -> 15%
where the time goes in v8:
time: 24.1 us; the launch traced here: 23.8 us
  starting transfers between devices  15.9 us (66%)
  Pallas kernels  4.96 us (21%)
  waiting for transfers between devices  2.8 us (12%)
    ppermute x8, starting transfers between devices, permute(): return lax.ppermute(array, ('shard', 'rep'), pairs)  13.7 us
    ppermute x8, waiting for transfers between devices, permute(): return lax.ppermute(array, ('shard', 'rep'), pairs)  2.68 us
    pallas_call x3, Pallas kernels, per_device(): pl.pallas_call(functools.partial(select_kernel, [rounds[t] for t in group...  2.27 us
    ppermute x5, starting transfers between devices, swap(): lax.ppermute(array, 'rep', [(r, r ^ mask) for r in range(lax.axis_size('r...  2.19 us
    pallas_call x1, Pallas kernels, per_device(): pl.pallas_call(functools.partial(best_kernel, stripe), out_shape=jax.Shap...  1.45 us
    pallas_call x1, Pallas kernels, per_device(): pl.pallas_call(functools.partial(place_kernel, chunks, send_cap), out_sha...  1.23 us
  transfers between devices with their start and end apart: 13, of which 4 were waited for; matrix products, arithmetic and copies ran while one was open for 0% of the time, Pallas kernels for 15%

profile of v8, /device:TPU:0, one launch (start us, length us, event | category | flops | bytes accessed | tf_op | source)
XLA Modules:
  0.0 23.8 jit_solution(4679379893617778186)
XLA Ops:
  0.0 0.0 copy-start
  0.0 4.0 %collective-permute-start = (s32[1,1024]{1,0:T(1,128)}, s32[1,1024]{1,0:T(1,128)S(1)}, u32[]{:S(2)}, u32[]{:S(2)}) collective-permute-start(s32[1,1024]{1,0:T(1,128)} %ids_ref.1), channel_id=1, source_target_pairs={{0,16},{1,17},{2,22},{3,23},{4,20},{5,21},{6,18},{7,19},{8,24},{9,... | collective-permute-start | bytes 12296 | tf_op jit(solution)/shard_map/ppermute | solution.py:164
  4.0 1.3 %collective-permute-start.2 = (s32[1,1024]{1,0:T(1,128)}, s32[1,1024]{1,0:T(1,128)S(1)}, u32[]{:S(2)}, u32[]{:S(2)}) collective-permute-start(s32[1,1024]{1,0:T(1,128)} %ids_ref.1), channel_id=1, source_target_pairs={{0,24},{1,29},{2,26},{3,31},{4,28},{5,25},{6,30},{7,27},{8,16},{9,... | collective-permute-start | bytes 12296 | tf_op jit(solution)/shard_map/ppermute | solution.py:164
  5.4 1.2 %collective-permute-start.4 = (s32[1,1024]{1,0:T(1,128)}, s32[1,1024]{1,0:T(1,128)S(1)}, u32[]{:S(2)}, u32[]{:S(2)}) collective-permute-start(s32[1,1024]{1,0:T(1,128)} %ids_ref.1), channel_id=1, source_target_pairs={{0,12},{1,9},{2,10},{3,15},{4,8},{5,13},{6,14},{7,11},{8,4},{9,1},... | collective-permute-start | bytes 12296 | tf_op jit(solution)/shard_map/ppermute | solution.py:164
  6.6 0.5 %collective-permute-start.5 = (s32[1,1024]{1,0:T(1,128)}, s32[1,1024]{1,0:T(1,128)S(1)}, u32[]{:S(2)}, u32[]{:S(2)}) collective-permute-start(s32[1,1024]{1,0:T(1,128)} %ids_ref.1), channel_id=1, source_target_pairs={{0,4},{1,5},{2,6},{3,7},{4,0},{5,1},{6,2},{7,3},{8,12},{9,13},{10,... | collective-permute-start | bytes 12296 | tf_op jit(solution)/shard_map/ppermute | solution.py:164
  7.1 0.0 collective-permute-done.refs_0_
  7.1 0.0 copy-done
  7.1 0.7 %shard_map.29.refs_2_ = bf16[64,512]{1,0:T(8,128)(2,1)S(1)} custom-call(s32[1,1024]{1,0:T(1,128)S(1)} %collective-permute-done.refs_0_, bf16[1024,512]{1,0:T(8,128)(2,1)S(1)} %copy-done, f32[8,128]{1,0:T(8,128)S(1)} %shard_map.28.refs_2_), custom_call_target="tpu_custom_call" | custom-call | flops 1000000000 | bytes 4096 | tf_op jit(solution)/shard_map/pallas_call | solution.py:205
  7.8 2.9 %collective-permute-start.1 = (bf16[64,512]{1,0:T(8,128)(2,1)S(1)}, bf16[64,512]{1,0:T(8,128)(2,1)S(1)}, u32[]{:S(2)}, u32[]{:S(2)}) collective-permute-start(bf16[64,512]{1,0:T(8,128)(2,1)S(1)} %shard_map.29.refs_2_), channel_id=1, source_target_pairs={{0,16},{1,17},{2,22},{3,23},{4,20},{5,21},{6,18},{7,19},{8,24},{9,... | collective-permute-start | bytes 196616 | tf_op jit(solution)/shard_map/ppermute | solution.py:164
  10.6 0.0 collective-permute-done.2.refs_0_
  10.6 0.7 %shard_map.32.refs_3_ = bf16[128,512]{1,0:T(8,128)(2,1)S(1)} custom-call(s32[1,1024]{1,0:T(1,128)S(1)} %collective-permute-done.2.refs_0_, bf16[1024,512]{1,0:T(8,128)(2,1)S(1)} %copy-done, bf16[64,512]{1,0:T(8,128)(2,1)S(1)} %shard_map.29.refs_2_), custom_call_target="tpu_custom_call" | custom-call | flops 1000000000 | bytes 4096 | tf_op jit(solution)/shard_map/pallas_call | solution.py:205
  11.4 0.0 collective-permute-done.4.refs_0_
  11.4 0.0 collective-permute-done.5.refs_1_
  11.4 0.9 %shard_map.33 = (bf16[128,512]{1,0:T(8,128)(2,1)S(1)}, bf16[128,512]{1,0:T(8,128)(2,1)S(1)}) custom-call(s32[1,1024]{1,0:T(1,128)S(1)} %collective-permute-done.4.refs_0_, s32[1,1024]{1,0:T(1,128)S(1)} %collective-permute-done.5.refs_1_, bf16[1024,512]{1,0:T(8,128)(2,1)S(1)} %copy-done, bf16[128,512]{1,0:T(8,128)(2,1)S(1)} %shard_map.32.refs_3_), custom_call_target="tpu_custom_call" | custom-call | flops 1000000000 | bytes 4096 | tf_op jit(solution)/shard_map/pallas_call | solution.py:205
  12.3 1.7 %collective-permute-start.6 = (bf16[128,512]{1,0:T(8,128)(2,1)S(1)}, bf16[128,512]{1,0:T(8,128)(2,1)S(1)}, u32[]{:S(2)}, u32[]{:S(2)}) collective-permute-start(bf16[128,512]{1,0:T(8,128)(2,1)S(1)} %get-tuple-element.11), channel_id=1, source_target_pairs={{0,12},{1,9},{2,10},{3,15},{4,8},{5,13},{6,14},{7,11},{8,4},{9,1},... | collective-permute-start | bytes 393224 | tf_op jit(solution)/shard_map/ppermute | solution.py:164
  14.0 1.6 %collective-permute-start.3 = (bf16[128,512]{1,0:T(8,128)(2,1)S(1)}, bf16[128,512]{1,0:T(8,128)(2,1)S(1)}, u32[]{:S(2)}, u32[]{:S(2)}) collective-permute-start(bf16[128,512]{1,0:T(8,128)(2,1)S(1)} %shard_map.32.refs_3_), channel_id=1, source_target_pairs={{0,24},{1,29},{2,26},{3,31},{4,28},{5,25},{6,30},{7,27},{8,16},{9,... | collective-permute-start | bytes 393224 | tf_op jit(solution)/shard_map/ppermute | solution.py:164
  15.6 0.0 collective-permute-done.1.rows_ref
  15.6 0.0 copy-start.1
  15.6 1.6 %collective-permute-start.10 = (bf16[64,512]{1,0:T(8,128)(2,1)S(1)}, bf16[64,512]{1,0:T(8,128)(2,1)S(1)}, u32[]{:S(2)}, u32[]{:S(2)}) collective-permute-start(bf16[64,512]{1,0:T(8,128)(2,1)S(1)} %shard_map.30.refs_0_.refs_6_), channel_id=1, source_target_pairs={{0,2},{1,3},{2,0},{3,1},{4,6},{5,7},{6,4},{7,5},{8,10},{9,11},{10,... | collective-permute-start | bytes 196616 | tf_op jit(solution)/shard_map/ppermute | solution.py:168
  17.2 0.5 %collective-permute-start.12 = (bf16[128,512]{1,0:T(8,128)(2,1)S(1)}, bf16[128,512]{1,0:T(8,128)(2,1)S(1)}, u32[]{:S(2)}, u32[]{:S(2)}) collective-permute-start(bf16[128,512]{1,0:T(8,128)(2,1)S(1)} %get-tuple-element.12), channel_id=1, source_target_pairs={{0,4},{1,5},{2,6},{3,7},{4,0},{5,1},{6,2},{7,3},{8,12},{9,13},{10,... | collective-permute-start | bytes 393224 | tf_op jit(solution)/shard_map/ppermute | solution.py:164
  17.7 0.0 collective-permute-start.9
  17.7 0.0 copy-done.1
  17.7 1.2 %shard_map.31 = (f32[8,128]{1,0:T(8,128)S(1)}, bf16[128,512]{1,0:T(8,128)(2,1)S(1)}) custom-call(s32[1,1024]{1,0:T(1,128)S(1)} %copy-done.1, bf16[1024,512]{1,0:T(8,128)(2,1)S(1)} %copy-done, bf16[64,512]{1,0:T(8,128)(2,1)S(1)} %shard_map.30.refs_0_.refs_6_), custom_call_target="tpu_custom_call" | custom-call | flops 300000000 | bytes 4096 | tf_op jit(solution)/shard_map/pallas_call | solution.py:228
  18.9 0.5 %collective-permute-done.6.rows_ref = bf16[128,512]{1,0:T(8,128)(2,1)S(1)} collective-permute-done((bf16[128,512]{1,0:T(8,128)(2,1)S(1)}, bf16[128,512]{1,0:T(8,128)(2,1)S(1)}, u32[]{:S(2)}, u32[]{:S(2)}) %collective-permute-start.6) | collective-permute-done | bytes 131104 | tf_op jit(solution)/shard_map/ppermute | solution.py:164
  19.5 0.1 collective-permute-start.8
  19.5 1.3 %collective-permute-done.3.refs_2_ = bf16[128,512]{1,0:T(8,128)(2,1)S(1)} collective-permute-done((bf16[128,512]{1,0:T(8,128)(2,1)S(1)}, bf16[128,512]{1,0:T(8,128)(2,1)S(1)}, u32[]{:S(2)}, u32[]{:S(2)}) %collective-permute-start.3) | collective-permute-done | bytes 131104 | tf_op jit(solution)/shard_map/ppermute | solution.py:164
  20.9 0.0 collective-permute-start.7
  20.9 0.0 collective-permute-done.10.rows_ref
  20.9 0.5 %collective-permute-start.11 = (bf16[64,512]{1,0:T(8,128)(2,1)S(1)}, bf16[64,512]{1,0:T(8,128)(2,1)S(1)}, u32[]{:S(2)}, u32[]{:S(2)}) collective-permute-start(bf16[64,512]{1,0:T(8,128)(2,1)S(1)} %shard_map.35.refs_8_), channel_id=1, source_target_pairs={{0,1},{1,0},{2,3},{3,2},{4,5},{5,4},{6,7},{7,6},{8,9},{9,8},{10,11... | collective-permute-start | bytes 196616 | tf_op jit(solution)/shard_map/ppermute | solution.py:168
  21.4 0.0 collective-permute-done.9.refs_7_
  21.4 0.8 %collective-permute-done.12.refs_10_ = bf16[128,512]{1,0:T(8,128)(2,1)S(1)} collective-permute-done((bf16[128,512]{1,0:T(8,128)(2,1)S(1)}, bf16[128,512]{1,0:T(8,128)(2,1)S(1)}, u32[]{:S(2)}, u32[]{:S(2)}) %collective-permute-start.12) | collective-permute-done | bytes 131104 | tf_op jit(solution)/shard_map/ppermute | solution.py:164
  22.2 0.1 collective-permute-done.11.refs_9_
  22.3 0.0 collective-permute-done.8.refs_5_
  22.3 0.0 collective-permute-done.7.refs_4_
  22.3 1.4 %shard_map.36 = f32[1,256]{1,0:T(1,128)} custom-call(f32[8,128]{1,0:T(8,128)S(1)} %get-tuple-element.9.refs_0_, bf16[128,512]{1,0:T(8,128)(2,1)S(1)} %get-tuple-element.10.refs_1_, bf16[128,512]{1,0:T(8,128)(2,1)S(1)} %collective-permute-done.3.refs_2_, bf16[128,512]{1,0:T(8,128)(2,1)S(1)} %shard_map.34.refs_3_, ...), custom_call_target="tpu_custom_call" | custom-call | flops 1000000000 | bytes 2097152 | tf_op jit(solution)/shard_map/pallas_call | solution.py:240
  (4 shorter events, 0.0 us)
Async XLA Ops:
  0.0 7.1 %copy-start = (bf16[1024,512]{1,0:T(8,128)(2,1)S(1)}, bf16[1024,512]{1,0:T(8,128)(2,1)}, u32[]{:S(2)}) copy-start(bf16[1024,512]{1,0:T(8,128)(2,1)} %refs_2_.1) | copy-start | bytes 3145732
  0.0 7.1 %collective-permute-start = (s32[1,1024]{1,0:T(1,128)}, s32[1,1024]{1,0:T(1,128)S(1)}, u32[]{:S(2)}, u32[]{:S(2)}) collective-permute-start(s32[1,1024]{1,0:T(1,128)} %ids_ref.1), channel_id=1, source_target_pairs={{0,16},{1,17},{2,22},{3,23},{4,20},{5,21},{6,18},{7,19},{8,24},{9,... | collective-permute-start | bytes 12296 | tf_op jit(solution)/shard_map/ppermute | solution.py:164
  4.0 6.6 %collective-permute-start.2 = (s32[1,1024]{1,0:T(1,128)}, s32[1,1024]{1,0:T(1,128)S(1)}, u32[]{:S(2)}, u32[]{:S(2)}) collective-permute-start(s32[1,1024]{1,0:T(1,128)} %ids_ref.1), channel_id=1, source_target_pairs={{0,24},{1,29},{2,26},{3,31},{4,28},{5,25},{6,30},{7,27},{8,16},{9,... | collective-permute-start | bytes 12296 | tf_op jit(solution)/shard_map/ppermute | solution.py:164
  5.4 6.0 %collective-permute-start.4 = (s32[1,1024]{1,0:T(1,128)}, s32[1,1024]{1,0:T(1,128)S(1)}, u32[]{:S(2)}, u32[]{:S(2)}) collective-permute-start(s32[1,1024]{1,0:T(1,128)} %ids_ref.1), channel_id=1, source_target_pairs={{0,12},{1,9},{2,10},{3,15},{4,8},{5,13},{6,14},{7,11},{8,4},{9,1},... | collective-permute-start | bytes 12296 | tf_op jit(solution)/shard_map/ppermute | solution.py:164
  6.6 4.8 %collective-permute-start.5 = (s32[1,1024]{1,0:T(1,128)}, s32[1,1024]{1,0:T(1,128)S(1)}, u32[]{:S(2)}, u32[]{:S(2)}) collective-permute-start(s32[1,1024]{1,0:T(1,128)} %ids_ref.1), channel_id=1, source_target_pairs={{0,4},{1,5},{2,6},{3,7},{4,0},{5,1},{6,2},{7,3},{8,12},{9,13},{10,... | collective-permute-start | bytes 12296 | tf_op jit(solution)/shard_map/ppermute | solution.py:164
  7.8 7.8 %collective-permute-start.1 = (bf16[64,512]{1,0:T(8,128)(2,1)S(1)}, bf16[64,512]{1,0:T(8,128)(2,1)S(1)}, u32[]{:S(2)}, u32[]{:S(2)}) collective-permute-start(bf16[64,512]{1,0:T(8,128)(2,1)S(1)} %shard_map.29.refs_2_), channel_id=1, source_target_pairs={{0,16},{1,17},{2,22},{3,23},{4,20},{5,21},{6,18},{7,19},{8,24},{9,... | collective-permute-start | bytes 196616 | tf_op jit(solution)/shard_map/ppermute | solution.py:164
  12.3 7.2 %collective-permute-start.6 = (bf16[128,512]{1,0:T(8,128)(2,1)S(1)}, bf16[128,512]{1,0:T(8,128)(2,1)S(1)}, u32[]{:S(2)}, u32[]{:S(2)}) collective-permute-start(bf16[128,512]{1,0:T(8,128)(2,1)S(1)} %get-tuple-element.11), channel_id=1, source_target_pairs={{0,12},{1,9},{2,10},{3,15},{4,8},{5,13},{6,14},{7,11},{8,4},{9,1},... | collective-permute-start | bytes 393224 | tf_op jit(solution)/shard_map/ppermute | solution.py:164
  14.0 6.9 %collective-permute-start.3 = (bf16[128,512]{1,0:T(8,128)(2,1)S(1)}, bf16[128,512]{1,0:T(8,128)(2,1)S(1)}, u32[]{:S(2)}, u32[]{:S(2)}) collective-permute-start(bf16[128,512]{1,0:T(8,128)(2,1)S(1)} %shard_map.32.refs_3_), channel_id=1, source_target_pairs={{0,24},{1,29},{2,26},{3,31},{4,28},{5,25},{6,30},{7,27},{8,16},{9,... | collective-permute-start | bytes 393224 | tf_op jit(solution)/shard_map/ppermute | solution.py:164
  15.6 2.1 %copy-start.1 = (s32[1,1024]{1,0:T(1,128)S(1)}, s32[1,1024]{1,0:T(1,128)}, u32[]{:S(2)}) copy-start(s32[1,1024]{1,0:T(1,128)} %ids_ref.1) | copy-start | bytes 12292
  15.6 5.3 %collective-permute-start.10 = (bf16[64,512]{1,0:T(8,128)(2,1)S(1)}, bf16[64,512]{1,0:T(8,128)(2,1)S(1)}, u32[]{:S(2)}, u32[]{:S(2)}) collective-permute-start(bf16[64,512]{1,0:T(8,128)(2,1)S(1)} %shard_map.30.refs_0_.refs_6_), channel_id=1, source_target_pairs={{0,2},{1,3},{2,0},{3,1},{4,6},{5,7},{6,4},{7,5},{8,10},{9,11},{10,... | collective-permute-start | bytes 196616 | tf_op jit(solution)/shard_map/ppermute | solution.py:168
  17.2 5.0 %collective-permute-start.12 = (bf16[128,512]{1,0:T(8,128)(2,1)S(1)}, bf16[128,512]{1,0:T(8,128)(2,1)S(1)}, u32[]{:S(2)}, u32[]{:S(2)}) collective-permute-start(bf16[128,512]{1,0:T(8,128)(2,1)S(1)} %get-tuple-element.12), channel_id=1, source_target_pairs={{0,4},{1,5},{2,6},{3,7},{4,0},{5,1},{6,2},{7,3},{8,12},{9,13},{10,... | collective-permute-start | bytes 393224 | tf_op jit(solution)/shard_map/ppermute | solution.py:164
  17.7 3.7 %collective-permute-start.9 = (bf16[64,512]{1,0:T(8,128)(2,1)S(1)}, bf16[64,512]{1,0:T(8,128)(2,1)S(1)}, u32[]{:S(2)}, u32[]{:S(2)}) collective-permute-start(bf16[64,512]{1,0:T(8,128)(2,1)S(1)} %shard_map.30.refs_0_.refs_6_), channel_id=1, source_target_pairs={{0,1},{1,0},{2,3},{3,2},{4,5},{5,4},{6,7},{7,6},{8,9},{9,8},{10,11... | collective-permute-start | bytes 196616 | tf_op jit(solution)/shard_map/ppermute | solution.py:168
  19.5 2.8 %collective-permute-start.8 = (bf16[128,512]{1,0:T(8,128)(2,1)S(1)}, bf16[128,512]{1,0:T(8,128)(2,1)S(1)}, u32[]{:S(2)}, u32[]{:S(2)}) collective-permute-start(bf16[128,512]{1,0:T(8,128)(2,1)S(1)} %shard_map.34.refs_3_), channel_id=1, source_target_pairs={{0,1},{1,0},{2,3},{3,2},{4,5},{5,4},{6,7},{7,6},{8,9},{9,8},{10,11... | collective-permute-start | bytes 393224 | tf_op jit(solution)/shard_map/ppermute | solution.py:168
  20.9 1.4 %collective-permute-start.7 = (bf16[128,512]{1,0:T(8,128)(2,1)S(1)}, bf16[128,512]{1,0:T(8,128)(2,1)S(1)}, u32[]{:S(2)}, u32[]{:S(2)}) collective-permute-start(bf16[128,512]{1,0:T(8,128)(2,1)S(1)} %collective-permute-done.3.refs_2_), channel_id=1, source_target_pairs={{0,1},{1,0},{2,3},{3,2},{4,5},{5,4},{6,7},{7,6},{8,9},{9,8},{10,11... | collective-permute-start | bytes 393224 | tf_op jit(solution)/shard_map/ppermute | solution.py:168
  20.9 1.4 %collective-permute-start.11 = (bf16[64,512]{1,0:T(8,128)(2,1)S(1)}, bf16[64,512]{1,0:T(8,128)(2,1)S(1)}, u32[]{:S(2)}, u32[]{:S(2)}) collective-permute-start(bf16[64,512]{1,0:T(8,128)(2,1)S(1)} %shard_map.35.refs_8_), channel_id=1, source_target_pairs={{0,1},{1,0},{2,3},{3,2},{4,5},{5,4},{6,7},{7,6},{8,9},{9,8},{10,11... | collective-permute-start | bytes 196616 | tf_op jit(solution)/shard_map/ppermute | solution.py:168
